TPU v7x, 32 devices: a whole 2x2x4 slice. The times are simulated.
32 devices in a mesh: rep: 4 (over y, x), fsdp: 8 (over z, core).
Axes of the slice: x: 2, y: 2, z: 4, core: 2. Of those that a mesh axis runs over, the one named last changes fastest.
Arguments:
- residual_in: bfloat16 [8192, 2560], P(('rep', 'fsdp')), may hold values from -60 to 60
- mixed: bfloat16 [8192, 2560], P(('rep', 'fsdp')), may hold values from -6 to 6
- upstream: bfloat16 [8192, 2560], P(('rep', 'fsdp')), may hold values from -6 to 6
- norm_gain: float32 [2560], replicated, may hold values from 0.5 to 1.5
- weight: bfloat16 [4, 2560, 2560], P('rep', 'fsdp'), may hold values from -6 to 6
- momentum: float32 [4, 2560, 2560], P('rep', 'fsdp'), may hold values from -6 to 6
Outputs:
- input_grad: bfloat16 [8192, 2560], P(('rep', 'fsdp'))
- new_weight: bfloat16 [4, 2560, 2560], P('rep', 'fsdp')
- new_momentum: float32 [4, 2560, 2560], P('rep', 'fsdp')
All inputs are finite; a program needn't handle non-finite values.
Results may differ from a plain program's by a relative error of at most 0.009.
Values may be sent and summed in bfloat16 or wider, within the bound.
No kernel may reach another device: no remote copies, remote signals or barrier semaphores. Data moves between devices by JAX's collectives and lax.ppermute only.
A program may use at most 128 MiB of HBM per device.

v0:
```python
import jax
import jax.numpy as jnp
from jax import lax
from jax.sharding import PartitionSpec as P

PARTNER_BIT = 1


EPSILON = 1e-05
LEARN_RATE = 0.05
MOMENTUM_DECAY = 0.9


def from_partner(block, axis, bit):
    count = lax.axis_size(axis)
    route = []
    for low in range(count):
        high = low | 1 << bit
        if high != low and high < count:
            route += [(low, high), (high, low)]
    return lax.ppermute(block, axis, route)


def per_device(residual_in, mixed, upstream, norm_gain, weight, momentum):
    weight_scale = residual_in.shape[1] ** (-0.5)
    local_weight = weight[0]
    local_moment = momentum[0]
    partner_weight = from_partner(local_weight, "rep", PARTNER_BIT)
    partner_moment = from_partner(local_moment.astype(jnp.bfloat16), "rep", PARTNER_BIT).astype(
        local_moment.dtype
    )
    full_weight = lax.all_gather(local_weight, "fsdp", axis=0, tiled=True)
    projected = jnp.dot(mixed, full_weight, preferred_element_type=jnp.float32) * weight_scale
    summed = residual_in.astype(jnp.float32) + projected
    inv_rms = lax.rsqrt(jnp.mean(summed * summed, axis=-1, keepdims=True) + EPSILON)
    scaled_cot = upstream.astype(jnp.float32) * norm_gain
    inner = jnp.mean(scaled_cot * summed, axis=-1, keepdims=True)
    cot_summed = (inv_rms * (scaled_cot - summed * inner * inv_rms * inv_rms)).astype(jnp.bfloat16)
    input_grad = lax.dot_general(
        cot_summed, full_weight, (((1,), (1,)), ((), ())), preferred_element_type=jnp.float32
    )
    input_grad = (input_grad * weight_scale).astype(jnp.bfloat16)
    term = (
        lax.dot_general(
            mixed, cot_summed, (((0,), (0,)), ((), ())), preferred_element_type=jnp.float32
        )
        * weight_scale
    )
    gradient = lax.psum_scatter(
        lax.optimization_barrier(term.astype(jnp.bfloat16))
        .astype(jnp.float32)
        .astype(jnp.bfloat16),
        "fsdp",
        scatter_dimension=0,
        tiled=True,
    ).astype(jnp.float32)
    moment_next = MOMENTUM_DECAY * local_moment + gradient
    weight_next = (local_weight.astype(jnp.float32) - LEARN_RATE * moment_next).astype(jnp.bfloat16)
    partner_grad = from_partner(gradient.astype(jnp.bfloat16), "rep", PARTNER_BIT).astype(
        gradient.dtype
    )
    other_moment = MOMENTUM_DECAY * partner_moment + partner_grad
    other_weight = (partner_weight.astype(jnp.float32) - LEARN_RATE * other_moment).astype(
        jnp.bfloat16
    )
    new_weight = (
        (weight_next.astype(jnp.float32) + other_weight.astype(jnp.float32)) * 0.5
    ).astype(jnp.bfloat16)
    new_momentum = (moment_next + other_moment) * 0.5
    return (input_grad, new_weight[None], new_momentum[None])


def solution(mesh):
    return jax.shard_map(
        per_device,
        mesh=mesh,
        in_specs=(
            P(("rep", "fsdp"), None),
            P(("rep", "fsdp"), None),
            P(("rep", "fsdp"), None),
            P(),
            P("rep", "fsdp", None),
            P("rep", "fsdp", None),
        ),
        out_specs=(P(("rep", "fsdp"), None), P("rep", "fsdp", None), P("rep", "fsdp", None)),
        check_vma=False,
    )
```

profile of v0, /device:TPU:0, one launch (start us, length us, event | category | flops | bytes accessed | tf_op | source)
XLA Modules:
  0.0 364.0 jit_solution(8310275446714241164)
XLA Ops:
  7.2 0.0 copy-start
  7.2 0.0 all-gather.3.cloned.1.call-start
  7.2 0.7 all-gather.3.cloned.1.call-update
  7.9 0.0 copy-start.2
  7.9 0.0 copy-start.4
  7.9 0.0 reduce-scatter.4.cloned.1.call-start
  8.0 125.4 %all-gather.3.cloned.1.call-done = bf16[1,2560,2560]{2,1,0:T(8,128)(2,1)} async-done(((bf16[1,320,2560]{2,1,0:T(8,128)(2,1)}), bf16[1,2560,2560]{2,1,0:T(8,128)(2,1)}) %all-gather.3.cloned.1.call-update) | async-done | bytes 13107216 | tf_op jit(solution)/shard_map/all_gather | solution.py:32
  133.4 0.0 copy-done
  133.4 9.2 %multiply_reduce_fusion.1 = (f32[256]{0:T(256)S(1)}, f32[256]{0:T(256)S(1)}, f32[256,2560]{1,0:T(8,128)S(1)}) fusion(f32[2560]{0:T(1024)} %param.9, bf16[256,2560]{1,0:T(8,128)(2,1)} %param.8, bf16[256,2560]{1,0:T(8,128)(2,1)S(1)} %copy-done, bf16[1,2560,2560]{2,1,0:T(8,128)(2,1)} %all-gather.3.cloned.1.call-done, bf16[256,2560]{1,0:T(8,128)(2,1)} %param.6), kind=kOutput, calls=%fused_computation.19 | convolution fusion | flops 3361340928 | bytes 19673088 | tf_op jit(solution)/shard_map/dot_general | solution.py:33
  142.7 0.0 copy-start.5
  142.7 1.5 copy-done.5
  144.1 0.0 copy-done.2
  144.2 0.0 copy-done.4
  144.2 7.0 %fusion = bf16[2560,2560]{0,1:T(8,128)(2,1)} fusion(bf16[256,2560]{1,0:T(8,128)(2,1)S(1)} %copy-done, f32[256,2560]{1,0:T(8,128)S(1)} %get-tuple-element.13, bf16[256,2560]{1,0:T(8,128)(2,1)S(1)} %copy-done.2, f32[256]{0:T(256)S(1)} %get-tuple-element.15, f32[2560]{0:T(1024)S(1)} %copy-done.4, f32[256]{0:T(256)S(1)} %get-tuple-element.14), kind=kOutput, calls=%fused_computation.1 | convolution fusion | flops 3373793280 | bytes 18362368 | tf_op jit(solution)/shard_map/dot_general | solution.py:44
  151.1 17.6 %copy.24 = bf16[2560,2560]{1,0:T(8,128)(2,1)} copy(bf16[2560,2560]{0,1:T(8,128)(2,1)} %fusion) | data formatting | bytes 26214400
  168.7 0.0 reduce-scatter.4.cloned.1.call-update
  168.8 3.3 convert_bitcast_fusion
  172.0 1.5 collective-permute-start.1
  173.5 0.6 collective-permute-start
  174.1 127.2 %reduce-scatter.4.cloned.1.call-done = bf16[320,2560]{1,0:T(8,128)(2,1)} async-done(((bf16[2560,2560]{1,0:T(8,128)(2,1)}), bf16[320,2560]{1,0:T(8,128)(2,1)}) %reduce-scatter.4.cloned.1.call-update) | async-done | bytes 1638416 | tf_op jit(solution)/shard_map/reduce_scatter | solution.py:49
  301.3 1.5 collective-permute-start.2
  302.8 5.1 %copy.15 = f32[1,320,2560]{1,2,0:T(8,128)} copy(f32[1,320,2560]{2,1,0:T(8,128)} %param.11) | data formatting | bytes 6553600 | tf_op args[5]
  307.9 3.6 copy.14
  311.5 0.0 collective-permute-done.1
  311.5 3.8 %copy.18 = bf16[320,2560]{0,1:T(8,128)(2,1)} copy(bf16[320,2560]{1,0:T(8,128)(2,1)} %collective-permute-done.1) | data formatting | bytes 3276800 | tf_op jit(solution)/shard_map/ppermute | solution.py:21
  315.3 0.0 copy-start.3
  315.3 0.0 collective-permute-done
  315.3 3.9 %copy.17 = bf16[320,2560]{0,1:T(8,128)(2,1)} copy(bf16[320,2560]{1,0:T(8,128)(2,1)} %collective-permute-done) | data formatting | bytes 3276800 | tf_op jit(solution)/shard_map/ppermute | solution.py:21
  319.2 0.0 copy-done.3
  319.2 10.2 %fusion.14 = bf16[256,2560]{1,0:T(8,128)(2,1)} fusion(bf16[1,2560,2560]{2,1,0:T(8,128)(2,1)} %all-gather.3.cloned.1.call-done, f32[256,2560]{1,0:T(8,128)} %copy-done.5, bf16[256,2560]{1,0:T(8,128)(2,1)S(1)} %copy-done.3, f32[256]{0:T(256)S(1)} %get-tuple-element.15, f32[2560]{0:T(1024)S(1)} %copy-done.4, f32[256]{0:T(256)S(1)} %get-tuple-element.14), kind=kOutput, calls=%fused_computation.15 | convolution fusion | flops 3361996800 | bytes 18362368 | tf_op jit(solution)/shard_map/dot_general | solution.py:39
  329.4 3.8 %copy.25 = bf16[320,2560]{0,1:T(8,128)(2,1)} copy(bf16[320,2560]{1,0:T(8,128)(2,1)} %reduce-scatter.4.cloned.1.call-done) | data formatting | bytes 3276800
  333.3 3.8 %collective-permute-done.2 = bf16[320,2560]{1,0:T(8,128)(2,1)} collective-permute-done((bf16[320,2560]{1,0:T(8,128)(2,1)}, bf16[320,2560]{1,0:T(8,128)(2,1)}, u32[]{:S(2)}, u32[]{:S(2)}) %collective-permute-start.2) | collective-permute-done | bytes 1638432 | tf_op jit(solution)/shard_map/ppermute | solution.py:21
  337.0 3.8 %copy.20 = bf16[320,2560]{0,1:T(8,128)(2,1)} copy(bf16[320,2560]{1,0:T(8,128)(2,1)} %collective-permute-done.2) | data formatting | bytes 3276800 | tf_op jit(solution)/shard_map/ppermute | solution.py:21
  340.8 7.1 %multiply_bitcast_fusion = (f32[1,320,2560]{1,2,0:T(8,128)}, bf16[1,320,2560]{1,2,0:T(8,128)(2,1)}) fusion(bf16[320,2560]{0,1:T(8,128)(2,1)} %copy.20, bf16[320,2560]{0,1:T(8,128)(2,1)} %copy.18, bf16[320,2560]{0,1:T(8,128)(2,1)} %copy.25, f32[1,320,2560]{1,2,0:T(8,128)} %copy.15, bf16[320,2560]{0,1:T(8,128)(2,1)} %copy.17, bf16[1,320,2560]{1,2,0:T(8,128)(2,1)S(1)} %copy.14), kind=kLoop, calls=%fused_computation.10 | loop fusion | flops 18022400 | bytes 16384000 | tf_op jit(solution)/shard_map/broadcast_in_dim | solution.py:70
  347.9 3.9 %copy.21 = bf16[1,320,2560]{2,1,0:T(8,128)(2,1)} copy(bf16[1,320,2560]{1,2,0:T(8,128)(2,1)} %get-tuple-element.12) | data formatting | bytes 3276800
  351.8 0.0 copy-start.1
  351.8 5.3 %copy.22 = f32[1,320,2560]{2,1,0:T(8,128)} copy(f32[1,320,2560]{1,2,0:T(8,128)} %get-tuple-element.11) | data formatting | bytes 6553600
  357.1 0.0 copy-done.1
  (1 shorter events, 0.0 us)
Async XLA Ops:
  7.2 126.3 %copy-start = (bf16[256,2560]{1,0:T(8,128)(2,1)S(1)}, bf16[256,2560]{1,0:T(8,128)(2,1)}, u32[]{:S(2)}) copy-start(bf16[256,2560]{1,0:T(8,128)(2,1)} %param.7) | copy-start | bytes 3932164
  7.2 126.2 %all-gather.3.cloned.1.call-start = ((), (), s32[]{:S(2)}) async-start(), calls=%async_computation.1 | async-start | bytes 14745600 | tf_op jit(solution)/shard_map/all_gather | solution.py:32
  7.9 136.2 %copy-start.2 = (bf16[256,2560]{1,0:T(8,128)(2,1)S(1)}, bf16[256,2560]{1,0:T(8,128)(2,1)}, u32[]{:S(2)}) copy-start(bf16[256,2560]{1,0:T(8,128)(2,1)} %param.8) | copy-start | bytes 3932164
  7.9 136.2 %copy-start.4 = (f32[2560]{0:T(1024)S(1)}, f32[2560]{0:T(1024)}, u32[]{:S(2)}) copy-start(f32[2560]{0:T(1024)} %param.9) | copy-start | bytes 30724
  7.9 293.4 %reduce-scatter.4.cloned.1.call-start = ((), (), s32[]{:S(2)}) async-start(), calls=%async_computation.2 | async-start | bytes 14745600 | tf_op jit(solution)/shard_map/reduce_scatter | solution.py:49
  142.7 1.5 copy-start.5
  172.0 139.4 %collective-permute-start.1 = (bf16[320,2560]{1,0:T(8,128)(2,1)}, bf16[320,2560]{1,0:T(8,128)(2,1)}, u32[]{:S(2)}, u32[]{:S(2)}) collective-permute-start(bf16[320,2560]{1,0:T(8,128)(2,1)} %convert_bitcast_fusion), channel_id=1, source_target_pairs={{0,16},{16,0},{8,24},{24,8},{1,17},{17,1},{9,25},{25,9},{2,18},{18... | collective-permute-start | bytes 4915208 | tf_op jit(solution)/shard_map/ppermute | solution.py:21
  173.5 141.8 %collective-permute-start = (bf16[320,2560]{1,0:T(8,128)(2,1)}, bf16[320,2560]{1,0:T(8,128)(2,1)}, u32[]{:S(2)}, u32[]{:S(2)}) collective-permute-start(bf16[320,2560]{1,0:T(8,128)(2,1)} %bitcast.4), channel_id=1, source_target_pairs={{0,16},{16,0},{8,24},{24,8},{1,17},{17,1},{9,25},{25,9},{2,18},{18... | collective-permute-start | bytes 4915208 | tf_op jit(solution)/shard_map/ppermute | solution.py:21
  301.3 35.7 %collective-permute-start.2 = (bf16[320,2560]{1,0:T(8,128)(2,1)}, bf16[320,2560]{1,0:T(8,128)(2,1)}, u32[]{:S(2)}, u32[]{:S(2)}) collective-permute-start(bf16[320,2560]{1,0:T(8,128)(2,1)} %reduce-scatter.4.cloned.1.call-done), channel_id=1, source_target_pairs={{0,16},{16,0},{8,24},{24,8},{1,17},{17,1},{9,25},{25,9},{2,18},{18... | collective-permute-start | bytes 4915208 | tf_op jit(solution)/shard_map/ppermute | solution.py:21
  315.3 3.9 %copy-start.3 = (bf16[256,2560]{1,0:T(8,128)(2,1)S(1)}, bf16[256,2560]{1,0:T(8,128)(2,1)}, u32[]{:S(2)}) copy-start(bf16[256,2560]{1,0:T(8,128)(2,1)} %param.8) | copy-start | bytes 3932164
  351.8 5.3 %copy-start.1 = (bf16[256,2560]{1,0:T(8,128)(2,1)S(1)}, bf16[256,2560]{1,0:T(8,128)(2,1)}, u32[]{:S(2)}) copy-start(bf16[256,2560]{1,0:T(8,128)(2,1)} %param.7) | copy-start | bytes 3932164
Sparse Core Ops, SparseCore 0:
  9.7 123.7 all-gather.2
  168.9 132.3 reduce-scatter.3
where the time goes:
time: 365 us; the launch traced here: 364 us
  waiting for transfers between devices  257 us (70%)
  local copies, waits for them, and re-layouts  52.4 us (14%)
  matrix products  26.4 us (7%)
  between operations  14.1 us (4%)
  other arithmetic  10.4 us (3%)
    reduce_scatter x1, waiting for transfers between devices, per_device(): lax.psum_scatter(lax.optimization_barrier(term.astype(jnp.bfloat16)).asty...  127 us
    all_gather x1, waiting for transfers between devices, per_device(): full_weight = lax.all_gather(local_weight, 'fsdp', axis=0, tiled=True)  125 us
    unnamed x18, local copies, waits for them, and re-layouts  40.8 us
    ppermute x3, local copies, waits for them, and re-layouts, from_partner(): return lax.ppermute(block, axis, route)  11.6 us
    dot_general x1, matrix products, per_device(): lax.dot_general(cot_summed, full_weight, (((1,), (1,)), ((), ())), prefer...  10.2 us
    dot_general x1, matrix products, per_device(): jnp.dot(mixed, full_weight, preferred_element_type=jnp.float32)  9.22 us
  transfers between devices with their start and end apart: 5, of which 3 were waited for; matrix products, arithmetic and copies ran while one was open for 9% of the time, Pallas kernels for 0%

commit v1 on v0

v1 whole, which is shorter than its diff:
```python
import functools

import jax
import jax.numpy as jnp
from jax import lax
from jax.experimental import pallas as pl
from jax.experimental.pallas import tpu as pltpu
from jax.sharding import PartitionSpec as P

PARTNER_BIT = 1

EPSILON = 1e-05
LEARN_RATE = 0.05
MOMENTUM_DECAY = 0.9

FWD_CHUNKS = 4
BWD_CHUNKS = 4
COST_SHARE = 0.01
BF = jnp.bfloat16
F32 = jnp.float32


def params(mib=48):
    return pltpu.CompilerParams(vmem_limit_bytes=mib << 20)


def cost(flops, moved):
    return pl.CostEstimate(
        flops=int(flops * COST_SHARE), bytes_accessed=int(moved * COST_SHARE), transcendentals=0
    )


def whole():
    return pl.BlockSpec(memory_space=pltpu.VMEM)


def after(block, *others):
    return lax.optimization_barrier((block, *others))[0]


def from_partner(block):
    count = lax.axis_size("rep")
    return lax.ppermute(block, "rep", [(g, g ^ (1 << PARTNER_BIT)) for g in range(count)])


def from_mate(block, bit):
    count = lax.axis_size("fsdp")
    return lax.ppermute(block, "fsdp", [(f, f ^ bit) for f in range(count)])


def shift_far(block, hops):
    count = lax.axis_size("fsdp")
    return lax.ppermute(block, "fsdp", [(f, (f + 4 * hops) % count) for f in range(count)])


def forward_kernel(scale, rows, n_far, place, x_ref, own_ref, mate_ref, *refs):
    fars, rest = refs[: 2 * n_far], refs[2 * n_far :]
    w_ref, keep_ref, give_ref = rest
    for i, ref in enumerate((own_ref, mate_ref, *fars)):
        w_ref[pl.ds(pl.multiple_of(place[i] * rows, 16), rows), :] = ref[...]
    part = jnp.dot(x_ref[...], w_ref[...], preferred_element_type=F32) * scale
    tokens = keep_ref.shape[0]
    keep_ref[...] = part[:tokens]
    give_ref[...] = part[tokens:].astype(BF)


def forward_part(place, x, own, mate, fars, chunk, width, scale):
    tokens, depth = x.shape[0] // 2, x.shape[1]
    rows = own.shape[0]
    column = pl.BlockSpec((rows, width), lambda i, place: (0, chunk))
    full = lambda shape: pl.BlockSpec(shape, lambda i, place: (0, 0))
    return pl.pallas_call(
        functools.partial(forward_kernel, scale, rows, len(fars) // 2),
        grid_spec=pltpu.PrefetchScalarGridSpec(
            num_scalar_prefetch=1,
            grid=(1,),
            in_specs=[full(x.shape), column, column] + [full(w.shape) for w in fars],
            out_specs=[full((depth, width)), full((tokens, width)), full((tokens, width))],
        ),
        out_shape=[
            jax.ShapeDtypeStruct((depth, width), BF),
            jax.ShapeDtypeStruct((tokens, width), F32),
            jax.ShapeDtypeStruct((tokens, width), BF),
        ],
        compiler_params=params(),
        cost_estimate=cost(4 * tokens * depth * width, 2 * depth * (2 * width + 2 * tokens)),
        name="forward_part",
    )(place, x, own, mate, *fars)


def norm_kernel(n_in, n_out, res_ref, up_ref, gain_ref, *refs):
    keeps, gots, cots = refs[:n_in], refs[n_in : 2 * n_in], refs[2 * n_in :]
    width = keeps[0].shape[1]
    features = n_in * width
    summed, scaled = [], []
    square = inner = 0.0
    for i in range(n_in):
        cols = slice(i * width, (i + 1) * width)
        s = res_ref[:, cols].astype(F32) + (keeps[i][...] + gots[i][...].astype(F32))
        c = up_ref[:, cols].astype(F32) * gain_ref[:, cols]
        square += jnp.sum(s * s, axis=-1, keepdims=True)
        inner += jnp.sum(c * s, axis=-1, keepdims=True)
        summed.append(s)
        scaled.append(c)
    inv_rms = lax.rsqrt(square / features + EPSILON)
    pull = inner / features * inv_rms * inv_rms
    out_width = cots[0].shape[1]
    for i in range(n_in):
        cot = (inv_rms * (scaled[i] - summed[i] * pull)).astype(BF)
        if n_in == n_out:
            cots[i][...] = cot
        else:
            start = i * width
            at = start
            while at < start + width:
                j = at // out_width
                end = min((j + 1) * out_width, start + width)
                cots[j][:, at - j * out_width : end - j * out_width] = cot[:, at - start : end - start]
                at = end


def norm_cot(residual, upstream, gain, keeps, gots, n_out):
    tokens, features = residual.shape
    tile = 64
    n_in = len(keeps)
    width, out_width = features // n_in, features // n_out
    row = lambda w: pl.BlockSpec((tile, w), lambda i: (i, 0))
    return pl.pallas_call(
        functools.partial(norm_kernel, n_in, n_out),
        grid=(tokens // tile,),
        in_specs=[row(features), row(features), pl.BlockSpec((1, features), lambda i: (0, 0))]
        + [row(width)] * (2 * n_in),
        out_specs=[row(out_width)] * n_out,
        out_shape=[jax.ShapeDtypeStruct((tokens, out_width), BF)] * n_out,
        compiler_params=params(),
        cost_estimate=cost(20 * tokens * features, 12 * tokens * features),
        name="norm_cot",
    )(residual, upstream, gain.reshape(1, features), *keeps, *gots)


def gradient_kernel(scale, x_ref, *refs):
    cots, (keep_ref, give_ref) = refs[:4], refs[4:]
    cot = jnp.concatenate([ref[...] for ref in cots], axis=0)
    part = jnp.dot(x_ref[...], cot, preferred_element_type=F32) * scale
    half = keep_ref.shape[0]
    keep_ref[...] = part[:half]
    give_ref[...] = part[half:].astype(BF)


def gradient_part(x_rows, cots, scale):
    rows, tokens = x_rows.shape
    width = cots[0].shape[1]
    return pl.pallas_call(
        functools.partial(gradient_kernel, scale),
        in_specs=[whole()] * 5,
        out_specs=[whole()] * 2,
        out_shape=[
            jax.ShapeDtypeStruct((rows // 2, width), F32),
            jax.ShapeDtypeStruct((rows // 2, width), BF),
        ],
        compiler_params=params(),
        cost_estimate=cost(2 * rows * tokens * width, 2 * tokens * (rows + width) + 3 * rows * width),
        name="gradient_part",
    )(x_rows, *cots)


def input_grad_kernel(scale, n_cot, n_weight, *refs):
    own, nb = refs[:n_cot], refs[n_cot : 2 * n_cot]
    weights = refs[2 * n_cot : 2 * n_cot + n_weight]
    keep_ref, give_ref = refs[2 * n_cot + n_weight :]
    cot = jnp.concatenate(
        [jnp.concatenate([ref[...] for ref in side], axis=1) for side in (own, nb)], axis=0
    )
    width = weights[0].shape[1]
    total = 0.0
    for i, ref in enumerate(weights):
        total += lax.dot_general(
            cot[:, i * width : (i + 1) * width],
            ref[...],
            (((1,), (1,)), ((), ())),
            preferred_element_type=F32,
        )
    total = (total * scale).astype(BF)
    tokens = keep_ref.shape[0]
    keep_ref[...] = total[:tokens]
    give_ref[...] = total[tokens:]


def input_grad_part(own, nb, weights, scale):
    tokens = own[0].shape[0]
    depth = weights[0].shape[0]
    features = len(weights) * weights[0].shape[1]
    count = 2 * len(own) + len(weights)
    return pl.pallas_call(
        functools.partial(input_grad_kernel, scale, len(own), len(weights)),
        in_specs=[whole()] * count,
        out_specs=[whole()] * 2,
        out_shape=[jax.ShapeDtypeStruct((tokens, depth), BF)] * 2,
        compiler_params=params(),
        cost_estimate=cost(
            4 * tokens * depth * features, 2 * depth * features + 4 * tokens * (depth + features)
        ),
        name="input_grad_part",
    )(*own, *nb, *weights)


def split_kernel(n_quad, near, mixed_ref, own_ref, give_ref):
    width = own_ref.shape[1] // n_quad
    for side in range(2):

        @pl.when(near[0] == side)
        def _():
            for i in range(n_quad):
                to = slice(i * width, (i + 1) * width)
                ours, theirs = 2 * i + side, 2 * i + 1 - side
                own_ref[:, to] = mixed_ref[:, ours * width : (ours + 1) * width]
                give_ref[:, to] = mixed_ref[:, theirs * width : (theirs + 1) * width]


def split(near, mixed, n_quad):
    tokens, features = mixed.shape
    tile = 64
    row = lambda w: pl.BlockSpec((tile, w), lambda i, near: (i, 0))
    return pl.pallas_call(
        functools.partial(split_kernel, n_quad),
        grid_spec=pltpu.PrefetchScalarGridSpec(
            num_scalar_prefetch=1,
            grid=(tokens // tile,),
            in_specs=[row(features)],
            out_specs=[row(features // 2)] * 2,
        ),
        out_shape=[jax.ShapeDtypeStruct((tokens, features // 2), BF)] * 2,
        compiler_params=params(),
        cost_estimate=cost(0, 4 * tokens * features),
        name="split",
    )(near, mixed)


def interleave_kernel(n_quad, near, own_ref, got_ref, out_ref):
    width = own_ref.shape[1] // n_quad
    for side in range(2):

        @pl.when(near[0] == side)
        def _():
            for i in range(n_quad):
                at = slice(i * width, (i + 1) * width)
                ours, theirs = 2 * i + side, 2 * i + 1 - side
                out_ref[:, ours * width : (ours + 1) * width] = own_ref[:, at]
                out_ref[:, theirs * width : (theirs + 1) * width] = got_ref[:, at]


def interleave(near, own, got, n_quad):
    tokens, depth = own.shape
    tile = 64
    row = lambda w: pl.BlockSpec((tile, w), lambda i, near: (i, 0))
    return pl.pallas_call(
        functools.partial(interleave_kernel, n_quad),
        grid_spec=pltpu.PrefetchScalarGridSpec(
            num_scalar_prefetch=1,
            grid=(tokens // tile,),
            in_specs=[row(depth)] * 2,
            out_specs=row(2 * depth),
        ),
        out_shape=jax.ShapeDtypeStruct((tokens, 2 * depth), BF),
        compiler_params=params(),
        cost_estimate=cost(0, 8 * tokens * depth),
        name="interleave",
    )(near, own, got)


def update_kernel(count, place, w_ref, pw_ref, m_ref, pm_ref, *refs):
    ours, theirs = refs[:count], refs[count : 2 * count]
    weight_ref, moment_ref = refs[2 * count :]
    mine = pl.program_id(0) == 0
    width = ours[0].shape[1]
    for i in range(count):
        cols = slice(i * width, (i + 1) * width)
        grads = jnp.where(mine, ours[i][...], theirs[i][...].astype(F32))
        moment = 0.5 * (
            MOMENTUM_DECAY * (m_ref[0, :, cols] + pm_ref[:, cols].astype(F32)) + grads
        )
        moment_ref[0, :, cols] = moment
        both = w_ref[0, :, cols].astype(F32) + pw_ref[:, cols].astype(F32)
        weight_ref[0, :, cols] = (0.5 * both - LEARN_RATE * moment).astype(BF)


def update(side, weight, partner_weight, momentum, partner_moment, ours, theirs):
    _, rows, features = weight.shape
    half = rows // 2
    width = ours[0].shape[1]
    block3 = pl.BlockSpec((1, half, features), lambda i, side: (0, (side[0] + i) % 2, 0))
    block2 = pl.BlockSpec((half, features), lambda i, side: ((side[0] + i) % 2, 0))
    fixed = pl.BlockSpec((half, width), lambda i, side: (0, 0))
    return pl.pallas_call(
        functools.partial(update_kernel, len(ours)),
        grid_spec=pltpu.PrefetchScalarGridSpec(
            num_scalar_prefetch=1,
            grid=(2,),
            in_specs=[block3, block2, block3, block2] + [fixed] * (2 * len(ours)),
            out_specs=[block3, block3],
        ),
        out_shape=[
            jax.ShapeDtypeStruct(weight.shape, BF),
            jax.ShapeDtypeStruct(momentum.shape, F32),
        ],
        compiler_params=params(),
        cost_estimate=cost(10 * rows * features, 18 * rows * features),
        name="update",
    )(side, weight, partner_weight, momentum, partner_moment, *ours, *theirs)


def per_device(residual_in, mixed, upstream, norm_gain, weight, momentum):
    tokens, features = mixed.shape
    scale = features ** (-0.5)
    count = lax.axis_size("fsdp")
    n_quad = count // 4
    rows = weight.shape[1]
    me = lax.axis_index("fsdp")
    quad, core, near = me // 4, me % 2, (me // 2) % 2
    side = (lax.axis_index("rep") >> PARTNER_BIT) & 1
    own = weight[0]

    width = features // FWD_CHUNKS
    cols = [slice(i * width, (i + 1) * width) for i in range(FWD_CHUNKS)]
    x_own, x_give = split(near.reshape(1).astype(jnp.int32), mixed, n_quad)
    x_nb = from_mate(x_give, 2)
    fars = [[shift_far(own[:, c], d) for d in range(1, n_quad)] for c in cols]
    mate = from_mate(own, 1)
    partner_weight = from_partner(own)
    partner_moment = from_partner(momentum[0].astype(BF))

    quads = [quad] + [(quad + n_quad - d) % n_quad for d in range(1, n_quad)]
    place = jnp.stack(
        [quads[0] * 2 + core, quads[0] * 2 + 1 - core]
        + [q * 2 + core for q in quads[1:]]
        + [q * 2 + 1 - core for q in quads[1:]]
    ).astype(jnp.int32)

    x = jnp.concatenate([x_own, x_nb], axis=0)
    on = [(quad + d) % n_quad for d in range(n_quad)]
    block = lambda q, c: lax.dynamic_slice(x, (0, (q * 2 + c) * rows), (2 * tokens, rows))
    x_mine = jnp.concatenate([block(q, core) for q in on], axis=1)
    x_theirs = from_mate(jnp.concatenate([block(q, 1 - core) for q in on], axis=1), 1)
    x_rows = jnp.concatenate([x_mine, x_theirs], axis=0).T.reshape(n_quad, 2, rows // 2, 4 * tokens)
    x_rows = jnp.where(side == 0, x_rows, x_rows[:, ::-1])
    x_rows = jnp.swapaxes(x_rows, 0, 1).reshape(n_quad * rows, 4 * tokens)

    weights, keeps, gots = [], [], []
    for i in range(FWD_CHUNKS):
        seen = [partner_weight] if i == 2 else [x_rows, partner_moment] if i == 3 else []
        seen += gots[i - 2 : i - 1] if i > 1 else []
        seen += keeps[-1:]
        far_mates = [from_mate(after(w, *seen), 1) for w in fars[i]]
        w_rows, keep, give = forward_part(place, x, own, mate, fars[i] + far_mates, i, width, scale)
        weights.append(w_rows)
        keeps.append(keep)
        gots.append(from_mate(give, 2))

    keeps[0] = after(keeps[0], partner_weight, partner_moment, x_rows)
    cots = list(norm_cot(residual_in, upstream, norm_gain, keeps, gots, BWD_CHUNKS))

    half = rows // 2
    nbs = [from_mate(cot, 2) for cot in cots]
    mates = [from_mate(cot, 1) for cot in cots]
    kept, got, ours, theirs = [], [], [], []

    def gather(i):
        both = kept[i] + got[i].astype(F32)
        total = both[:half]
        for d in range(1, n_quad):
            total += shift_far(both[d * half : (d + 1) * half].astype(BF), d).astype(F32)
        ours.append(total)
        theirs.append(from_partner(total.astype(BF)))

    far_sums = []

    def sum_far(i):
        both = kept[i] + got[i].astype(F32)
        far_sums.append(
            [shift_far(both[d * half : (d + 1) * half].astype(BF), d) for d in range(1, n_quad)]
        )
        ours.append(both[:half])

    def give_back(i):
        for block in far_sums[i]:
            ours[i] += block.astype(F32)
        theirs.append(from_partner(ours[i].astype(BF)))

    nb_mates = []
    for i in range(BWD_CHUNKS):
        nb_mates.append(from_mate(nbs[i], 1))
    for i in range(BWD_CHUNKS + 2):
        if i < BWD_CHUNKS:
            seen = got[-1:] + (far_sums[-1] if far_sums else []) + theirs[-1:]
            seen += nb_mates[i + 1 : i + 2] if i else []
            keep, give = gradient_part(
                after(x_rows, *seen) if seen else x_rows, [cots[i], nbs[i], mates[i], nb_mates[i]], scale
            )
            kept.append(keep)
        if 0 <= i - 2:
            give_back(i - 2)
        if 0 <= i - 1 < BWD_CHUNKS:
            sum_far(i - 1)
        if i < BWD_CHUNKS:
            got.append(from_partner(give))

    ig_own, ig_nb = input_grad_part([after(cots[0], kept[-1])] + cots[1:], nbs, weights, scale)
    ig_got = from_mate(ig_nb, 2)
    input_grad = interleave(near.reshape(1).astype(jnp.int32), ig_own, ig_got, n_quad)

    new_weight, new_momentum = update(
        side.reshape(1).astype(jnp.int32), weight, partner_weight, momentum, partner_moment, ours, theirs
    )
    return (input_grad, new_weight, new_momentum)


def solution(mesh):
    return jax.shard_map(
        per_device,
        mesh=mesh,
        in_specs=(
            P(("rep", "fsdp"), None),
            P(("rep", "fsdp"), None),
            P(("rep", "fsdp"), None),
            P(),
            P("rep", "fsdp", None),
            P("rep", "fsdp", None),
        ),
        out_specs=(P(("rep", "fsdp"), None), P("rep", "fsdp", None), P("rep", "fsdp", None)),
        check_vma=False,
    )
```

time: 365 us -> 227 us (0.62)
  waiting for transfers between devices: 257 us -> 131 us
  Pallas kernels: 0 us -> 36.5 us
  local copies, waits for them, and re-layouts: 52.4 us -> 18.7 us
  starting transfers between devices: 3.6 us -> 31.6 us
  matrix products: 26.4 us -> 0 us
  between operations: 14.1 us -> 0.9 us
    reduce_scatter x1 -> x0, waiting for transfers between devices: 127 us -> none  [per_device(): lax.psum_scatter(lax.optimization_barrier(term.astype(jnp.bfloat16)).asty...]
    ppermute x3 -> x42, waiting for transfers between devices: 3.78 us -> 131 us  [the longest x8 74.5 us: shift_far(): lax.ppermute(block, 'fsdp', [(f, (f + 4 * hops) % count) for f in range(c...]
    all_gather x1 -> x0, waiting for transfers between devices: 125 us -> none  [per_device(): full_weight = lax.all_gather(local_weight, 'fsdp', axis=0, tiled=True)]
    pallas_call x0 -> x13, Pallas kernels: none -> 36.5 us  [the longest x4 13.9 us: forward_part(): pl.pallas_call(functools.partial(forward_kernel, scale, rows, len(fars) /...]
    unnamed x18 -> x37, local copies, waits for them, and re-layouts: 40.8 us -> 10.7 us
    ppermute x3 -> x42, starting transfers between devices: 3.52 us -> 31.6 us  [the longest x24 13.8 us: from_mate(): return lax.ppermute(block, 'fsdp', [(f, f ^ bit) for f in range(count)])]
    dot_general x3 -> x0, matrix products: 26.4 us -> none  [the longest x1 10.2 us: per_device(): lax.dot_general(cot_summed, full_weight, (((1,), (1,)), ((), ())), prefer...]
    ppermute x3 -> x0, local copies, waits for them, and re-layouts: 11.6 us -> none  [from_partner(): return lax.ppermute(block, axis, route)]
  transfers between devices with their start and end apart: 5 -> 42, of which waited for: 3 -> 22; matrix products, arithmetic and copies ran while one was open for 9% -> 7% of each run, Pallas kernels for 0% -> 12%
where the time goes in v1:
time: 227 us; the launch traced here: 226 us
  waiting for transfers between devices  131 us (58%)
  Pallas kernels  36.5 us (16%)
  starting transfers between devices  31.6 us (14%)
  local copies, waits for them, and re-layouts  18.7 us (8%)
  other arithmetic  7.64 us (3%)
    ppermute x8, waiting for transfers between devices, shift_far(): lax.ppermute(block, 'fsdp', [(f, (f + 4 * hops) % count) for f in range(c...  74.5 us
    ppermute x24, waiting for transfers between devices, from_mate(): return lax.ppermute(block, 'fsdp', [(f, f ^ bit) for f in range(count)])  49.7 us
    pallas_call x4, Pallas kernels, forward_part(): pl.pallas_call(functools.partial(forward_kernel, scale, rows, len(fars) /...  13.9 us
    ppermute x24, starting transfers between devices, from_mate(): return lax.ppermute(block, 'fsdp', [(f, f ^ bit) for f in range(count)])  13.8 us
    unnamed x37, local copies, waits for them, and re-layouts  10.7 us
    ppermute x10, starting transfers between devices, from_partner(): lax.ppermute(block, 'rep', [(g, g ^ 1 << PARTNER_BIT) for g in range(coun...  10.2 us
    ppermute x8, starting transfers between devices, shift_far(): lax.ppermute(block, 'fsdp', [(f, (f + 4 * hops) % count) for f in range(c...  7.54 us
    pallas_call x1, Pallas kernels, input_grad_part(): pl.pallas_call(functools.partial(input_grad_kernel, scale, len(own), len(...  6.69 us
  transfers between devices with their start and end apart: 42, of which 22 were waited for; matrix products, arithmetic and copies ran while one was open for 7% of the time, Pallas kernels for 12%

profile of v1, /device:TPU:0, one launch (start us, length us, event | category | flops | bytes accessed | tf_op | source)
XLA Modules:
  0.0 226.1 jit_solution(4370547141865549916)
XLA Ops:
  0.6 3.0 %collective-permute-start.4 = (bf16[320,2560]{1,0:T(8,128)(2,1)}, bf16[320,2560]{1,0:T(8,128)(2,1)S(1)}, u32[]{:S(2)}, u32[]{:S(2)}) collective-permute-start(bf16[320,2560]{1,0:T(8,128)(2,1)} %bitcast.15), channel_id=1, source_target_pairs={{0,16},{8,24},{16,0},{24,8},{1,17},{9,25},{17,1},{25,9},{2,18},{10... | collective-permute-start | bytes 4915208 | tf_op jit(solution)/shard_map/ppermute | solution.py:43
  3.7 1.3 copy-done.6
  5.0 1.4 split.1
  6.4 1.6 collective-permute-start
  8.0 2.6 %fusion.5 = (bf16[320,640]{1,0:T(8,128)(2,1)}, bf16[320,640]{1,0:T(8,128)(2,1)}, bf16[320,640]{1,0:T(8,128)(2,1)}, bf16[320,640]{1,0:T(8,128)(2,1)}) fusion(bf16[320,2560]{1,0:T(8,128)(2,1)} %bitcast.17), kind=kLoop, calls=%fused_computation.28 | loop fusion | bytes 3276800 | tf_op jit(solution)/shard_map/slice | solution.py:327
  10.6 2.6 %collective-permute-start.7 = (bf16[320,640]{1,0:T(8,128)(2,1)}, bf16[320,640]{1,0:T(8,128)(2,1)S(1)}, u32[]{:S(2)}, u32[]{:S(2)}) collective-permute-start(bf16[320,640]{1,0:T(8,128)(2,1)} %get-tuple-element.89), channel_id=1, source_target_pairs={{0,4},{1,5},{2,6},{3,7},{4,0},{5,1},{6,2},{7,3},{8,12},{9,13},{10,... | collective-permute-start | bytes 1228808 | tf_op jit(solution)/shard_map/ppermute | solution.py:53
  13.5 1.4 convert_bitcast_fusion
  14.9 1.1 constant_dynamic-update-slice_fusion.1
  16.0 33.8 %collective-permute-done.2.refs_0_ = bf16[320,640]{1,0:T(8,128)(2,1)} collective-permute-done((bf16[320,640]{1,0:T(8,128)(2,1)}, bf16[320,640]{1,0:T(8,128)(2,1)}, u32[]{:S(2)}, u32[]{:S(2)}) %collective-permute-start.2) | collective-permute-done | bytes 409632 | tf_op jit(solution)/shard_map/ppermute | solution.py:53
  50.4 1.1 constant_dynamic-update-slice_fusion.x_ref
  51.5 1.7 constant_dynamic-slice_fusion.3
  53.2 4.0 %forward_part.4 = (bf16[1280,640]{1,0:T(8,128)(2,1)S(1)}, f32[256,640]{1,0:T(8,128)S(1)}, bf16[256,640]{1,0:T(8,128)(2,1)}) custom-call(s32[4]{0:T(128)S(1)} %pad_add_fusion.place, bf16[512,1280]{1,0:T(8,128)(2,1)S(1)} %constant_dynamic-update-slice_fusion.x_ref, bf16[320,2560]{1,0:T(8,128)(2,1)} %bitcast.18, ...), custom_call_target="tpu_custom_call" | custom-call | flops 8388608 | bytes 45875 | tf_op jit(solution)/shard_map/forward_part/pallas_call | solution.py:72
  57.2 1.2 copy-done.1
  58.3 0.9 copy-done.7
  59.7 1.1 pad_maximum_fusion
  61.1 0.7 copy-done.12
  61.8 3.1 %collective-permute-start.10 = (bf16[256,640]{1,0:T(8,128)(2,1)}, bf16[256,640]{1,0:T(8,128)(2,1)}, u32[]{:S(2)}, u32[]{:S(2)}) collective-permute-start(bf16[256,640]{1,0:T(8,128)(2,1)} %get-tuple-element.47), channel_id=1, source_target_pairs={{0,2},{1,3},{2,0},{3,1},{4,6},{5,7},{6,4},{7,5},{8,10},{9,11},{10,... | collective-permute-start | bytes 983048 | tf_op jit(solution)/shard_map/ppermute | solution.py:48
  64.9 1.0 copy-done.13
  65.9 3.7 %forward_part.5 = (bf16[1280,640]{1,0:T(8,128)(2,1)S(1)}, f32[256,640]{1,0:T(8,128)S(1)}, bf16[256,640]{1,0:T(8,128)(2,1)}) custom-call(s32[4]{0:T(128)S(1)} %pad_add_fusion.place, bf16[512,1280]{1,0:T(8,128)(2,1)S(1)} %constant_dynamic-update-slice_fusion.x_ref, bf16[320,2560]{1,0:T(8,128)(2,1)} %bitcast.19, ...), custom_call_target="tpu_custom_call" | custom-call | flops 8388608 | bytes 45875 | tf_op jit(solution)/shard_map/forward_part/pallas_call | solution.py:72
  69.6 1.2 copy-done.3
  70.8 0.9 copy-done.9
  71.7 11.0 %collective-permute-done.9.refs_0_ = bf16[320,640]{1,0:T(8,128)(2,1)} collective-permute-done((bf16[320,640]{1,0:T(8,128)(2,1)}, bf16[320,640]{1,0:T(8,128)(2,1)}, u32[]{:S(2)}, u32[]{:S(2)}) %collective-permute-start.9) | collective-permute-done | bytes 409632 | tf_op jit(solution)/shard_map/ppermute | solution.py:53
  82.7 1.7 collective-permute-start.13
  84.4 2.4 %maximum_bitcast_fusion = bf16[640,1024]{0,1:T(8,128)(2,1)} fusion(bf16[512,640]{1,0:T(8,128)(2,1)} %collective-permute-done.6, bf16[512,320]{1,0:T(8,128)(2,1)S(1)} %copy-done.16, bf16[512,320]{1,0:T(8,128)(2,1)S(1)} %copy-done.15), kind=kLoop, calls=%fused_computation.3 | loop fusion | flops 3932160 | bytes 2621440 | tf_op jit(solution)/shard_map/transpose | solution.py:344
  86.8 2.5 %copy.11 = bf16[640,1024]{1,0:T(8,128)(2,1)} copy(bf16[640,1024]{0,1:T(8,128)(2,1)} %maximum_bitcast_fusion) | data formatting | bytes 2621440 | tf_op jit(solution)/shard_map/transpose | solution.py:344
  89.3 2.3 %fusion = bf16[2,2,160,1024]{3,2,0,1:T(8,128)(2,1)S(1)} fusion(bf16[2,2,160,1024]{3,2,1,0:T(8,128)(2,1)} %bitcast.26, pred[]{:T(512)S(6)} %eq.9), kind=kLoop, calls=%fused_computation.2 | loop fusion | flops 655360 | bytes 2621441 | tf_op jit(solution)/shard_map/transpose | solution.py:346
  91.7 3.2 %forward_part.6 = (bf16[1280,640]{1,0:T(8,128)(2,1)S(1)}, f32[256,640]{1,0:T(8,128)S(1)}, bf16[256,640]{1,0:T(8,128)(2,1)S(1)}) custom-call(s32[4]{0:T(128)S(1)} %pad_add_fusion.place, bf16[512,1280]{1,0:T(8,128)(2,1)S(1)} %constant_dynamic-update-slice_fusion.x_ref, bf16[320,2560]{1,0:T(8,128)(2,1)} %bitcast.20, ...), custom_call_target="tpu_custom_call" | custom-call | flops 8388608 | bytes 45875 | tf_op jit(solution)/shard_map/forward_part/pallas_call | solution.py:72
  94.9 1.2 copy-done.4
  96.1 6.4 %collective-permute-done.12.refs_0_ = bf16[320,640]{1,0:T(8,128)(2,1)S(1)} collective-permute-done((bf16[320,640]{1,0:T(8,128)(2,1)}, bf16[320,640]{1,0:T(8,128)(2,1)S(1)}, u32[]{:S(2)}, u32[]{:S(2)}) %collective-permute-start.12) | collective-permute-done | bytes 409632 | tf_op jit(solution)/shard_map/ppermute | solution.py:53
  102.7 1.6 collective-permute-done.14.refs_1_
  104.3 3.0 %forward_part.7 = (bf16[1280,640]{1,0:T(8,128)(2,1)S(1)}, f32[256,640]{1,0:T(8,128)S(1)}, bf16[256,640]{1,0:T(8,128)(2,1)S(1)}) custom-call(s32[4]{0:T(128)S(1)} %pad_add_fusion.place, bf16[512,1280]{1,0:T(8,128)(2,1)S(1)} %constant_dynamic-update-slice_fusion.x_ref, bf16[320,2560]{1,0:T(8,128)(2,1)} %bitcast.21, ...), custom_call_target="tpu_custom_call" | custom-call | flops 8388608 | bytes 45875 | tf_op jit(solution)/shard_map/forward_part/pallas_call | solution.py:72
  107.3 1.2 copy-done.5
  108.8 4.3 %collective-permute-done.15.refs_6_ = bf16[256,640]{1,0:T(8,128)(2,1)S(1)} collective-permute-done((bf16[256,640]{1,0:T(8,128)(2,1)S(1)}, bf16[256,640]{1,0:T(8,128)(2,1)S(1)}, u32[]{:S(2)}, u32[]{:S(2)}) %collective-permute-start.15) | collective-permute-done | bytes 327712 | tf_op jit(solution)/shard_map/ppermute | solution.py:48
  113.2 6.5 %collective-permute-done.16.refs_7_ = bf16[256,640]{1,0:T(8,128)(2,1)S(1)} collective-permute-done((bf16[256,640]{1,0:T(8,128)(2,1)S(1)}, bf16[256,640]{1,0:T(8,128)(2,1)S(1)}, u32[]{:S(2)}, u32[]{:S(2)}) %collective-permute-start.16) | collective-permute-done | bytes 327712 | tf_op jit(solution)/shard_map/ppermute | solution.py:48
  119.7 3.6 %norm_cot.1 = (bf16[256,640]{1,0:T(8,128)(2,1)S(1)}, bf16[256,640]{1,0:T(8,128)(2,1)S(1)}, bf16[256,640]{1,0:T(8,128)(2,1)S(1)}, bf16[256,640]{1,0:T(8,128)(2,1)S(1)}) custom-call(bf16[256,2560]{1,0:T(8,128)(2,1)} %res_ref.1, bf16[256,2560]{1,0:T(8,128)(2,1)} %up_ref.1, f32[1,2560]{1,0:T(1,128)S(1)} %reshape.24.gain_ref, f32[256,640]{1,0:T(8,128)S(1)} %copy-done.8, ...), custom_call_target="tpu_custom_call" | custom-call | flops 131072 | bytes 78643 | tf_op jit(solution)/shard_map/norm_cot/pallas_call | solution.py:128
  123.6 9.0 %collective-permute-done.17.refs_1_.refs_4_ = bf16[256,640]{1,0:T(8,128)(2,1)S(1)} collective-permute-done((bf16[256,640]{1,0:T(8,128)(2,1)S(1)}, bf16[256,640]{1,0:T(8,128)(2,1)S(1)}, u32[]{:S(2)}, u32[]{:S(2)}) %collective-permute-start.17) | collective-permute-done | bytes 327712 | tf_op jit(solution)/shard_map/ppermute | solution.py:48
  132.6 1.6 collective-permute-done.19.refs_3_
  134.3 1.2 gradient_part.4
  135.4 1.6 collective-permute-start.20
  137.5 1.6 collective-permute-start.23
  139.1 8.6 %collective-permute-done.21.refs_1_.refs_6_ = bf16[256,640]{1,0:T(8,128)(2,1)S(1)} collective-permute-done((bf16[256,640]{1,0:T(8,128)(2,1)S(1)}, bf16[256,640]{1,0:T(8,128)(2,1)S(1)}, u32[]{:S(2)}, u32[]{:S(2)}) %collective-permute-start.21) | collective-permute-done | bytes 327712 | tf_op jit(solution)/shard_map/ppermute | solution.py:48
  148.1 5.4 %collective-permute-done.23.refs_1_.refs_5_ = bf16[256,640]{1,0:T(8,128)(2,1)S(1)} collective-permute-done((bf16[256,640]{1,0:T(8,128)(2,1)S(1)}, bf16[256,640]{1,0:T(8,128)(2,1)S(1)}, u32[]{:S(2)}, u32[]{:S(2)}) %collective-permute-start.23) | collective-permute-done | bytes 327712 | tf_op jit(solution)/shard_map/ppermute | solution.py:48
  154.1 2.6 %collective-permute-start.27 = (bf16[160,640]{1,0:T(8,128)(2,1)S(1)}, bf16[160,640]{1,0:T(8,128)(2,1)S(1)}, u32[]{:S(2)}, u32[]{:S(2)}) collective-permute-start(bf16[160,640]{1,0:T(8,128)(2,1)S(1)} %slice.75), channel_id=1, source_target_pairs={{0,4},{1,5},{2,6},{3,7},{4,0},{5,1},{6,2},{7,3},{8,12},{9,13},{10,... | collective-permute-start | bytes 614408 | tf_op jit(solution)/shard_map/ppermute | solution.py:53
  156.7 1.2 gradient_part.5
  158.5 9.6 %collective-permute-done.28.refs_1_.refs_7_ = bf16[256,640]{1,0:T(8,128)(2,1)S(1)} collective-permute-done((bf16[256,640]{1,0:T(8,128)(2,1)S(1)}, bf16[256,640]{1,0:T(8,128)(2,1)S(1)}, u32[]{:S(2)}, u32[]{:S(2)}) %collective-permute-start.28) | collective-permute-done | bytes 327712 | tf_op jit(solution)/shard_map/ppermute | solution.py:48
  170.1 1.2 gradient_part.6
  171.3 0.7 collective-permute-start.31
  172.1 0.9 collective-permute-start.32
  173.0 3.6 %collective-permute-done.33.refs_4_ = bf16[160,640]{1,0:T(8,128)(2,1)S(1)} collective-permute-done((bf16[160,640]{1,0:T(8,128)(2,1)S(1)}, bf16[160,640]{1,0:T(8,128)(2,1)S(1)}, u32[]{:S(2)}, u32[]{:S(2)}) %collective-permute-start.33) | collective-permute-done | bytes 204832 | tf_op jit(solution)/shard_map/ppermute | solution.py:43
  176.6 7.6 %collective-permute-done.32 = bf16[160,640]{1,0:T(8,128)(2,1)S(1)} collective-permute-done((bf16[160,640]{1,0:T(8,128)(2,1)S(1)}, bf16[160,640]{1,0:T(8,128)(2,1)S(1)}, u32[]{:S(2)}, u32[]{:S(2)}) %collective-permute-start.32) | collective-permute-done | bytes 204832 | tf_op jit(solution)/shard_map/ppermute | solution.py:53
  184.1 0.8 collective-permute-done.31
  184.9 1.2 gradient_part.7
  186.1 0.6 collective-permute-start.37
  186.8 1.6 collective-permute-start.39
  189.0 6.7 %input_grad_part.1 = (bf16[256,1280]{1,0:T(8,128)(2,1)S(1)}, bf16[256,1280]{1,0:T(8,128)(2,1)S(1)}) custom-call(bf16[256,640]{1,0:T(8,128)(2,1)S(1)} %get-tuple-element.68.refs_0_, bf16[256,640]{1,0:T(8,128)(2,1)S(1)} %get-tuple-element.59.refs_0_.refs_1_, bf16[256,640]{1,0:T(8,128)(2,1)S(1)} %get-tuple-element.57.refs_0_.refs_2_, ...), custom_call_target="tpu_custom_call" | custom-call | flops 33554432 | bytes 104857 | tf_op jit(solution)/shard_map/input_grad_part/pallas_call | solution.py:194
  195.7 2.5 %collective-permute-start.35 = (bf16[256,1280]{1,0:T(8,128)(2,1)S(1)}, bf16[256,1280]{1,0:T(8,128)(2,1)S(1)}, u32[]{:S(2)}, u32[]{:S(2)}) collective-permute-start(bf16[256,1280]{1,0:T(8,128)(2,1)S(1)} %get-tuple-element.74), channel_id=1, source_target_pairs={{0,2},{1,3},{2,0},{3,1},{4,6},{5,7},{6,4},{7,5},{8,10},{9,11},{10,... | collective-permute-start | bytes 1966088 | tf_op jit(solution)/shard_map/ppermute | solution.py:48
  198.7 0.6 collective-permute-start.38
  199.9 0.6 collective-permute-start.40
  200.5 15.2 %collective-permute-done.38 = bf16[160,640]{1,0:T(8,128)(2,1)S(1)} collective-permute-done((bf16[160,640]{1,0:T(8,128)(2,1)S(1)}, bf16[160,640]{1,0:T(8,128)(2,1)S(1)}, u32[]{:S(2)}, u32[]{:S(2)}) %collective-permute-start.38) | collective-permute-done | bytes 204832 | tf_op jit(solution)/shard_map/ppermute | solution.py:53
  215.7 0.6 collective-permute-start.41
  216.3 1.8 collective-permute-done.35.got_ref
  218.2 1.6 interleave.1
  219.8 1.8 collective-permute-done.41.refs_7_
  221.6 4.6 %update.1 = (bf16[1,320,2560]{2,1,0:T(8,128)(2,1)}, f32[1,320,2560]{2,1,0:T(8,128)}) custom-call(s32[1]{0:T(128)} %bitcast.11.place, bf16[1,320,2560]{2,1,0:T(8,128)(2,1)S(1)} %copy-done, bf16[320,2560]{1,0:T(8,128)(2,1)S(1)} %collective-permute-done.4.pw_ref, f32[1,320,2560]{2,1,0:T(8,128)} %m_ref.1, bf16[320,2560]{1,0:T(8,128)(2,1)} %collective-permute-done.5.pm_ref, ...), custom_call_target="tpu_custom_call" | custom-call | flops 81920 | bytes 147456 | tf_op jit(solution)/shard_map/update/pallas_call | solution.py:294
  (93 shorter events, 8.8 us)
Async XLA Ops:
  0.6 82.0 %collective-permute-start.4 = (bf16[320,2560]{1,0:T(8,128)(2,1)}, bf16[320,2560]{1,0:T(8,128)(2,1)S(1)}, u32[]{:S(2)}, u32[]{:S(2)}) collective-permute-start(bf16[320,2560]{1,0:T(8,128)(2,1)} %bitcast.15), channel_id=1, source_target_pairs={{0,16},{8,24},{16,0},{24,8},{1,17},{9,25},{17,1},{25,9},{2,18},{10... | collective-permute-start | bytes 4915208 | tf_op jit(solution)/shard_map/ppermute | solution.py:43
  3.7 49.5 %collective-permute-start.1 = (bf16[320,2560]{1,0:T(8,128)(2,1)}, bf16[320,2560]{1,0:T(8,128)(2,1)}, u32[]{:S(2)}, u32[]{:S(2)}) collective-permute-start(bf16[320,2560]{1,0:T(8,128)(2,1)} %bitcast.16), channel_id=1, source_target_pairs={{0,1},{1,0},{2,3},{3,2},{4,5},{5,4},{6,7},{7,6},{8,9},{9,8},{10,11... | collective-permute-start | bytes 4915208 | tf_op jit(solution)/shard_map/ppermute | solution.py:48
  3.7 1.3 copy-start.6
  6.4 4.2 %copy-start.11 = (bf16[256,1280]{1,0:T(8,128)(2,1)}, bf16[256,1280]{1,0:T(8,128)(2,1)S(1)}, u32[]{:S(2)}) copy-start(bf16[256,1280]{1,0:T(8,128)(2,1)S(1)} %get-tuple-element.41) | copy-start | bytes 1966084
  6.4 7.1 %copy-start.14 = (f32[1,320,2560]{2,1,0:T(8,128)S(1)}, f32[1,320,2560]{2,1,0:T(8,128)}, u32[]{:S(2)}) copy-start(f32[1,320,2560]{2,1,0:T(8,128)} %m_ref.1) | copy-start | bytes 9830404
  6.4 43.9 %collective-permute-start = (bf16[256,1280]{1,0:T(8,128)(2,1)}, bf16[256,1280]{1,0:T(8,128)(2,1)}, u32[]{:S(2)}, u32[]{:S(2)}) collective-permute-start(bf16[256,1280]{1,0:T(8,128)(2,1)} %get-tuple-element.42), channel_id=1, source_target_pairs={{0,2},{1,3},{2,0},{3,1},{4,6},{5,7},{6,4},{7,5},{8,10},{9,11},{10,... | collective-permute-start | bytes 1966088 | tf_op jit(solution)/shard_map/ppermute | solution.py:48
  10.6 48.6 %collective-permute-start.7 = (bf16[320,640]{1,0:T(8,128)(2,1)}, bf16[320,640]{1,0:T(8,128)(2,1)S(1)}, u32[]{:S(2)}, u32[]{:S(2)}) collective-permute-start(bf16[320,640]{1,0:T(8,128)(2,1)} %get-tuple-element.89), channel_id=1, source_target_pairs={{0,4},{1,5},{2,6},{3,7},{4,0},{5,1},{6,2},{7,3},{8,12},{9,13},{10,... | collective-permute-start | bytes 1228808 | tf_op jit(solution)/shard_map/ppermute | solution.py:53
  13.2 36.6 %collective-permute-start.2 = (bf16[320,640]{1,0:T(8,128)(2,1)}, bf16[320,640]{1,0:T(8,128)(2,1)}, u32[]{:S(2)}, u32[]{:S(2)}) collective-permute-start(bf16[320,640]{1,0:T(8,128)(2,1)} %get-tuple-element.90), channel_id=1, source_target_pairs={{0,4},{1,5},{2,6},{3,7},{4,0},{5,1},{6,2},{7,3},{8,12},{9,13},{10,... | collective-permute-start | bytes 1228808 | tf_op jit(solution)/shard_map/ppermute | solution.py:53
  49.8 52.7 %collective-permute-start.5 = (bf16[320,2560]{1,0:T(8,128)(2,1)}, bf16[320,2560]{1,0:T(8,128)(2,1)}, u32[]{:S(2)}, u32[]{:S(2)}) collective-permute-start(bf16[320,2560]{1,0:T(8,128)(2,1)} %convert_bitcast_fusion), channel_id=1, source_target_pairs={{0,16},{8,24},{16,0},{24,8},{1,17},{9,25},{17,1},{25,9},{2,18},{10... | collective-permute-start | bytes 4915208 | tf_op jit(solution)/shard_map/ppermute | solution.py:43
  50.3 2.9 %collective-permute-start.3 = (bf16[320,640]{1,0:T(8,128)(2,1)}, bf16[320,640]{1,0:T(8,128)(2,1)}, u32[]{:S(2)}, u32[]{:S(2)}) collective-permute-start(bf16[320,640]{1,0:T(8,128)(2,1)} %collective-permute-done.2.refs_0_), channel_id=1, source_target_pairs={{0,1},{1,0},{2,3},{3,2},{4,5},{5,4},{6,7},{7,6},{8,9},{9,8},{10,11... | collective-permute-start | bytes 1228808 | tf_op jit(solution)/shard_map/ppermute | solution.py:48
  57.2 1.2 copy-start.1
  58.3 0.9 copy-start.7
  59.2 1.9 collective-permute-start.8
  60.8 23.6 %collective-permute-start.6 = (bf16[512,640]{1,0:T(8,128)(2,1)}, bf16[512,640]{1,0:T(8,128)(2,1)}, u32[]{:S(2)}, u32[]{:S(2)}) collective-permute-start(bf16[512,640]{1,0:T(8,128)(2,1)} %pad_maximum_fusion), channel_id=1, source_target_pairs={{0,1},{1,0},{2,3},{3,2},{4,5},{5,4},{6,7},{7,6},{8,9},{9,8},{10,11... | collective-permute-start | bytes 1966088 | tf_op jit(solution)/shard_map/ppermute | solution.py:48
  60.8 21.9 %collective-permute-start.9 = (bf16[320,640]{1,0:T(8,128)(2,1)}, bf16[320,640]{1,0:T(8,128)(2,1)}, u32[]{:S(2)}, u32[]{:S(2)}) collective-permute-start(bf16[320,640]{1,0:T(8,128)(2,1)} %get-tuple-element.88), channel_id=1, source_target_pairs={{0,4},{1,5},{2,6},{3,7},{4,0},{5,1},{6,2},{7,3},{8,12},{9,13},{10,... | collective-permute-start | bytes 1228808 | tf_op jit(solution)/shard_map/ppermute | solution.py:53
  61.1 0.8 copy-start.12
  61.8 20.8 %collective-permute-start.10 = (bf16[256,640]{1,0:T(8,128)(2,1)}, bf16[256,640]{1,0:T(8,128)(2,1)}, u32[]{:S(2)}, u32[]{:S(2)}) collective-permute-start(bf16[256,640]{1,0:T(8,128)(2,1)} %get-tuple-element.47), channel_id=1, source_target_pairs={{0,2},{1,3},{2,0},{3,1},{4,6},{5,7},{6,4},{7,5},{8,10},{9,11},{10,... | collective-permute-start | bytes 983048 | tf_op jit(solution)/shard_map/ppermute | solution.py:48
  64.9 1.0 copy-start.13
  65.9 18.5 %copy-start.15 = (bf16[512,320]{1,0:T(8,128)(2,1)S(1)}, bf16[512,320]{1,0:T(8,128)(2,1)}, u32[]{:S(2)}) copy-start(bf16[512,320]{1,0:T(8,128)(2,1)} %get-tuple-element.91) | copy-start | bytes 983044
  65.9 18.5 %copy-start.16 = (bf16[512,320]{1,0:T(8,128)(2,1)S(1)}, bf16[512,320]{1,0:T(8,128)(2,1)}, u32[]{:S(2)}) copy-start(bf16[512,320]{1,0:T(8,128)(2,1)} %get-tuple-element.94) | copy-start | bytes 983044
  69.6 1.2 copy-start.3
  70.8 0.9 copy-start.9
  82.7 19.9 %collective-permute-start.12 = (bf16[320,640]{1,0:T(8,128)(2,1)}, bf16[320,640]{1,0:T(8,128)(2,1)S(1)}, u32[]{:S(2)}, u32[]{:S(2)}) collective-permute-start(bf16[320,640]{1,0:T(8,128)(2,1)} %get-tuple-element.87), channel_id=1, source_target_pairs={{0,4},{1,5},{2,6},{3,7},{4,0},{5,1},{6,2},{7,3},{8,12},{9,13},{10,... | collective-permute-start | bytes 1228808 | tf_op jit(solution)/shard_map/ppermute | solution.py:53
  82.7 19.9 %collective-permute-start.13 = (bf16[256,640]{1,0:T(8,128)(2,1)}, bf16[256,640]{1,0:T(8,128)(2,1)}, u32[]{:S(2)}, u32[]{:S(2)}) collective-permute-start(bf16[256,640]{1,0:T(8,128)(2,1)} %get-tuple-element.50), channel_id=1, source_target_pairs={{0,2},{1,3},{2,0},{3,1},{4,6},{5,7},{6,4},{7,5},{8,10},{9,11},{10,... | collective-permute-start | bytes 983048 | tf_op jit(solution)/shard_map/ppermute | solution.py:48
  84.4 7.3 %collective-permute-start.11 = (bf16[320,640]{1,0:T(8,128)(2,1)}, bf16[320,640]{1,0:T(8,128)(2,1)}, u32[]{:S(2)}, u32[]{:S(2)}) collective-permute-start(bf16[320,640]{1,0:T(8,128)(2,1)} %collective-permute-done.9.refs_0_), channel_id=1, source_target_pairs={{0,1},{1,0},{2,3},{3,2},{4,5},{5,4},{6,7},{7,6},{8,9},{9,8},{10,11... | collective-permute-start | bytes 1228808 | tf_op jit(solution)/shard_map/ppermute | solution.py:48
  94.9 1.2 copy-start.4
  102.5 1.7 collective-permute-start.14
  102.5 6.3 %copy-start.17 = (f32[2560]{0:T(1024)S(1)}, f32[2560]{0:T(1024)}, u32[]{:S(2)}) copy-start(f32[2560]{0:T(1024)} %param.9) | copy-start | bytes 30724
  102.6 17.2 %copy-start.8 = (f32[256,640]{1,0:T(8,128)S(1)}, f32[256,640]{1,0:T(8,128)}, u32[]{:S(2)}) copy-start(f32[256,640]{1,0:T(8,128)} %copy-done.7) | copy-start | bytes 1966084
  102.6 17.1 %copy-start.10 = (f32[256,640]{1,0:T(8,128)S(1)}, f32[256,640]{1,0:T(8,128)}, u32[]{:S(2)}) copy-start(f32[256,640]{1,0:T(8,128)} %copy-done.9) | copy-start | bytes 1966084
  102.6 10.6 %collective-permute-start.15 = (bf16[256,640]{1,0:T(8,128)(2,1)S(1)}, bf16[256,640]{1,0:T(8,128)(2,1)S(1)}, u32[]{:S(2)}, u32[]{:S(2)}) collective-permute-start(bf16[256,640]{1,0:T(8,128)(2,1)S(1)} %get-tuple-element.53), channel_id=1, source_target_pairs={{0,2},{1,3},{2,0},{3,1},{4,6},{5,7},{6,4},{7,5},{8,10},{9,11},{10,... | collective-permute-start | bytes 983048 | tf_op jit(solution)/shard_map/ppermute | solution.py:48
  107.3 1.2 copy-start.5
  108.4 11.3 %collective-permute-start.16 = (bf16[256,640]{1,0:T(8,128)(2,1)S(1)}, bf16[256,640]{1,0:T(8,128)(2,1)S(1)}, u32[]{:S(2)}, u32[]{:S(2)}) collective-permute-start(bf16[256,640]{1,0:T(8,128)(2,1)S(1)} %get-tuple-element.54), channel_id=1, source_target_pairs={{0,2},{1,3},{2,0},{3,1},{4,6},{5,7},{6,4},{7,5},{8,10},{9,11},{10,... | collective-permute-start | bytes 983048 | tf_op jit(solution)/shard_map/ppermute | solution.py:48
  123.3 9.3 %collective-permute-start.17 = (bf16[256,640]{1,0:T(8,128)(2,1)S(1)}, bf16[256,640]{1,0:T(8,128)(2,1)S(1)}, u32[]{:S(2)}, u32[]{:S(2)}) collective-permute-start(bf16[256,640]{1,0:T(8,128)(2,1)S(1)} %get-tuple-element.68.refs_0_), channel_id=1, source_target_pairs={{0,2},{1,3},{2,0},{3,1},{4,6},{5,7},{6,4},{7,5},{8,10},{9,11},{10,... | collective-permute-start | bytes 983048 | tf_op jit(solution)/shard_map/ppermute | solution.py:48
  123.6 9.0 %collective-permute-start.18 = (bf16[256,640]{1,0:T(8,128)(2,1)S(1)}, bf16[256,640]{1,0:T(8,128)(2,1)S(1)}, u32[]{:S(2)}, u32[]{:S(2)}) collective-permute-start(bf16[256,640]{1,0:T(8,128)(2,1)S(1)} %get-tuple-element.68.refs_0_), channel_id=1, source_target_pairs={{0,1},{1,0},{2,3},{3,2},{4,5},{5,4},{6,7},{7,6},{8,9},{9,8},{10,11... | collective-permute-start | bytes 983048 | tf_op jit(solution)/shard_map/ppermute | solution.py:48
  132.6 1.6 collective-permute-start.19
  135.4 18.5 %collective-permute-start.20 = (bf16[320,640]{1,0:T(8,128)(2,1)S(1)}, bf16[320,640]{1,0:T(8,128)(2,1)S(1)}, u32[]{:S(2)}, u32[]{:S(2)}) collective-permute-start(bf16[320,640]{1,0:T(8,128)(2,1)S(1)} %get-tuple-element.56), channel_id=1, source_target_pairs={{0,16},{8,24},{16,0},{24,8},{1,17},{9,25},{17,1},{25,9},{2,18},{10... | collective-permute-start | bytes 1228808 | tf_op jit(solution)/shard_map/ppermute | solution.py:43
  137.0 10.6 %collective-permute-start.21 = (bf16[256,640]{1,0:T(8,128)(2,1)S(1)}, bf16[256,640]{1,0:T(8,128)(2,1)S(1)}, u32[]{:S(2)}, u32[]{:S(2)}) collective-permute-start(bf16[256,640]{1,0:T(8,128)(2,1)S(1)} %get-tuple-element.57.refs_0_.refs_2_), channel_id=1, source_target_pairs={{0,2},{1,3},{2,0},{3,1},{4,6},{5,7},{6,4},{7,5},{8,10},{9,11},{10,... | collective-permute-start | bytes 983048 | tf_op jit(solution)/shard_map/ppermute | solution.py:48
  137.5 16.0 %collective-permute-start.23 = (bf16[256,640]{1,0:T(8,128)(2,1)S(1)}, bf16[256,640]{1,0:T(8,128)(2,1)S(1)}, u32[]{:S(2)}, u32[]{:S(2)}) collective-permute-start(bf16[256,640]{1,0:T(8,128)(2,1)S(1)} %get-tuple-element.59.refs_0_.refs_1_), channel_id=1, source_target_pairs={{0,2},{1,3},{2,0},{3,1},{4,6},{5,7},{6,4},{7,5},{8,10},{9,11},{10,... | collective-permute-start | bytes 983048 | tf_op jit(solution)/shard_map/ppermute | solution.py:48
  147.6 9.0 %collective-permute-start.22 = (bf16[256,640]{1,0:T(8,128)(2,1)S(1)}, bf16[256,640]{1,0:T(8,128)(2,1)S(1)}, u32[]{:S(2)}, u32[]{:S(2)}) collective-permute-start(bf16[256,640]{1,0:T(8,128)(2,1)S(1)} %collective-permute-done.21.refs_1_.refs_6_), channel_id=1, source_target_pairs={{0,1},{1,0},{2,3},{3,2},{4,5},{5,4},{6,7},{7,6},{8,9},{9,8},{10,11... | collective-permute-start | bytes 983048 | tf_op jit(solution)/shard_map/ppermute | solution.py:48
  147.6 9.0 %collective-permute-start.24 = (bf16[256,640]{1,0:T(8,128)(2,1)S(1)}, bf16[256,640]{1,0:T(8,128)(2,1)S(1)}, u32[]{:S(2)}, u32[]{:S(2)}) collective-permute-start(bf16[256,640]{1,0:T(8,128)(2,1)S(1)} %get-tuple-element.59.refs_0_.refs_1_), channel_id=1, source_target_pairs={{0,1},{1,0},{2,3},{3,2},{4,5},{5,4},{6,7},{7,6},{8,9},{9,8},{10,11... | collective-permute-start | bytes 983048 | tf_op jit(solution)/shard_map/ppermute | solution.py:48
  153.5 3.2 %collective-permute-start.25 = (bf16[256,640]{1,0:T(8,128)(2,1)S(1)}, bf16[256,640]{1,0:T(8,128)(2,1)S(1)}, u32[]{:S(2)}, u32[]{:S(2)}) collective-permute-start(bf16[256,640]{1,0:T(8,128)(2,1)S(1)} %collective-permute-done.23.refs_1_.refs_5_), channel_id=1, source_target_pairs={{0,1},{1,0},{2,3},{3,2},{4,5},{5,4},{6,7},{7,6},{8,9},{9,8},{10,11... | collective-permute-start | bytes 983048 | tf_op jit(solution)/shard_map/ppermute | solution.py:48
  153.5 14.5 %collective-permute-start.28 = (bf16[256,640]{1,0:T(8,128)(2,1)S(1)}, bf16[256,640]{1,0:T(8,128)(2,1)S(1)}, u32[]{:S(2)}, u32[]{:S(2)}) collective-permute-start(bf16[256,640]{1,0:T(8,128)(2,1)S(1)} %get-tuple-element.62.refs_0_.refs_3_), channel_id=1, source_target_pairs={{0,2},{1,3},{2,0},{3,1},{4,6},{5,7},{6,4},{7,5},{8,10},{9,11},{10,... | collective-permute-start | bytes 983048 | tf_op jit(solution)/shard_map/ppermute | solution.py:48
  154.1 14.5 %collective-permute-start.27 = (bf16[160,640]{1,0:T(8,128)(2,1)S(1)}, bf16[160,640]{1,0:T(8,128)(2,1)S(1)}, u32[]{:S(2)}, u32[]{:S(2)}) collective-permute-start(bf16[160,640]{1,0:T(8,128)(2,1)S(1)} %slice.75), channel_id=1, source_target_pairs={{0,4},{1,5},{2,6},{3,7},{4,0},{5,1},{6,2},{7,3},{8,12},{9,13},{10,... | collective-permute-start | bytes 614408 | tf_op jit(solution)/shard_map/ppermute | solution.py:53
  157.9 11.8 %collective-permute-start.26 = (bf16[320,640]{1,0:T(8,128)(2,1)S(1)}, bf16[320,640]{1,0:T(8,128)(2,1)S(1)}, u32[]{:S(2)}, u32[]{:S(2)}) collective-permute-start(bf16[320,640]{1,0:T(8,128)(2,1)S(1)} %get-tuple-element.60), channel_id=1, source_target_pairs={{0,16},{8,24},{16,0},{24,8},{1,17},{9,25},{17,1},{25,9},{2,18},{10... | collective-permute-start | bytes 1228808 | tf_op jit(solution)/shard_map/ppermute | solution.py:43
  168.0 1.6 collective-permute-start.29
  168.0 2.1 collective-permute-start.30
  168.5 16.4 %collective-permute-start.34 = (bf16[256,640]{1,0:T(8,128)(2,1)S(1)}, bf16[256,640]{1,0:T(8,128)(2,1)S(1)}, u32[]{:S(2)}, u32[]{:S(2)}) collective-permute-start(bf16[256,640]{1,0:T(8,128)(2,1)S(1)} %get-tuple-element.62.refs_0_.refs_3_), channel_id=1, source_target_pairs={{0,1},{1,0},{2,3},{3,2},{4,5},{5,4},{6,7},{7,6},{8,9},{9,8},{10,11... | collective-permute-start | bytes 983048 | tf_op jit(solution)/shard_map/ppermute | solution.py:48
  168.6 7.9 %collective-permute-start.33 = (bf16[160,640]{1,0:T(8,128)(2,1)S(1)}, bf16[160,640]{1,0:T(8,128)(2,1)S(1)}, u32[]{:S(2)}, u32[]{:S(2)}) collective-permute-start(bf16[160,640]{1,0:T(8,128)(2,1)S(1)} %get-tuple-element.85), channel_id=1, source_target_pairs={{0,16},{8,24},{16,0},{24,8},{1,17},{9,25},{17,1},{25,9},{2,18},{10... | collective-permute-start | bytes 614408 | tf_op jit(solution)/shard_map/ppermute | solution.py:43
  171.3 13.6 %collective-permute-start.31 = (bf16[320,640]{1,0:T(8,128)(2,1)S(1)}, bf16[320,640]{1,0:T(8,128)(2,1)S(1)}, u32[]{:S(2)}, u32[]{:S(2)}) collective-permute-start(bf16[320,640]{1,0:T(8,128)(2,1)S(1)} %get-tuple-element.64), channel_id=1, source_target_pairs={{0,16},{8,24},{16,0},{24,8},{1,17},{9,25},{17,1},{25,9},{2,18},{10... | collective-permute-start | bytes 1228808 | tf_op jit(solution)/shard_map/ppermute | solution.py:43
  172.1 12.0 %collective-permute-start.32 = (bf16[160,640]{1,0:T(8,128)(2,1)S(1)}, bf16[160,640]{1,0:T(8,128)(2,1)S(1)}, u32[]{:S(2)}, u32[]{:S(2)}) collective-permute-start(bf16[160,640]{1,0:T(8,128)(2,1)S(1)} %slice.74), channel_id=1, source_target_pairs={{0,4},{1,5},{2,6},{3,7},{4,0},{5,1},{6,2},{7,3},{8,12},{9,13},{10,... | collective-permute-start | bytes 614408 | tf_op jit(solution)/shard_map/ppermute | solution.py:53
  186.1 12.4 %collective-permute-start.37 = (bf16[320,640]{1,0:T(8,128)(2,1)S(1)}, bf16[320,640]{1,0:T(8,128)(2,1)S(1)}, u32[]{:S(2)}, u32[]{:S(2)}) collective-permute-start(bf16[320,640]{1,0:T(8,128)(2,1)S(1)} %get-tuple-element.76), channel_id=1, source_target_pairs={{0,16},{8,24},{16,0},{24,8},{1,17},{9,25},{17,1},{25,9},{2,18},{10... | collective-permute-start | bytes 1228808 | tf_op jit(solution)/shard_map/ppermute | solution.py:43
  186.8 2.2 copy-start.2
  186.8 33.0 %collective-permute-start.39 = (bf16[160,640]{1,0:T(8,128)(2,1)S(1)}, bf16[160,640]{1,0:T(8,128)(2,1)S(1)}, u32[]{:S(2)}, u32[]{:S(2)}) collective-permute-start(bf16[160,640]{1,0:T(8,128)(2,1)S(1)} %get-tuple-element.83), channel_id=1, source_target_pairs={{0,16},{8,24},{16,0},{24,8},{1,17},{9,25},{17,1},{25,9},{2,18},{10... | collective-permute-start | bytes 614408 | tf_op jit(solution)/shard_map/ppermute | solution.py:43
  188.5 11.4 %collective-permute-start.36 = (bf16[160,640]{1,0:T(8,128)(2,1)S(1)}, bf16[160,640]{1,0:T(8,128)(2,1)S(1)}, u32[]{:S(2)}, u32[]{:S(2)}) collective-permute-start(bf16[160,640]{1,0:T(8,128)(2,1)S(1)} %slice.73), channel_id=1, source_target_pairs={{0,4},{1,5},{2,6},{3,7},{4,0},{5,1},{6,2},{7,3},{8,12},{9,13},{10,... | collective-permute-start | bytes 614408 | tf_op jit(solution)/shard_map/ppermute | solution.py:53
  195.7 22.5 %collective-permute-start.35 = (bf16[256,1280]{1,0:T(8,128)(2,1)S(1)}, bf16[256,1280]{1,0:T(8,128)(2,1)S(1)}, u32[]{:S(2)}, u32[]{:S(2)}) collective-permute-start(bf16[256,1280]{1,0:T(8,128)(2,1)S(1)} %get-tuple-element.74), channel_id=1, source_target_pairs={{0,2},{1,3},{2,0},{3,1},{4,6},{5,7},{6,4},{7,5},{8,10},{9,11},{10,... | collective-permute-start | bytes 1966088 | tf_op jit(solution)/shard_map/ppermute | solution.py:48
  198.7 17.0 %collective-permute-start.38 = (bf16[160,640]{1,0:T(8,128)(2,1)S(1)}, bf16[160,640]{1,0:T(8,128)(2,1)S(1)}, u32[]{:S(2)}, u32[]{:S(2)}) collective-permute-start(bf16[160,640]{1,0:T(8,128)(2,1)S(1)} %slice.72), channel_id=1, source_target_pairs={{0,4},{1,5},{2,6},{3,7},{4,0},{5,1},{6,2},{7,3},{8,12},{9,13},{10,... | collective-permute-start | bytes 614408 | tf_op jit(solution)/shard_map/ppermute | solution.py:53
  199.9 19.9 %collective-permute-start.40 = (bf16[160,640]{1,0:T(8,128)(2,1)S(1)}, bf16[160,640]{1,0:T(8,128)(2,1)S(1)}, u32[]{:S(2)}, u32[]{:S(2)}) collective-permute-start(bf16[160,640]{1,0:T(8,128)(2,1)S(1)} %get-tuple-element.81), channel_id=1, source_target_pairs={{0,16},{8,24},{16,0},{24,8},{1,17},{9,25},{17,1},{25,9},{2,18},{10... | collective-permute-start | bytes 614408 | tf_op jit(solution)/shard_map/ppermute | solution.py:43
  215.7 5.8 %collective-permute-start.41 = (bf16[160,640]{1,0:T(8,128)(2,1)S(1)}, bf16[160,640]{1,0:T(8,128)(2,1)S(1)}, u32[]{:S(2)}, u32[]{:S(2)}) collective-permute-start(bf16[160,640]{1,0:T(8,128)(2,1)S(1)} %get-tuple-element.79), channel_id=1, source_target_pairs={{0,16},{8,24},{16,0},{24,8},{1,17},{9,25},{17,1},{25,9},{2,18},{10... | collective-permute-start | bytes 614408 | tf_op jit(solution)/shard_map/ppermute | solution.py:43
  218.2 3.4 %copy-start = (bf16[1,320,2560]{2,1,0:T(8,128)(2,1)S(1)}, bf16[1,320,2560]{2,1,0:T(8,128)(2,1)}, u32[]{:S(2)}) copy-start(bf16[1,320,2560]{2,1,0:T(8,128)(2,1)} %w_ref.1) | copy-start | bytes 4915204

commit v2 on v1

--- a/solution.py
+++ b/solution.py
@@ -13,8 +13,9 @@
 LEARN_RATE = 0.05
 MOMENTUM_DECAY = 0.9
 
-FWD_CHUNKS = 4
-BWD_CHUNKS = 4
+FWD_PARTS = (8, 8, 4)
+BWD_PARTS = (8, 8, 4)
+IN_FLIGHT = 1
 COST_SHARE = 0.01
 BF = jnp.bfloat16
 F32 = jnp.float32
@@ -53,32 +54,41 @@
     return lax.ppermute(block, "fsdp", [(f, (f + 4 * hops) % count) for f in range(count)])
 
 
-def forward_kernel(scale, rows, n_far, place, x_ref, own_ref, mate_ref, *refs):
-    fars, rest = refs[: 2 * n_far], refs[2 * n_far :]
-    w_ref, keep_ref, give_ref = rest
-    for i, ref in enumerate((own_ref, mate_ref, *fars)):
-        w_ref[pl.ds(pl.multiple_of(place[i] * rows, 16), rows), :] = ref[...]
+def chunks(parts, features):
+    unit = features // sum(parts)
+    return [(sum(parts[:i]) * unit, part * unit) for i, part in enumerate(parts)]
+
+
+def put_rows(place, rows, refs, w_ref, start):
+    for i, ref in enumerate(refs):
+        at = pl.ds(pl.multiple_of(place[i] * rows, 16), rows)
+        w_ref[at, start : start + ref.shape[1]] = ref[...]
+
+
+def forward_kernel(scale, rows, place, x_ref, *refs):
+    pieces, (keep_ref, give_ref, w_ref) = refs[:-3], refs[-3:]
+    put_rows(place, rows, pieces, w_ref, 0)
     part = jnp.dot(x_ref[...], w_ref[...], preferred_element_type=F32) * scale
     tokens = keep_ref.shape[0]
     keep_ref[...] = part[:tokens]
     give_ref[...] = part[tokens:].astype(BF)
 
 
-def forward_part(place, x, own, mate, fars, chunk, width, scale):
+def forward_part(place, x, own, mate, fars, start, width, scale):
     tokens, depth = x.shape[0] // 2, x.shape[1]
     rows = own.shape[0]
-    column = pl.BlockSpec((rows, width), lambda i, place: (0, chunk))
+    column = pl.BlockSpec((rows, width), lambda i, place: (0, start // width))
     full = lambda shape: pl.BlockSpec(shape, lambda i, place: (0, 0))
     return pl.pallas_call(
-        functools.partial(forward_kernel, scale, rows, len(fars) // 2),
+        functools.partial(forward_kernel, scale, rows),
         grid_spec=pltpu.PrefetchScalarGridSpec(
             num_scalar_prefetch=1,
             grid=(1,),
             in_specs=[full(x.shape), column, column] + [full(w.shape) for w in fars],
-            out_specs=[full((depth, width)), full((tokens, width)), full((tokens, width))],
+            out_specs=[full((tokens, width)), full((tokens, width))],
+            scratch_shapes=[pltpu.VMEM((depth, width), BF)],
         ),
         out_shape=[
-            jax.ShapeDtypeStruct((depth, width), BF),
             jax.ShapeDtypeStruct((tokens, width), F32),
             jax.ShapeDtypeStruct((tokens, width), BF),
         ],
@@ -90,13 +100,14 @@
 
 def norm_kernel(n_in, n_out, res_ref, up_ref, gain_ref, *refs):
     keeps, gots, cots = refs[:n_in], refs[n_in : 2 * n_in], refs[2 * n_in :]
-    width = keeps[0].shape[1]
-    features = n_in * width
+    features = res_ref.shape[1]
     summed, scaled = [], []
     square = inner = 0.0
-    for i in range(n_in):
-        cols = slice(i * width, (i + 1) * width)
-        s = res_ref[:, cols].astype(F32) + (keeps[i][...] + gots[i][...].astype(F32))
+    start = 0
+    for keep, got in zip(keeps, gots):
+        cols = slice(start, start + keep.shape[1])
+        start = cols.stop
+        s = res_ref[:, cols].astype(F32) + (keep[...] + got[...].astype(F32))
         c = up_ref[:, cols].astype(F32) * gain_ref[:, cols]
         square += jnp.sum(s * s, axis=-1, keepdims=True)
         inner += jnp.sum(c * s, axis=-1, keepdims=True)
@@ -104,34 +115,31 @@
         scaled.append(c)
     inv_rms = lax.rsqrt(square / features + EPSILON)
     pull = inner / features * inv_rms * inv_rms
-    out_width = cots[0].shape[1]
-    for i in range(n_in):
-        cot = (inv_rms * (scaled[i] - summed[i] * pull)).astype(BF)
-        if n_in == n_out:
-            cots[i][...] = cot
-        else:
-            start = i * width
-            at = start
-            while at < start + width:
-                j = at // out_width
-                end = min((j + 1) * out_width, start + width)
-                cots[j][:, at - j * out_width : end - j * out_width] = cot[:, at - start : end - start]
-                at = end
-
-
-def norm_cot(residual, upstream, gain, keeps, gots, n_out):
+    start = 0
+    for s, c in zip(summed, scaled):
+        cot = (inv_rms * (c - s * pull)).astype(BF)
+        end = start + s.shape[1]
+        first = 0
+        for ref in cots:
+            last = first + ref.shape[1]
+            low, high = max(first, start), min(last, end)
+            if low < high:
+                ref[:, low - first : high - first] = cot[:, low - start : high - start]
+            first = last
+        start = end
+
+
+def norm_cot(residual, upstream, gain, keeps, gots, widths):
     tokens, features = residual.shape
     tile = 64
-    n_in = len(keeps)
-    width, out_width = features // n_in, features // n_out
     row = lambda w: pl.BlockSpec((tile, w), lambda i: (i, 0))
     return pl.pallas_call(
-        functools.partial(norm_kernel, n_in, n_out),
+        functools.partial(norm_kernel, len(keeps), len(widths)),
         grid=(tokens // tile,),
         in_specs=[row(features), row(features), pl.BlockSpec((1, features), lambda i: (0, 0))]
-        + [row(width)] * (2 * n_in),
-        out_specs=[row(out_width)] * n_out,
-        out_shape=[jax.ShapeDtypeStruct((tokens, out_width), BF)] * n_out,
+        + [row(keep.shape[1]) for keep in keeps] * 2,
+        out_specs=[row(w) for w in widths],
+        out_shape=[jax.ShapeDtypeStruct((tokens, w), BF) for w in widths],
         compiler_params=params(),
         cost_estimate=cost(20 * tokens * features, 12 * tokens * features),
         name="norm_cot",
@@ -164,44 +172,49 @@
     )(x_rows, *cots)
 
 
-def input_grad_kernel(scale, n_cot, n_weight, *refs):
+def input_grad_kernel(scale, rows, n_cot, place, own_ref, mate_ref, *refs):
     own, nb = refs[:n_cot], refs[n_cot : 2 * n_cot]
-    weights = refs[2 * n_cot : 2 * n_cot + n_weight]
-    keep_ref, give_ref = refs[2 * n_cot + n_weight :]
-    cot = jnp.concatenate(
-        [jnp.concatenate([ref[...] for ref in side], axis=1) for side in (own, nb)], axis=0
-    )
-    width = weights[0].shape[1]
-    total = 0.0
-    for i, ref in enumerate(weights):
-        total += lax.dot_general(
-            cot[:, i * width : (i + 1) * width],
-            ref[...],
-            (((1,), (1,)), ((), ())),
-            preferred_element_type=F32,
+    fars, (keep_ref, give_ref, w_ref) = refs[2 * n_cot : -3], refs[-3:]
+    put_rows(place, rows, (own_ref, mate_ref), w_ref, 0)
+    each = w_ref.shape[0] // rows - 2
+    start = 0
+    for i in range(0, len(fars), each):
+        for n, ref in enumerate(fars[i : i + each]):
+            at = pl.ds(pl.multiple_of(place[2 + n] * rows, 16), rows)
+            w_ref[at, start : start + ref.shape[1]] = ref[...]
+        start += fars[i].shape[1]
+    tokens = keep_ref.shape[0]
+    for cots, out_ref in ((nb, give_ref), (own, keep_ref)):
+        cot = jnp.concatenate([ref[...] for ref in cots], axis=1)
+        total = lax.dot_general(
+            cot, w_ref[...], (((1,), (1,)), ((), ())), preferred_element_type=F32
         )
-    total = (total * scale).astype(BF)
-    tokens = keep_ref.shape[0]
-    keep_ref[...] = total[:tokens]
-    give_ref[...] = total[tokens:]
-
-
-def input_grad_part(own, nb, weights, scale):
-    tokens = own[0].shape[0]
-    depth = weights[0].shape[0]
-    features = len(weights) * weights[0].shape[1]
-    count = 2 * len(own) + len(weights)
-    return pl.pallas_call(
-        functools.partial(input_grad_kernel, scale, len(own), len(weights)),
-        in_specs=[whole()] * count,
-        out_specs=[whole()] * 2,
+        out_ref[...] = (total * scale).astype(BF)
+
+
+def input_grad_part(place, own, mate, own_cots, nb_cots, fars, scale):
+    tokens = own_cots[0].shape[0]
+    rows, features = own.shape
+    depth = rows * (2 + len(fars[0]))
+    flat = [w for chunk in fars for w in chunk]
+    operands = [own, mate, *own_cots, *nb_cots, *flat]
+    full = lambda shape: pl.BlockSpec(shape, lambda i, place: (0, 0))
+    return pl.pallas_call(
+        functools.partial(input_grad_kernel, scale, rows, len(own_cots)),
+        grid_spec=pltpu.PrefetchScalarGridSpec(
+            num_scalar_prefetch=1,
+            grid=(1,),
+            in_specs=[full(a.shape) for a in operands],
+            out_specs=[full((tokens, depth))] * 2,
+            scratch_shapes=[pltpu.VMEM((depth, features), BF)],
+        ),
         out_shape=[jax.ShapeDtypeStruct((tokens, depth), BF)] * 2,
         compiler_params=params(),
         cost_estimate=cost(
             4 * tokens * depth * features, 2 * depth * features + 4 * tokens * (depth + features)
         ),
         name="input_grad_part",
-    )(*own, *nb, *weights)
+    )(place, *operands)
 
 
 def split_kernel(n_quad, near, mixed_ref, own_ref, give_ref):
@@ -272,9 +285,10 @@
     ours, theirs = refs[:count], refs[count : 2 * count]
     weight_ref, moment_ref = refs[2 * count :]
     mine = pl.program_id(0) == 0
-    width = ours[0].shape[1]
+    start = 0
     for i in range(count):
-        cols = slice(i * width, (i + 1) * width)
+        cols = slice(start, start + ours[i].shape[1])
+        start = cols.stop
         grads = jnp.where(mine, ours[i][...], theirs[i][...].astype(F32))
         moment = 0.5 * (
             MOMENTUM_DECAY * (m_ref[0, :, cols] + pm_ref[:, cols].astype(F32)) + grads
@@ -287,16 +301,15 @@
 def update(side, weight, partner_weight, momentum, partner_moment, ours, theirs):
     _, rows, features = weight.shape
     half = rows // 2
-    width = ours[0].shape[1]
     block3 = pl.BlockSpec((1, half, features), lambda i, side: (0, (side[0] + i) % 2, 0))
     block2 = pl.BlockSpec((half, features), lambda i, side: ((side[0] + i) % 2, 0))
-    fixed = pl.BlockSpec((half, width), lambda i, side: (0, 0))
+    fixed = [pl.BlockSpec(block.shape, lambda i, side: (0, 0)) for block in ours]
     return pl.pallas_call(
         functools.partial(update_kernel, len(ours)),
         grid_spec=pltpu.PrefetchScalarGridSpec(
             num_scalar_prefetch=1,
             grid=(2,),
-            in_specs=[block3, block2, block3, block2] + [fixed] * (2 * len(ours)),
+            in_specs=[block3, block2, block3, block2] + fixed * 2,
             out_specs=[block3, block3],
         ),
         out_shape=[
@@ -320,11 +333,15 @@
     side = (lax.axis_index("rep") >> PARTNER_BIT) & 1
     own = weight[0]
 
-    width = features // FWD_CHUNKS
-    cols = [slice(i * width, (i + 1) * width) for i in range(FWD_CHUNKS)]
-    x_own, x_give = split(near.reshape(1).astype(jnp.int32), mixed, n_quad)
+    cols = chunks(FWD_PARTS, features)
+    slices = [own[:, start : start + width] for start, width in cols]
+    fars = []
+    for i, piece in enumerate(slices):
+        if i >= IN_FLIGHT:
+            piece = after(piece, *fars[i - IN_FLIGHT])
+        fars.append([shift_far(piece, d) for d in range(1, n_quad)])
+    x_own, x_give = split(near.reshape(1).astype(jnp.int32), after(mixed, *slices), n_quad)
     x_nb = from_mate(x_give, 2)
-    fars = [[shift_far(own[:, c], d) for d in range(1, n_quad)] for c in cols]
     mate = from_mate(own, 1)
     partner_weight = from_partner(own)
     partner_moment = from_partner(momentum[0].astype(BF))
@@ -345,19 +362,21 @@
     x_rows = jnp.where(side == 0, x_rows, x_rows[:, ::-1])
     x_rows = jnp.swapaxes(x_rows, 0, 1).reshape(n_quad * rows, 4 * tokens)
 
-    weights, keeps, gots = [], [], []
-    for i in range(FWD_CHUNKS):
-        seen = [partner_weight] if i == 2 else [x_rows, partner_moment] if i == 3 else []
-        seen += gots[i - 2 : i - 1] if i > 1 else []
-        seen += keeps[-1:]
-        far_mates = [from_mate(after(w, *seen), 1) for w in fars[i]]
-        w_rows, keep, give = forward_part(place, x, own, mate, fars[i] + far_mates, i, width, scale)
-        weights.append(w_rows)
+    pieces, keeps, gots = [], [], []
+    for i, (start, width) in enumerate(cols):
+        seen = keeps[-1:]
+        if i == len(cols) - 1:
+            seen += gots[:-1] + [x_rows, partner_weight]
+        far_mates = [from_mate(after(w, *seen) if seen else w, 1) for w in fars[i]]
+        pieces.append(fars[i] + far_mates)
+        keep, give = forward_part(place, x, own, mate, pieces[i], start, width, scale)
         keeps.append(keep)
         gots.append(from_mate(give, 2))
 
     keeps[0] = after(keeps[0], partner_weight, partner_moment, x_rows)
-    cots = list(norm_cot(residual_in, upstream, norm_gain, keeps, gots, BWD_CHUNKS))
+    widths = [width for _, width in chunks(BWD_PARTS, features)]
+    count = len(widths)
+    cots = list(norm_cot(residual_in, upstream, norm_gain, keeps, gots, widths))
 
     half = rows // 2
     nbs = [from_mate(cot, 2) for cot in cots]
@@ -386,25 +405,26 @@
             ours[i] += block.astype(F32)
         theirs.append(from_partner(ours[i].astype(BF)))
 
-    nb_mates = []
-    for i in range(BWD_CHUNKS):
-        nb_mates.append(from_mate(nbs[i], 1))
-    for i in range(BWD_CHUNKS + 2):
-        if i < BWD_CHUNKS:
+    nb_mates = [from_mate(nb, 1) for nb in nbs]
+    for i in range(count + 2):
+        if i < count:
             seen = got[-1:] + (far_sums[-1] if far_sums else []) + theirs[-1:]
-            seen += nb_mates[i + 1 : i + 2] if i else []
+            if i == count - 1:
+                ig_own, ig_nb = input_grad_part(
+                    place, own, mate, [after(cots[0], kept[-1])] + cots[1:], nbs, pieces, scale
+                )
+                seen += [ig_nb]
             keep, give = gradient_part(
                 after(x_rows, *seen) if seen else x_rows, [cots[i], nbs[i], mates[i], nb_mates[i]], scale
             )
             kept.append(keep)
         if 0 <= i - 2:
             give_back(i - 2)
-        if 0 <= i - 1 < BWD_CHUNKS:
+        if 0 <= i - 1 < count:
             sum_far(i - 1)
-        if i < BWD_CHUNKS:
+        if i < count:
             got.append(from_partner(give))
 
-    ig_own, ig_nb = input_grad_part([after(cots[0], kept[-1])] + cots[1:], nbs, weights, scale)
     ig_got = from_mate(ig_nb, 2)
     input_grad = interleave(near.reshape(1).astype(jnp.int32), ig_own, ig_got, n_quad)
 

time: 227 us -> 209 us (0.921)
  starting transfers between devices: 31.6 us -> 23.8 us
  local copies, waits for them, and re-layouts: 18.7 us -> 13.8 us
  Pallas kernels: 36.5 us -> 33.1 us
    ppermute x8 -> x6, waiting for transfers between devices: 74.5 us -> 53 us  [shift_far(): lax.ppermute(block, 'fsdp', [(f, (f + 4 * hops) % count) for f in range(c...]
    ppermute x10 -> x8, waiting for transfers between devices: 6.5 us -> 16.8 us  [from_partner(): lax.ppermute(block, 'rep', [(g, g ^ 1 << PARTNER_BIT) for g in range(coun...]
    ppermute x24 -> x19, waiting for transfers between devices: 49.7 us -> 59.5 us  [from_mate(): return lax.ppermute(block, 'fsdp', [(f, f ^ bit) for f in range(count)])]
    ppermute x24 -> x19, starting transfers between devices: 13.8 us -> 4.1 us  [from_mate(): return lax.ppermute(block, 'fsdp', [(f, f ^ bit) for f in range(count)])]
    unnamed x37 -> x23, local copies, waits for them, and re-layouts: 10.7 us -> 4.99 us
    pallas_call x6 -> x5, Pallas kernels: 24.2 us -> 21.1 us  [the longest x3 10.5 us: forward_part(): pl.pallas_call(functools.partial(forward_kernel, scale, rows), grid_spec=...]
    ppermute x8 -> x6, starting transfers between devices: 7.54 us -> 9.95 us  [shift_far(): lax.ppermute(block, 'fsdp', [(f, (f + 4 * hops) % count) for f in range(c...]
    pallas_call x4 -> x3, Pallas kernels: 4.74 us -> 3.88 us  [gradient_part(): pl.pallas_call(functools.partial(gradient_kernel, scale), in_specs=[whole...]
  transfers between devices with their start and end apart: 42 -> 33, of which waited for: 22 -> 18; matrix products, arithmetic and copies ran while one was open for 7% -> 7% of each run, Pallas kernels for 12% -> 11%
where the time goes in v2:
time: 209 us
  waiting for transfers between devices  129 us (62%)
  Pallas kernels  33.1 us (16%)
  starting transfers between devices  23.8 us (11%)
  local copies, waits for them, and re-layouts  13.8 us (7%)
  other arithmetic  8.04 us (4%)
    ppermute x19, waiting for transfers between devices, from_mate(): return lax.ppermute(block, 'fsdp', [(f, f ^ bit) for f in range(count)])  59.5 us
    ppermute x6, waiting for transfers between devices, shift_far(): lax.ppermute(block, 'fsdp', [(f, (f + 4 * hops) % count) for f in range(c...  53 us
    ppermute x8, waiting for transfers between devices, from_partner(): lax.ppermute(block, 'rep', [(g, g ^ 1 << PARTNER_BIT) for g in range(coun...  16.8 us
    pallas_call x3, Pallas kernels, forward_part(): pl.pallas_call(functools.partial(forward_kernel, scale, rows), grid_spec=...  10.5 us
    ppermute x6, starting transfers between devices, shift_far(): lax.ppermute(block, 'fsdp', [(f, (f + 4 * hops) % count) for f in range(c...  9.95 us
    ppermute x8, starting transfers between devices, from_partner(): lax.ppermute(block, 'rep', [(g, g ^ 1 << PARTNER_BIT) for g in range(coun...  9.77 us
    pallas_call x1, Pallas kernels, input_grad_part(): pl.pallas_call(functools.partial(input_grad_kernel, scale, rows, len(own_...  7.01 us
    unnamed x23, local copies, waits for them, and re-layouts  4.99 us
  transfers between devices with their start and end apart: 33, of which 18 were waited for; matrix products, arithmetic and copies ran while one was open for 7% of the time, Pallas kernels for 11%

profile of v2, /device:TPU:0, one launch (start us, length us, event | category | flops | bytes accessed | tf_op | source)
XLA Modules:
  0.0 208.9 jit_solution(14846287081416447027)
XLA Ops:
  0.7 2.6 %fusion.4 = (bf16[320,1024]{1,0:T(8,128)(2,1)}, bf16[320,1024]{1,0:T(8,128)(2,1)}) fusion(bf16[320,2560]{1,0:T(8,128)(2,1)} %bitcast.15), kind=kLoop, calls=%fused_computation.24 | loop fusion | bytes 2621440 | tf_op jit(solution)/shard_map/slice | solution.py:337
  3.2 4.0 %collective-permute-start.2 = (bf16[320,1024]{1,0:T(8,128)(2,1)}, bf16[320,1024]{1,0:T(8,128)(2,1)}, u32[]{:S(2)}, u32[]{:S(2)}) collective-permute-start(bf16[320,1024]{1,0:T(8,128)(2,1)} %get-tuple-element.70), channel_id=1, source_target_pairs={{0,4},{1,5},{2,6},{3,7},{4,0},{5,1},{6,2},{7,3},{8,12},{9,13},{10,... | collective-permute-start | bytes 1966088 | tf_op jit(solution)/shard_map/ppermute | solution.py:54
  7.3 0.7 slice.41
  8.0 1.4 split.1
  9.5 0.8 copy-done.8
  10.3 1.6 collective-permute-start.1
  11.9 1.5 collective-permute-start.4
  13.4 1.1 constant_dynamic-update-slice_fusion.1
  14.5 21.9 %collective-permute-done.2.refs_2_.refs_6_ = bf16[320,1024]{1,0:T(8,128)(2,1)} collective-permute-done((bf16[320,1024]{1,0:T(8,128)(2,1)}, bf16[320,1024]{1,0:T(8,128)(2,1)}, u32[]{:S(2)}, u32[]{:S(2)}) %collective-permute-start.2) | collective-permute-done | bytes 655392 | tf_op jit(solution)/shard_map/ppermute | solution.py:54
  36.5 4.9 %collective-permute-done.1 = bf16[256,1280]{1,0:T(8,128)(2,1)} collective-permute-done((bf16[256,1280]{1,0:T(8,128)(2,1)}, bf16[256,1280]{1,0:T(8,128)(2,1)}, u32[]{:S(2)}, u32[]{:S(2)}) %collective-permute-start.1) | collective-permute-done | bytes 655392 | tf_op jit(solution)/shard_map/ppermute | solution.py:49
  41.4 1.1 constant_dynamic-update-slice_fusion.x_ref
  42.5 1.7 constant_dynamic-slice_fusion.3
  44.2 1.1 pad_maximum_fusion
  45.3 0.5 collective-permute-start.3
  45.8 1.3 convert_bitcast_fusion
  47.1 1.4 collective-permute-done.3.refs_3_.refs_7_
  48.5 0.9 copy-done.2
  49.4 1.8 collective-permute-start.5
  51.3 1.1 copy-done.3
  52.4 4.4 %forward_part.3 = (f32[256,1024]{1,0:T(8,128)S(1)}, bf16[256,1024]{1,0:T(8,128)(2,1)}) custom-call(s32[4]{0:T(128)S(1)} %pad_add_fusion.place, bf16[512,1280]{1,0:T(8,128)(2,1)S(1)} %constant_dynamic-update-slice_fusion.x_ref, bf16[320,2560]{1,0:T(8,128)(2,1)S(1)} %bitcast.20, bf16[320,2560]{1,0:T(8,128)(2,1)} %collective-permute-done.refs_1_.mate_ref, ...), custom_call_target="tpu_custom_call" | custom-call | flops 13421772 | bytes 65536 | tf_op jit(solution)/shard_map/forward_part/pallas_call | solution.py:82
  56.8 1.0 copy-done.6
  57.8 9.9 %collective-permute-done.7.refs_2_.refs_8_ = bf16[320,1024]{1,0:T(8,128)(2,1)} collective-permute-done((bf16[320,1024]{1,0:T(8,128)(2,1)}, bf16[320,1024]{1,0:T(8,128)(2,1)}, u32[]{:S(2)}, u32[]{:S(2)}) %collective-permute-start.7) | collective-permute-done | bytes 655392 | tf_op jit(solution)/shard_map/ppermute | solution.py:54
  67.7 1.7 collective-permute-start.9
  69.4 2.6 %maximum_bitcast_fusion = bf16[640,1024]{0,1:T(8,128)(2,1)} fusion(bf16[512,640]{1,0:T(8,128)(2,1)} %collective-permute-done.6, bf16[512,320]{1,0:T(8,128)(2,1)} %get-tuple-element.74, bf16[512,320]{1,0:T(8,128)(2,1)} %get-tuple-element.71), kind=kLoop, calls=%fused_computation.3 | loop fusion | flops 3932160 | bytes 2621440 | tf_op jit(solution)/shard_map/transpose | solution.py:361
  72.0 2.4 %copy.11 = bf16[640,1024]{1,0:T(8,128)(2,1)} copy(bf16[640,1024]{0,1:T(8,128)(2,1)} %maximum_bitcast_fusion) | data formatting | bytes 2621440 | tf_op jit(solution)/shard_map/transpose | solution.py:361
  74.4 2.3 %fusion = bf16[2,2,160,1024]{3,2,0,1:T(8,128)(2,1)S(1)} fusion(bf16[2,2,160,1024]{3,2,1,0:T(8,128)(2,1)} %bitcast.26, pred[]{:T(512)S(6)} %eq.9), kind=kLoop, calls=%fused_computation.2 | loop fusion | flops 655360 | bytes 2621441 | tf_op jit(solution)/shard_map/transpose | solution.py:363
  76.8 3.7 %forward_part.4 = (f32[256,1024]{1,0:T(8,128)S(1)}, bf16[256,1024]{1,0:T(8,128)(2,1)S(1)}) custom-call(s32[4]{0:T(128)S(1)} %pad_add_fusion.place, bf16[512,1280]{1,0:T(8,128)(2,1)S(1)} %constant_dynamic-update-slice_fusion.x_ref, bf16[320,2560]{1,0:T(8,128)(2,1)S(1)} %bitcast.21, bf16[320,2560]{1,0:T(8,128)(2,1)} %collective-permute-done.refs_1_.mate_ref, ...), custom_call_target="tpu_custom_call" | custom-call | flops 13421772 | bytes 65536 | tf_op jit(solution)/shard_map/forward_part/pallas_call | solution.py:82
  80.5 6.6 %collective-permute-done.9.refs_2_.refs_10_ = bf16[320,512]{1,0:T(8,128)(2,1)S(1)} collective-permute-done((bf16[320,512]{1,0:T(8,128)(2,1)}, bf16[320,512]{1,0:T(8,128)(2,1)S(1)}, u32[]{:S(2)}, u32[]{:S(2)}) %collective-permute-start.9) | collective-permute-done | bytes 327712 | tf_op jit(solution)/shard_map/ppermute | solution.py:54
  87.1 2.2 %collective-permute-done.10.refs_3_ = bf16[256,1024]{1,0:T(8,128)(2,1)} collective-permute-done((bf16[256,1024]{1,0:T(8,128)(2,1)}, bf16[256,1024]{1,0:T(8,128)(2,1)}, u32[]{:S(2)}, u32[]{:S(2)}) %collective-permute-start.10) | collective-permute-done | bytes 524320 | tf_op jit(solution)/shard_map/ppermute | solution.py:49
  89.4 1.5 collective-permute-done.11.refs_3_.refs_11_
  91.0 2.5 %forward_part.5 = (f32[256,512]{1,0:T(8,128)S(1)}, bf16[256,512]{1,0:T(8,128)(2,1)S(1)}) custom-call(s32[4]{0:T(128)S(1)} %pad_add_fusion.place, bf16[512,1280]{1,0:T(8,128)(2,1)S(1)} %constant_dynamic-update-slice_fusion.x_ref, bf16[320,2560]{1,0:T(8,128)(2,1)S(1)} %bitcast.22, bf16[320,2560]{1,0:T(8,128)(2,1)} %collective-permute-done.refs_1_.mate_ref, ...), custom_call_target="tpu_custom_call" | custom-call | flops 6710886 | bytes 39321 | tf_op jit(solution)/shard_map/forward_part/pallas_call | solution.py:82
  93.4 0.5 collective-permute-start.13
  94.0 10.1 %collective-permute-done.12.refs_4_ = bf16[256,1024]{1,0:T(8,128)(2,1)S(1)} collective-permute-done((bf16[256,1024]{1,0:T(8,128)(2,1)S(1)}, bf16[256,1024]{1,0:T(8,128)(2,1)S(1)}, u32[]{:S(2)}, u32[]{:S(2)}) %collective-permute-start.12) | collective-permute-done | bytes 524320 | tf_op jit(solution)/shard_map/ppermute | solution.py:49
  104.1 5.2 %collective-permute-done.13.refs_5_ = bf16[256,512]{1,0:T(8,128)(2,1)S(1)} collective-permute-done((bf16[256,512]{1,0:T(8,128)(2,1)S(1)}, bf16[256,512]{1,0:T(8,128)(2,1)S(1)}, u32[]{:S(2)}, u32[]{:S(2)}) %collective-permute-start.13) | collective-permute-done | bytes 262176 | tf_op jit(solution)/shard_map/ppermute | solution.py:49
  109.3 3.6 %norm_cot.1 = (bf16[256,1024]{1,0:T(8,128)(2,1)S(1)}, bf16[256,1024]{1,0:T(8,128)(2,1)S(1)}, bf16[256,512]{1,0:T(8,128)(2,1)S(1)}) custom-call(bf16[256,2560]{1,0:T(8,128)(2,1)} %res_ref.1, bf16[256,2560]{1,0:T(8,128)(2,1)} %up_ref.1, f32[1,2560]{1,0:T(1,128)S(1)} %reshape.24.gain_ref, f32[256,1024]{1,0:T(8,128)S(1)} %copy-done.7, ...), custom_call_target="tpu_custom_call" | custom-call | flops 131072 | bytes 78643 | tf_op jit(solution)/shard_map/norm_cot/pallas_call | solution.py:136
  112.9 0.3 collective-permute-start.14
  113.2 13.2 %collective-permute-done.14.refs_1_.refs_3_ = bf16[256,1024]{1,0:T(8,128)(2,1)S(1)} collective-permute-done((bf16[256,1024]{1,0:T(8,128)(2,1)S(1)}, bf16[256,1024]{1,0:T(8,128)(2,1)S(1)}, u32[]{:S(2)}, u32[]{:S(2)}) %collective-permute-start.14) | collective-permute-done | bytes 524320 | tf_op jit(solution)/shard_map/ppermute | solution.py:49
  126.4 0.5 collective-permute-start.18
  126.9 1.4 collective-permute-done.16.refs_3_
  128.3 1.5 gradient_part.3
  129.9 1.3 collective-permute-start.17
  131.2 9.6 %collective-permute-done.18.refs_1_.refs_4_ = bf16[256,1024]{1,0:T(8,128)(2,1)S(1)} collective-permute-done((bf16[256,1024]{1,0:T(8,128)(2,1)S(1)}, bf16[256,1024]{1,0:T(8,128)(2,1)S(1)}, u32[]{:S(2)}, u32[]{:S(2)}) %collective-permute-start.18) | collective-permute-done | bytes 524320 | tf_op jit(solution)/shard_map/ppermute | solution.py:49
  140.8 5.9 %collective-permute-done.17 = bf16[320,1024]{1,0:T(8,128)(2,1)S(1)} collective-permute-done((bf16[320,1024]{1,0:T(8,128)(2,1)S(1)}, bf16[320,1024]{1,0:T(8,128)(2,1)S(1)}, u32[]{:S(2)}, u32[]{:S(2)}) %collective-permute-start.17) | collective-permute-done | bytes 655392 | tf_op jit(solution)/shard_map/ppermute | solution.py:44
  146.7 1.5 gradient_part.4
  148.2 1.3 collective-permute-start.24
  149.6 0.5 collective-permute-start.21
  150.1 0.2 convert_add_fusion.1
  150.3 1.3 collective-permute-start.23
  151.6 9.9 %collective-permute-done.21.refs_5_.refs_1_ = bf16[256,512]{1,0:T(8,128)(2,1)S(1)} collective-permute-done((bf16[256,512]{1,0:T(8,128)(2,1)S(1)}, bf16[256,512]{1,0:T(8,128)(2,1)S(1)}, u32[]{:S(2)}, u32[]{:S(2)}) %collective-permute-start.21) | collective-permute-done | bytes 262176 | tf_op jit(solution)/shard_map/ppermute | solution.py:49
  161.6 7.0 %input_grad_part.1 = (bf16[256,1280]{1,0:T(8,128)(2,1)S(1)}, bf16[256,1280]{1,0:T(8,128)(2,1)S(1)}) custom-call(s32[4]{0:T(128)S(1)} %pad_add_fusion.place, bf16[320,2560]{1,0:T(8,128)(2,1)} %bitcast.16, bf16[320,2560]{1,0:T(8,128)(2,1)} %collective-permute-done.refs_1_.mate_ref, bf16[256,1024]{1,0:T(8,128)(2,1)S(1)} %get-tuple-element.52.refs_0_, ...), custom_call_target="tpu_custom_call" | custom-call | flops 33554432 | bytes 104857 | tf_op jit(solution)/shard_map/input_grad_part/pallas_call | solution.py:202
  168.7 0.8 gradient_part.5
  169.6 0.8 collective-permute-start.28
  170.4 0.2 convert_add_fusion
  170.6 1.5 collective-permute-start.25
  172.1 1.3 collective-permute-start.30
  173.5 6.7 %collective-permute-done.28 = bf16[320,512]{1,0:T(8,128)(2,1)S(1)} collective-permute-done((bf16[320,512]{1,0:T(8,128)(2,1)S(1)}, bf16[320,512]{1,0:T(8,128)(2,1)S(1)}, u32[]{:S(2)}, u32[]{:S(2)}) %collective-permute-start.28) | collective-permute-done | bytes 327712 | tf_op jit(solution)/shard_map/ppermute | solution.py:44
  180.2 1.5 collective-permute-start.29
  181.7 9.1 %collective-permute-done.25 = bf16[160,1024]{1,0:T(8,128)(2,1)S(1)} collective-permute-done((bf16[160,1024]{1,0:T(8,128)(2,1)S(1)}, bf16[160,1024]{1,0:T(8,128)(2,1)S(1)}, u32[]{:S(2)}, u32[]{:S(2)}) %collective-permute-start.25) | collective-permute-done | bytes 327712 | tf_op jit(solution)/shard_map/ppermute | solution.py:54
  191.0 0.8 collective-permute-start.31
  191.8 5.4 %collective-permute-done.29 = bf16[160,512]{1,0:T(8,128)(2,1)S(1)} collective-permute-done((bf16[160,512]{1,0:T(8,128)(2,1)S(1)}, bf16[160,512]{1,0:T(8,128)(2,1)S(1)}, u32[]{:S(2)}, u32[]{:S(2)}) %collective-permute-start.29) | collective-permute-done | bytes 163872 | tf_op jit(solution)/shard_map/ppermute | solution.py:54
  197.3 0.8 collective-permute-start.32
  198.1 1.6 interleave.1
  199.7 4.2 %collective-permute-done.32.refs_5_ = bf16[160,512]{1,0:T(8,128)(2,1)S(1)} collective-permute-done((bf16[160,512]{1,0:T(8,128)(2,1)S(1)}, bf16[160,512]{1,0:T(8,128)(2,1)S(1)}, u32[]{:S(2)}, u32[]{:S(2)}) %collective-permute-start.32) | collective-permute-done | bytes 163872 | tf_op jit(solution)/shard_map/ppermute | solution.py:44
  203.9 5.0 %update.1 = (bf16[1,320,2560]{2,1,0:T(8,128)(2,1)}, f32[1,320,2560]{2,1,0:T(8,128)}) custom-call(s32[1]{0:T(128)} %bitcast.11.place, bf16[1,320,2560]{2,1,0:T(8,128)(2,1)S(1)} %copy-done.1, bf16[320,2560]{1,0:T(8,128)(2,1)} %collective-permute-done.4.pw_ref, f32[1,320,2560]{2,1,0:T(8,128)} %m_ref.1, bf16[320,2560]{1,0:T(8,128)(2,1)} %collective-permute-done.5.pm_ref, ...), custom_call_target="tpu_custom_call" | custom-call | flops 81920 | bytes 147456 | tf_op jit(solution)/shard_map/update/pallas_call | solution.py:307
  (57 shorter events, 0.9 us)
Async XLA Ops:
  0.6 6.7 %copy-start = (bf16[1,320,2560]{2,1,0:T(8,128)(2,1)S(1)}, bf16[1,320,2560]{2,1,0:T(8,128)(2,1)}, u32[]{:S(2)}) copy-start(bf16[1,320,2560]{2,1,0:T(8,128)(2,1)} %w_ref.1) | copy-start | bytes 4915204
  0.6 7.4 %copy-start.5 = (bf16[256,2560]{1,0:T(8,128)(2,1)S(1)}, bf16[256,2560]{1,0:T(8,128)(2,1)}, u32[]{:S(2)}) copy-start(bf16[256,2560]{1,0:T(8,128)(2,1)} %mixed_ref) | copy-start | bytes 3932164
  3.2 33.2 %collective-permute-start.2 = (bf16[320,1024]{1,0:T(8,128)(2,1)}, bf16[320,1024]{1,0:T(8,128)(2,1)}, u32[]{:S(2)}, u32[]{:S(2)}) collective-permute-start(bf16[320,1024]{1,0:T(8,128)(2,1)} %get-tuple-element.70), channel_id=1, source_target_pairs={{0,4},{1,5},{2,6},{3,7},{4,0},{5,1},{6,2},{7,3},{8,12},{9,13},{10,... | collective-permute-start | bytes 1966088 | tf_op jit(solution)/shard_map/ppermute | solution.py:54
  9.5 0.8 copy-start.8
  10.3 31.1 %collective-permute-start.1 = (bf16[256,1280]{1,0:T(8,128)(2,1)}, bf16[256,1280]{1,0:T(8,128)(2,1)}, u32[]{:S(2)}, u32[]{:S(2)}) collective-permute-start(bf16[256,1280]{1,0:T(8,128)(2,1)} %get-tuple-element.35), channel_id=1, source_target_pairs={{0,2},{1,3},{2,0},{3,1},{4,6},{5,7},{6,4},{7,5},{8,10},{9,11},{10,... | collective-permute-start | bytes 1966088 | tf_op jit(solution)/shard_map/ppermute | solution.py:49
  11.9 39.4 %collective-permute-start = (bf16[320,2560]{1,0:T(8,128)(2,1)S(1)}, bf16[320,2560]{1,0:T(8,128)(2,1)}, u32[]{:S(2)}, u32[]{:S(2)}) collective-permute-start(bf16[320,2560]{1,0:T(8,128)(2,1)S(1)} %bitcast.18), channel_id=1, source_target_pairs={{0,1},{1,0},{2,3},{3,2},{4,5},{5,4},{6,7},{7,6},{8,9},{9,8},{10,11... | collective-permute-start | bytes 4915208 | tf_op jit(solution)/shard_map/ppermute | solution.py:49
  11.9 75.2 %collective-permute-start.4 = (bf16[320,2560]{1,0:T(8,128)(2,1)S(1)}, bf16[320,2560]{1,0:T(8,128)(2,1)}, u32[]{:S(2)}, u32[]{:S(2)}) collective-permute-start(bf16[320,2560]{1,0:T(8,128)(2,1)S(1)} %bitcast.19), channel_id=1, source_target_pairs={{0,16},{8,24},{16,0},{24,8},{1,17},{9,25},{17,1},{25,9},{2,18},{10... | collective-permute-start | bytes 4915208 | tf_op jit(solution)/shard_map/ppermute | solution.py:44
  36.5 31.2 %collective-permute-start.7 = (bf16[320,1024]{1,0:T(8,128)(2,1)}, bf16[320,1024]{1,0:T(8,128)(2,1)}, u32[]{:S(2)}, u32[]{:S(2)}) collective-permute-start(bf16[320,1024]{1,0:T(8,128)(2,1)} %get-tuple-element.38), channel_id=1, source_target_pairs={{0,4},{1,5},{2,6},{3,7},{4,0},{5,1},{6,2},{7,3},{8,12},{9,13},{10,... | collective-permute-start | bytes 1966088 | tf_op jit(solution)/shard_map/ppermute | solution.py:54
  42.5 3.2 %copy-start.9 = (f32[1,320,2560]{2,1,0:T(8,128)S(1)}, f32[1,320,2560]{2,1,0:T(8,128)}, u32[]{:S(2)}) copy-start(f32[1,320,2560]{2,1,0:T(8,128)} %m_ref.1) | copy-start | bytes 9830404
  45.3 22.4 %collective-permute-start.6 = (bf16[512,640]{1,0:T(8,128)(2,1)}, bf16[512,640]{1,0:T(8,128)(2,1)}, u32[]{:S(2)}, u32[]{:S(2)}) collective-permute-start(bf16[512,640]{1,0:T(8,128)(2,1)} %pad_maximum_fusion), channel_id=1, source_target_pairs={{0,1},{1,0},{2,3},{3,2},{4,5},{5,4},{6,7},{7,6},{8,9},{9,8},{10,11... | collective-permute-start | bytes 1966088 | tf_op jit(solution)/shard_map/ppermute | solution.py:49
  45.3 3.2 %collective-permute-start.3 = (bf16[320,1024]{1,0:T(8,128)(2,1)}, bf16[320,1024]{1,0:T(8,128)(2,1)S(1)}, u32[]{:S(2)}, u32[]{:S(2)}) collective-permute-start(bf16[320,1024]{1,0:T(8,128)(2,1)} %collective-permute-done.2.refs_2_.refs_6_), channel_id=1, source_target_pairs={{0,1},{1,0},{2,3},{3,2},{4,5},{5,4},{6,7},{7,6},{8,9},{9,8},{10,11... | collective-permute-start | bytes 1966088 | tf_op jit(solution)/shard_map/ppermute | solution.py:49
  48.5 0.9 copy-start.2
  49.4 44.5 %collective-permute-start.5 = (bf16[320,2560]{1,0:T(8,128)(2,1)}, bf16[320,2560]{1,0:T(8,128)(2,1)}, u32[]{:S(2)}, u32[]{:S(2)}) collective-permute-start(bf16[320,2560]{1,0:T(8,128)(2,1)} %convert_bitcast_fusion), channel_id=1, source_target_pairs={{0,16},{8,24},{16,0},{24,8},{1,17},{9,25},{17,1},{25,9},{2,18},{10... | collective-permute-start | bytes 4915208 | tf_op jit(solution)/shard_map/ppermute | solution.py:44
  51.3 1.1 copy-start.3
  56.8 1.0 copy-start.6
  67.6 9.1 %collective-permute-start.8 = (bf16[320,1024]{1,0:T(8,128)(2,1)}, bf16[320,1024]{1,0:T(8,128)(2,1)}, u32[]{:S(2)}, u32[]{:S(2)}) collective-permute-start(bf16[320,1024]{1,0:T(8,128)(2,1)} %collective-permute-done.7.refs_2_.refs_8_), channel_id=1, source_target_pairs={{0,1},{1,0},{2,3},{3,2},{4,5},{5,4},{6,7},{7,6},{8,9},{9,8},{10,11... | collective-permute-start | bytes 1966088 | tf_op jit(solution)/shard_map/ppermute | solution.py:49
  67.6 21.7 %collective-permute-start.10 = (bf16[256,1024]{1,0:T(8,128)(2,1)}, bf16[256,1024]{1,0:T(8,128)(2,1)}, u32[]{:S(2)}, u32[]{:S(2)}) collective-permute-start(bf16[256,1024]{1,0:T(8,128)(2,1)} %get-tuple-element.42), channel_id=1, source_target_pairs={{0,2},{1,3},{2,0},{3,1},{4,6},{5,7},{6,4},{7,5},{8,10},{9,11},{10,... | collective-permute-start | bytes 1572872 | tf_op jit(solution)/shard_map/ppermute | solution.py:49
  67.7 19.5 %collective-permute-start.9 = (bf16[320,512]{1,0:T(8,128)(2,1)}, bf16[320,512]{1,0:T(8,128)(2,1)S(1)}, u32[]{:S(2)}, u32[]{:S(2)}) collective-permute-start(bf16[320,512]{1,0:T(8,128)(2,1)} %slice.41), channel_id=1, source_target_pairs={{0,4},{1,5},{2,6},{3,7},{4,0},{5,1},{6,2},{7,3},{8,12},{9,13},{10,... | collective-permute-start | bytes 983048 | tf_op jit(solution)/shard_map/ppermute | solution.py:54
  89.3 1.6 collective-permute-start.11
  89.3 4.6 %copy-start.10 = (f32[2560]{0:T(1024)S(1)}, f32[2560]{0:T(1024)}, u32[]{:S(2)}) copy-start(f32[2560]{0:T(1024)} %param.9) | copy-start | bytes 30724
  89.3 20.0 %copy-start.7 = (f32[256,1024]{1,0:T(8,128)S(1)}, f32[256,1024]{1,0:T(8,128)}, u32[]{:S(2)}) copy-start(f32[256,1024]{1,0:T(8,128)} %copy-done.6) | copy-start | bytes 3145732
  89.3 14.8 %collective-permute-start.12 = (bf16[256,1024]{1,0:T(8,128)(2,1)S(1)}, bf16[256,1024]{1,0:T(8,128)(2,1)S(1)}, u32[]{:S(2)}, u32[]{:S(2)}) collective-permute-start(bf16[256,1024]{1,0:T(8,128)(2,1)S(1)} %get-tuple-element.45), channel_id=1, source_target_pairs={{0,2},{1,3},{2,0},{3,1},{4,6},{5,7},{6,4},{7,5},{8,10},{9,11},{10,... | collective-permute-start | bytes 1572872 | tf_op jit(solution)/shard_map/ppermute | solution.py:49
  93.4 15.9 %collective-permute-start.13 = (bf16[256,512]{1,0:T(8,128)(2,1)S(1)}, bf16[256,512]{1,0:T(8,128)(2,1)S(1)}, u32[]{:S(2)}, u32[]{:S(2)}) collective-permute-start(bf16[256,512]{1,0:T(8,128)(2,1)S(1)} %get-tuple-element.46), channel_id=1, source_target_pairs={{0,2},{1,3},{2,0},{3,1},{4,6},{5,7},{6,4},{7,5},{8,10},{9,11},{10,... | collective-permute-start | bytes 786440 | tf_op jit(solution)/shard_map/ppermute | solution.py:49
  112.9 13.6 %collective-permute-start.14 = (bf16[256,1024]{1,0:T(8,128)(2,1)S(1)}, bf16[256,1024]{1,0:T(8,128)(2,1)S(1)}, u32[]{:S(2)}, u32[]{:S(2)}) collective-permute-start(bf16[256,1024]{1,0:T(8,128)(2,1)S(1)} %get-tuple-element.52.refs_0_), channel_id=1, source_target_pairs={{0,2},{1,3},{2,0},{3,1},{4,6},{5,7},{6,4},{7,5},{8,10},{9,11},{10,... | collective-permute-start | bytes 1572872 | tf_op jit(solution)/shard_map/ppermute | solution.py:49
  113.2 13.7 %collective-permute-start.15 = (bf16[256,1024]{1,0:T(8,128)(2,1)S(1)}, bf16[256,1024]{1,0:T(8,128)(2,1)S(1)}, u32[]{:S(2)}, u32[]{:S(2)}) collective-permute-start(bf16[256,1024]{1,0:T(8,128)(2,1)S(1)} %get-tuple-element.52.refs_0_), channel_id=1, source_target_pairs={{0,1},{1,0},{2,3},{3,2},{4,5},{5,4},{6,7},{7,6},{8,9},{9,8},{10,11... | collective-permute-start | bytes 1572872 | tf_op jit(solution)/shard_map/ppermute | solution.py:49
  126.4 1.9 collective-permute-start.16
  126.4 14.3 %collective-permute-start.18 = (bf16[256,1024]{1,0:T(8,128)(2,1)S(1)}, bf16[256,1024]{1,0:T(8,128)(2,1)S(1)}, u32[]{:S(2)}, u32[]{:S(2)}) collective-permute-start(bf16[256,1024]{1,0:T(8,128)(2,1)S(1)} %get-tuple-element.50.refs_0_.refs_1_), channel_id=1, source_target_pairs={{0,2},{1,3},{2,0},{3,1},{4,6},{5,7},{6,4},{7,5},{8,10},{9,11},{10,... | collective-permute-start | bytes 1572872 | tf_op jit(solution)/shard_map/ppermute | solution.py:49
  129.9 16.8 %collective-permute-start.17 = (bf16[320,1024]{1,0:T(8,128)(2,1)S(1)}, bf16[320,1024]{1,0:T(8,128)(2,1)S(1)}, u32[]{:S(2)}, u32[]{:S(2)}) collective-permute-start(bf16[320,1024]{1,0:T(8,128)(2,1)S(1)} %get-tuple-element.48), channel_id=1, source_target_pairs={{0,16},{8,24},{16,0},{24,8},{1,17},{9,25},{17,1},{25,9},{2,18},{10... | collective-permute-start | bytes 1966088 | tf_op jit(solution)/shard_map/ppermute | solution.py:44
  131.2 15.5 %collective-permute-start.19 = (bf16[256,1024]{1,0:T(8,128)(2,1)S(1)}, bf16[256,1024]{1,0:T(8,128)(2,1)S(1)}, u32[]{:S(2)}, u32[]{:S(2)}) collective-permute-start(bf16[256,1024]{1,0:T(8,128)(2,1)S(1)} %get-tuple-element.50.refs_0_.refs_1_), channel_id=1, source_target_pairs={{0,1},{1,0},{2,3},{3,2},{4,5},{5,4},{6,7},{7,6},{8,9},{9,8},{10,11... | collective-permute-start | bytes 1572872 | tf_op jit(solution)/shard_map/ppermute | solution.py:49
  140.8 5.9 %collective-permute-start.20 = (bf16[256,1024]{1,0:T(8,128)(2,1)S(1)}, bf16[256,1024]{1,0:T(8,128)(2,1)S(1)}, u32[]{:S(2)}, u32[]{:S(2)}) collective-permute-start(bf16[256,1024]{1,0:T(8,128)(2,1)S(1)} %collective-permute-done.18.refs_1_.refs_4_), channel_id=1, source_target_pairs={{0,1},{1,0},{2,3},{3,2},{4,5},{5,4},{6,7},{7,6},{8,9},{9,8},{10,11... | collective-permute-start | bytes 1572872 | tf_op jit(solution)/shard_map/ppermute | solution.py:49
  148.2 20.4 %collective-permute-start.24 = (bf16[320,1024]{1,0:T(8,128)(2,1)S(1)}, bf16[320,1024]{1,0:T(8,128)(2,1)S(1)}, u32[]{:S(2)}, u32[]{:S(2)}) collective-permute-start(bf16[320,1024]{1,0:T(8,128)(2,1)S(1)} %get-tuple-element.57), channel_id=1, source_target_pairs={{0,16},{8,24},{16,0},{24,8},{1,17},{9,25},{17,1},{25,9},{2,18},{10... | collective-permute-start | bytes 1966088 | tf_op jit(solution)/shard_map/ppermute | solution.py:44
  149.6 12.0 %collective-permute-start.21 = (bf16[256,512]{1,0:T(8,128)(2,1)S(1)}, bf16[256,512]{1,0:T(8,128)(2,1)S(1)}, u32[]{:S(2)}, u32[]{:S(2)}) collective-permute-start(bf16[256,512]{1,0:T(8,128)(2,1)S(1)} %get-tuple-element.53.refs_2_.refs_0_), channel_id=1, source_target_pairs={{0,2},{1,3},{2,0},{3,1},{4,6},{5,7},{6,4},{7,5},{8,10},{9,11},{10,... | collective-permute-start | bytes 786440 | tf_op jit(solution)/shard_map/ppermute | solution.py:49
  150.1 11.5 %copy-start.4 = (bf16[320,1024]{1,0:T(8,128)(2,1)S(1)}, bf16[320,1024]{1,0:T(8,128)(2,1)}, u32[]{:S(2)}) copy-start(bf16[320,1024]{1,0:T(8,128)(2,1)} %copy-done.2) | copy-start | bytes 1966084
  150.3 18.3 %collective-permute-start.23 = (bf16[160,1024]{1,0:T(8,128)(2,1)S(1)}, bf16[160,1024]{1,0:T(8,128)(2,1)S(1)}, u32[]{:S(2)}, u32[]{:S(2)}) collective-permute-start(bf16[160,1024]{1,0:T(8,128)(2,1)S(1)} %slice.55), channel_id=1, source_target_pairs={{0,4},{1,5},{2,6},{3,7},{4,0},{5,1},{6,2},{7,3},{8,12},{9,13},{10,... | collective-permute-start | bytes 983048 | tf_op jit(solution)/shard_map/ppermute | solution.py:54
  151.6 17.1 %collective-permute-start.26 = (bf16[256,512]{1,0:T(8,128)(2,1)S(1)}, bf16[256,512]{1,0:T(8,128)(2,1)S(1)}, u32[]{:S(2)}, u32[]{:S(2)}) collective-permute-start(bf16[256,512]{1,0:T(8,128)(2,1)S(1)} %get-tuple-element.53.refs_2_.refs_0_), channel_id=1, source_target_pairs={{0,1},{1,0},{2,3},{3,2},{4,5},{5,4},{6,7},{7,6},{8,9},{9,8},{10,11... | collective-permute-start | bytes 786440 | tf_op jit(solution)/shard_map/ppermute | solution.py:49
  161.6 7.1 %collective-permute-start.27 = (bf16[256,512]{1,0:T(8,128)(2,1)S(1)}, bf16[256,512]{1,0:T(8,128)(2,1)S(1)}, u32[]{:S(2)}, u32[]{:S(2)}) collective-permute-start(bf16[256,512]{1,0:T(8,128)(2,1)S(1)} %collective-permute-done.21.refs_5_.refs_1_), channel_id=1, source_target_pairs={{0,1},{1,0},{2,3},{3,2},{4,5},{5,4},{6,7},{7,6},{8,9},{9,8},{10,11... | collective-permute-start | bytes 786440 | tf_op jit(solution)/shard_map/ppermute | solution.py:49
  168.6 29.5 %collective-permute-start.22 = (bf16[256,1280]{1,0:T(8,128)(2,1)S(1)}, bf16[256,1280]{1,0:T(8,128)(2,1)S(1)}, u32[]{:S(2)}, u32[]{:S(2)}) collective-permute-start(bf16[256,1280]{1,0:T(8,128)(2,1)S(1)} %get-tuple-element.55), channel_id=1, source_target_pairs={{0,2},{1,3},{2,0},{3,1},{4,6},{5,7},{6,4},{7,5},{8,10},{9,11},{10,... | collective-permute-start | bytes 1966088 | tf_op jit(solution)/shard_map/ppermute | solution.py:49
  169.6 10.6 %collective-permute-start.28 = (bf16[320,512]{1,0:T(8,128)(2,1)S(1)}, bf16[320,512]{1,0:T(8,128)(2,1)S(1)}, u32[]{:S(2)}, u32[]{:S(2)}) collective-permute-start(bf16[320,512]{1,0:T(8,128)(2,1)S(1)} %get-tuple-element.60), channel_id=1, source_target_pairs={{0,16},{8,24},{16,0},{24,8},{1,17},{9,25},{17,1},{25,9},{2,18},{10... | collective-permute-start | bytes 983048 | tf_op jit(solution)/shard_map/ppermute | solution.py:44
  170.6 20.3 %collective-permute-start.25 = (bf16[160,1024]{1,0:T(8,128)(2,1)S(1)}, bf16[160,1024]{1,0:T(8,128)(2,1)S(1)}, u32[]{:S(2)}, u32[]{:S(2)}) collective-permute-start(bf16[160,1024]{1,0:T(8,128)(2,1)S(1)} %slice.54), channel_id=1, source_target_pairs={{0,4},{1,5},{2,6},{3,7},{4,0},{5,1},{6,2},{7,3},{8,12},{9,13},{10,... | collective-permute-start | bytes 983048 | tf_op jit(solution)/shard_map/ppermute | solution.py:54
  172.1 27.6 %collective-permute-start.30 = (bf16[160,1024]{1,0:T(8,128)(2,1)S(1)}, bf16[160,1024]{1,0:T(8,128)(2,1)S(1)}, u32[]{:S(2)}, u32[]{:S(2)}) collective-permute-start(bf16[160,1024]{1,0:T(8,128)(2,1)S(1)} %get-tuple-element.67), channel_id=1, source_target_pairs={{0,16},{8,24},{16,0},{24,8},{1,17},{9,25},{17,1},{25,9},{2,18},{10... | collective-permute-start | bytes 983048 | tf_op jit(solution)/shard_map/ppermute | solution.py:44
  180.2 17.0 %collective-permute-start.29 = (bf16[160,512]{1,0:T(8,128)(2,1)S(1)}, bf16[160,512]{1,0:T(8,128)(2,1)S(1)}, u32[]{:S(2)}, u32[]{:S(2)}) collective-permute-start(bf16[160,512]{1,0:T(8,128)(2,1)S(1)} %slice.56), channel_id=1, source_target_pairs={{0,4},{1,5},{2,6},{3,7},{4,0},{5,1},{6,2},{7,3},{8,12},{9,13},{10,... | collective-permute-start | bytes 491528 | tf_op jit(solution)/shard_map/ppermute | solution.py:54
  191.0 12.9 %collective-permute-start.31 = (bf16[160,1024]{1,0:T(8,128)(2,1)S(1)}, bf16[160,1024]{1,0:T(8,128)(2,1)S(1)}, u32[]{:S(2)}, u32[]{:S(2)}) collective-permute-start(bf16[160,1024]{1,0:T(8,128)(2,1)S(1)} %get-tuple-element.65), channel_id=1, source_target_pairs={{0,16},{8,24},{16,0},{24,8},{1,17},{9,25},{17,1},{25,9},{2,18},{10... | collective-permute-start | bytes 983048 | tf_op jit(solution)/shard_map/ppermute | solution.py:44
  197.3 6.6 %collective-permute-start.32 = (bf16[160,512]{1,0:T(8,128)(2,1)S(1)}, bf16[160,512]{1,0:T(8,128)(2,1)S(1)}, u32[]{:S(2)}, u32[]{:S(2)}) collective-permute-start(bf16[160,512]{1,0:T(8,128)(2,1)S(1)} %get-tuple-element.63), channel_id=1, source_target_pairs={{0,16},{8,24},{16,0},{24,8},{1,17},{9,25},{17,1},{25,9},{2,18},{10... | collective-permute-start | bytes 491528 | tf_op jit(solution)/shard_map/ppermute | solution.py:44
  198.1 5.8 %copy-start.1 = (bf16[1,320,2560]{2,1,0:T(8,128)(2,1)S(1)}, bf16[1,320,2560]{2,1,0:T(8,128)(2,1)}, u32[]{:S(2)}) copy-start(bf16[1,320,2560]{2,1,0:T(8,128)(2,1)} %w_ref.1) | copy-start | bytes 4915204

commit v3 on v2

v3 whole, which is shorter than its diff:
```python
import functools
import math

import jax
import jax.numpy as jnp
from jax import lax
from jax.experimental import pallas as pl
from jax.experimental.pallas import tpu as pltpu
from jax.sharding import PartitionSpec as P

PARTNER_BIT = 1

EPSILON = 1e-05
LEARN_RATE = 0.05
MOMENTUM_DECAY = 0.9

FWD_PARTS = (8, 8, 4)
BWD_PARTS = (8, 8, 4)
SWAP_PARTS = 2
GIVE_PARTS = 1
COST_SHARE = 0.01
VMEM_MIB = 48
BF = jnp.bfloat16
F32 = jnp.float32


def params(mib=VMEM_MIB):
    return pltpu.CompilerParams(vmem_limit_bytes=mib << 20)


def cost(flops, moved):
    return pl.CostEstimate(
        flops=int(flops * COST_SHARE), bytes_accessed=int(moved * COST_SHARE), transcendentals=0
    )


def whole(*shape):
    return pl.BlockSpec(shape, lambda *_: (0,) * len(shape))


def after(block, *others):
    return lax.optimization_barrier((block, *others))[0]


def from_partner(block):
    count = lax.axis_size("rep")
    return lax.ppermute(block, "rep", [(g, g ^ (1 << PARTNER_BIT)) for g in range(count)])


def from_mate(block, bit):
    count = lax.axis_size("fsdp")
    return lax.ppermute(block, "fsdp", [(f, f ^ bit) for f in range(count)])


def shift_far(block, hops):
    count = lax.axis_size("fsdp")
    return lax.ppermute(block, "fsdp", [(f, (f + 4 * hops) % count) for f in range(count)])


def chunks(parts, features):
    unit = features // sum(parts)
    return [(sum(parts[:i]) * unit, part * unit) for i, part in enumerate(parts)]


def put_rows(place, rows, refs, w_ref, start):
    block = done = 0
    for ref in refs:
        count = ref.shape[0]
        at = pl.ds(pl.multiple_of(place[block] * rows + done, 8), count)
        w_ref[at, start : start + ref.shape[1]] = ref[...]
        done += count
        if done == rows:
            block, done = block + 1, 0


def forward_kernel(scale, rows, parts, place, x_ref, nb_ref, *refs):
    pieces, w_ref = refs[: -2 * parts - 1], refs[-1]
    keeps, gives = refs[-2 * parts - 1 : -parts - 1], refs[-parts - 1 : -1]
    put_rows(place, rows, pieces, w_ref, 0)
    x = jnp.concatenate([x_ref[...], nb_ref[...]], axis=0)
    part = jnp.dot(x, w_ref[...], preferred_element_type=F32) * scale
    tokens, width = keeps[0].shape
    for i in range(parts):
        cols = slice(i * width, (i + 1) * width)
        keeps[i][...] = part[:tokens, cols]
        gives[i][...] = part[tokens:, cols].astype(BF)


def forward_part(place, x_own, x_nb, weights, scale, parts):
    tokens, depth = x_own.shape
    rows, width = weights[0].shape
    operands = (x_own, x_nb, *weights)
    out = pl.pallas_call(
        functools.partial(forward_kernel, scale, rows, parts),
        grid_spec=pltpu.PrefetchScalarGridSpec(
            num_scalar_prefetch=1,
            grid=(1,),
            in_specs=[whole(*a.shape) for a in operands],
            out_specs=[whole(tokens, width // parts)] * (2 * parts),
            scratch_shapes=[pltpu.VMEM((depth, width), BF)],
        ),
        out_shape=[
            jax.ShapeDtypeStruct((tokens, width // parts), kind)
            for kind in (F32, BF)
            for _ in range(parts)
        ],
        compiler_params=params(),
        cost_estimate=cost(4 * tokens * depth * width, 2 * depth * (2 * width + 2 * tokens)),
        name="forward_part",
    )(place, *operands)
    return out[:parts], out[parts:]


def norm_kernel(n_in, n_out, res_ref, up_ref, gain_ref, *refs):
    keeps, gots, cots = refs[:n_in], refs[n_in : 2 * n_in], refs[2 * n_in :]
    features = res_ref.shape[1]
    summed, scaled = [], []
    square = inner = 0.0
    start = 0
    for keep, got in zip(keeps, gots):
        cols = slice(start, start + keep.shape[1])
        start = cols.stop
        s = res_ref[:, cols].astype(F32) + (keep[...] + got[...].astype(F32))
        c = up_ref[:, cols].astype(F32) * gain_ref[:, cols]
        square += jnp.sum(s * s, axis=-1, keepdims=True)
        inner += jnp.sum(c * s, axis=-1, keepdims=True)
        summed.append(s)
        scaled.append(c)
    inv_rms = lax.rsqrt(square / features + EPSILON)
    pull = inner / features * inv_rms * inv_rms
    start = 0
    for s, c in zip(summed, scaled):
        cot = (inv_rms * (c - s * pull)).astype(BF)
        end = start + s.shape[1]
        first = 0
        for ref in cots:
            last = first + ref.shape[1]
            low, high = max(first, start), min(last, end)
            if low < high:
                ref[:, low - first : high - first] = cot[:, low - start : high - start]
            first = last
        start = end


def norm_cot(residual, upstream, gain, keeps, gots, widths):
    tokens, features = residual.shape
    tile = 64
    row = lambda w: pl.BlockSpec((tile, w), lambda i: (i, 0))
    return pl.pallas_call(
        functools.partial(norm_kernel, len(keeps), len(widths)),
        grid=(tokens // tile,),
        in_specs=[row(features), row(features), pl.BlockSpec((1, features), lambda i: (0, 0))]
        + [row(keep.shape[1]) for keep in keeps] * 2,
        out_specs=[row(w) for w in widths],
        out_shape=[jax.ShapeDtypeStruct((tokens, w), BF) for w in widths],
        compiler_params=params(),
        cost_estimate=cost(20 * tokens * features, 12 * tokens * features),
        name="norm_cot",
    )(residual, upstream, gain.reshape(1, features), *keeps, *gots)


def turn_kernel(rows, place, x_ref, nb_ref, mine_ref, theirs_ref, turned_ref):
    tokens = x_ref.shape[0]
    turned_ref[:, :tokens] = x_ref[...].astype(F32).T
    turned_ref[:, tokens:] = nb_ref[...].astype(F32).T
    half = rows // 2
    n_quad = mine_ref.shape[0] // rows
    for to in range(2):
        for d in range(n_quad):
            low = (to * n_quad + d) * half
            for ref, core in ((mine_ref, 0), (theirs_ref, 1)):
                at = place[2 * d + core] * rows + (place[2 * n_quad] ^ to) * half
                block = turned_ref[pl.ds(pl.multiple_of(at, 8), half), :]
                ref[low : low + half, :] = block.astype(BF)


def turn(place, x_own, x_nb, rows):
    tokens, depth = x_own.shape
    full = lambda shape: pl.BlockSpec(shape, lambda i, place: (0, 0))
    return pl.pallas_call(
        functools.partial(turn_kernel, rows),
        grid_spec=pltpu.PrefetchScalarGridSpec(
            num_scalar_prefetch=1,
            grid=(1,),
            in_specs=[full(x_own.shape)] * 2,
            out_specs=[full((depth // 2, 2 * tokens))] * 2,
            scratch_shapes=[pltpu.VMEM((depth, 2 * tokens), F32)],
        ),
        out_shape=[jax.ShapeDtypeStruct((depth // 2, 2 * tokens), BF)] * 2,
        compiler_params=params(),
        cost_estimate=cost(0, 8 * depth * tokens),
        name="turn",
    )(place, x_own, x_nb)


def gradient_kernel(scale, x_ref, *refs):
    cots, (keep_ref, give_ref) = refs[:4], refs[4:]
    cot = jnp.concatenate([ref[...] for ref in cots], axis=0)
    part = jnp.dot(x_ref[...], cot, preferred_element_type=F32) * scale
    half = keep_ref.shape[0]
    keep_ref[...] = part[:half]
    give_ref[...] = part[half:].astype(BF)


def gradient_part(x_rows, cots, scale):
    rows, tokens = x_rows.shape
    width = cots[0].shape[1]
    return pl.pallas_call(
        functools.partial(gradient_kernel, scale),
        grid=(1,),
        in_specs=[whole(*a.shape) for a in (x_rows, *cots)],
        out_specs=[whole(rows // 2, width)] * 2,
        out_shape=[
            jax.ShapeDtypeStruct((rows // 2, width), F32),
            jax.ShapeDtypeStruct((rows // 2, width), BF),
        ],
        compiler_params=params(),
        cost_estimate=cost(2 * rows * tokens * width, 2 * tokens * (rows + width) + 3 * rows * width),
        name="gradient_part",
    )(x_rows, *cots)


def input_grad_kernel(scale, rows, n_cot, counts, place, *refs):
    cots, weights, (out_ref, w_ref) = refs[:n_cot], refs[n_cot:-2], refs[-2:]
    start = first = 0
    for count in counts:
        part = weights[first : first + count]
        put_rows(place, rows, part, w_ref, start)
        first += count
        start += part[0].shape[1]
    cot = jnp.concatenate([ref[...] for ref in cots], axis=1)
    total = lax.dot_general(cot, w_ref[...], (((1,), (1,)), ((), ())), preferred_element_type=F32)
    out_ref[...] = (total * scale).astype(BF)


def input_grad_part(place, cots, weights, scale):
    tokens = cots[0].shape[0]
    features = sum(cot.shape[1] for cot in cots)
    rows = weights[0][0].shape[0]
    depth = sum(w.shape[0] for w in weights[0])
    operands = [*cots] + [w for chunk in weights for w in chunk]
    return pl.pallas_call(
        functools.partial(input_grad_kernel, scale, rows, len(cots), [len(w) for w in weights]),
        grid_spec=pltpu.PrefetchScalarGridSpec(
            num_scalar_prefetch=1,
            grid=(1,),
            in_specs=[whole(*a.shape) for a in operands],
            out_specs=whole(tokens, depth),
            scratch_shapes=[pltpu.VMEM((depth, features), BF)],
        ),
        out_shape=jax.ShapeDtypeStruct((tokens, depth), BF),
        compiler_params=params(),
        cost_estimate=cost(
            2 * tokens * depth * features, 2 * depth * features + 2 * tokens * (depth + features)
        ),
        name="input_grad_part",
    )(place, *operands)


def split_kernel(n_quad, near, mixed_ref, own_ref, give_ref):
    width = own_ref.shape[1] // n_quad
    for side in range(2):

        @pl.when(near[0] == side)
        def _():
            for i in range(n_quad):
                to = slice(i * width, (i + 1) * width)
                ours, theirs = 2 * i + side, 2 * i + 1 - side
                own_ref[:, to] = mixed_ref[:, ours * width : (ours + 1) * width]
                give_ref[:, to] = mixed_ref[:, theirs * width : (theirs + 1) * width]


def split(near, mixed, n_quad):
    tokens, features = mixed.shape
    tile = 64
    row = lambda w: pl.BlockSpec((tile, w), lambda i, near: (i, 0))
    return pl.pallas_call(
        functools.partial(split_kernel, n_quad),
        grid_spec=pltpu.PrefetchScalarGridSpec(
            num_scalar_prefetch=1,
            grid=(tokens // tile,),
            in_specs=[row(features)],
            out_specs=[row(features // 2)] * 2,
        ),
        out_shape=[jax.ShapeDtypeStruct((tokens, features // 2), BF)] * 2,
        compiler_params=params(),
        cost_estimate=cost(0, 4 * tokens * features),
        name="split",
    )(near, mixed)


def interleave_kernel(n_quad, near, own_ref, got_ref, out_ref):
    width = own_ref.shape[1] // n_quad
    for side in range(2):

        @pl.when(near[0] == side)
        def _():
            for i in range(n_quad):
                at = slice(i * width, (i + 1) * width)
                ours, theirs = 2 * i + side, 2 * i + 1 - side
                out_ref[:, ours * width : (ours + 1) * width] = own_ref[:, at]
                out_ref[:, theirs * width : (theirs + 1) * width] = got_ref[:, at]


def interleave(near, own, got, n_quad):
    tokens, depth = own.shape
    tile = 64
    row = lambda w: pl.BlockSpec((tile, w), lambda i, near: (i, 0))
    return pl.pallas_call(
        functools.partial(interleave_kernel, n_quad),
        grid_spec=pltpu.PrefetchScalarGridSpec(
            num_scalar_prefetch=1,
            grid=(tokens // tile,),
            in_specs=[row(depth)] * 2,
            out_specs=row(2 * depth),
        ),
        out_shape=jax.ShapeDtypeStruct((tokens, 2 * depth), BF),
        compiler_params=params(),
        cost_estimate=cost(0, 8 * tokens * depth),
        name="interleave",
    )(near, own, got)


def update_kernel(w_ref, pw_ref, m_ref, pm_ref, ours_ref, theirs_ref, *refs):
    weight_ref, moment_ref = refs[-2:]
    mine = pl.program_id(0) == 0
    grads = jnp.where(mine, ours_ref[...], theirs_ref[...].astype(F32))
    moment = 0.5 * (MOMENTUM_DECAY * (m_ref[0] + pm_ref[...].astype(F32)) + grads)
    moment_ref[0] = moment
    both = w_ref[0].astype(F32) + pw_ref[...].astype(F32)
    weight_ref[0] = (0.5 * both - LEARN_RATE * moment).astype(BF)


def update(side, weight, partner_weight, momentum, partner_moment, ours, theirs, start, made):
    _, rows, _ = weight.shape
    half, width = ours.shape
    unit = math.gcd(start, width)
    at = start // unit
    block3 = pl.BlockSpec((1, half, unit), lambda i, j, side: (0, (side[0] + i) % 2, at + j))
    block2 = pl.BlockSpec((half, unit), lambda i, j, side: ((side[0] + i) % 2, at + j))
    fixed = pl.BlockSpec((half, unit), lambda i, j, side: (0, j))

    def kernel(side, *refs):
        update_kernel(*refs)

    return pl.pallas_call(
        kernel,
        grid_spec=pltpu.PrefetchScalarGridSpec(
            num_scalar_prefetch=1,
            grid=(2, width // unit),
            in_specs=[block3, block2, block3, block2, fixed, fixed]
            + [pl.BlockSpec(memory_space=pl.ANY)] * len(made),
            out_specs=[block3, block3],
        ),
        out_shape=[
            jax.ShapeDtypeStruct(weight.shape, BF),
            jax.ShapeDtypeStruct(momentum.shape, F32),
        ],
        input_output_aliases={7 + i: i for i in range(len(made))},
        compiler_params=params(),
        cost_estimate=cost(10 * rows * width, 18 * rows * width),
        name="update",
    )(side, weight, partner_weight, momentum, partner_moment, ours, theirs, *made)


def per_device(residual_in, mixed, upstream, norm_gain, weight, momentum):
    tokens, features = mixed.shape
    scale = features ** (-0.5)
    count = lax.axis_size("fsdp")
    n_quad = count // 4
    rows = weight.shape[1]
    me = lax.axis_index("fsdp")
    quad, core, near = me // 4, me % 2, (me // 2) % 2
    side = (lax.axis_index("rep") >> PARTNER_BIT) & 1
    own = weight[0]

    cols = chunks(FWD_PARTS, features)
    slices = [own[:, start : start + width] for start, width in cols]
    x_own, x_give = split(near.reshape(1).astype(jnp.int32), after(mixed, *slices), n_quad)
    x_nb = from_mate(x_give, 2)
    small_moment = momentum[0].astype(BF)
    mates = [from_mate(piece, 1) for piece in slices]
    partner_weight = from_partner(own)
    partner_moment = from_partner(small_moment)

    quads = [quad] + [(quad + n_quad - d) % n_quad for d in range(1, n_quad)]
    place = jnp.stack(
        [quads[0] * 2 + core, quads[0] * 2 + 1 - core]
        + [q * 2 + core for q in quads[1:]]
        + [q * 2 + 1 - core for q in quads[1:]]
    ).astype(jnp.int32)

    on = [(quad + d) % n_quad for d in range(n_quad)]
    order = jnp.stack([2 * q + c for q in on for c in (core, 1 - core)] + [side]).astype(jnp.int32)

    def send_far(i, *others):
        piece = after(slices[i], *fars[-1], *others) if i else slices[i]
        fars.append([shift_far(piece, d) for d in range(1, n_quad)])

    def swap_rows(block, parts):
        parts = parts if rows % (16 * parts) == 0 else 1
        return [from_mate(part, 1) for part in jnp.split(block, parts, axis=0)]

    fars, pieces, keeps, gots = [], [], [], []
    send_far(0)
    send_far(1)
    last = len(cols) - 1
    for i in range(len(cols)):
        seen = keeps[-1:]
        if i == last:
            x_mine, x_theirs = turn(order, after(x_own, keeps[-1]), x_nb, rows)
            x_rows = jnp.concatenate([x_mine, from_mate(x_theirs, 1)], axis=1)
        if i == last:
            seen += gots[:1] + [partner_weight]
        parts = SWAP_PARTS if i == last else 1
        far_mates = [p for w in fars[i] for p in swap_rows(after(w, *seen) if seen else w, parts)]
        pieces.append([slices[i], mates[i]] + fars[i] + far_mates)
        kept, given = forward_part(place, x_own, x_nb, pieces[i], scale, GIVE_PARTS)
        keeps += kept
        gots += [from_mate(give, 2) for give in given]
        if i + 2 <= last:
            send_far(i + 2)

    keeps[0] = after(keeps[0], partner_moment, x_rows)
    widths = [width for _, width in chunks(BWD_PARTS, features)]
    count = len(widths)
    cots = list(norm_cot(residual_in, upstream, norm_gain, keeps, gots, widths))

    half = rows // 2
    nbs = [from_mate(cot, 2) for cot in cots]
    mates = [from_mate(cot, 1) for cot in cots]
    kept, got, ours, theirs = [], [], [], []

    def gather(i):
        both = kept[i] + got[i].astype(F32)
        total = both[:half]
        for d in range(1, n_quad):
            total += shift_far(both[d * half : (d + 1) * half].astype(BF), d).astype(F32)
        ours.append(total)
        theirs.append(from_partner(total.astype(BF)))

    far_sums = []

    def sum_far(i):
        both = kept[i] + got[i].astype(F32)
        far_sums.append(
            [shift_far(both[d * half : (d + 1) * half].astype(BF), d) for d in range(1, n_quad)]
        )
        ours.append(both[:half])

    made, first_made, ig_own = [], [], []

    def give_back(i):
        total = ours[i]
        for block in far_sums[i]:
            total += block.astype(F32)
        if i == 1:
            total = after(total, ig_own[0])
        if i == count - 1:
            total = after(total, first_made[0])
        ours[i] = total
        theirs.append(from_partner(total.astype(BF)))

    def finish(i):
        start = chunks(BWD_PARTS, features)[i][0]
        made[:] = update(
            side.reshape(1).astype(jnp.int32),
            weight,
            partner_weight,
            momentum,
            partner_moment,
            ours[i],
            theirs[i],
            start,
            made,
        )
        first_made.append(made[0])

    nb_mates = [from_mate(nb, 1) for nb in nbs]
    for i in range(count + 2):
        if i < count:
            seen = kept[-1:]
            if i == 1:
                seen += nb_mates[2:]
            if i == 2:
                seen += [ig_nb]
            x_seen = after(x_rows, *seen) if seen else x_rows
            keep, give = gradient_part(x_seen, [cots[i], nbs[i], mates[i], nb_mates[i]], scale)
            kept.append(keep)
            got.append(from_partner(after(give, *got[-1:]) if got else give))
            if i == 1:
                first_nb = after(nbs[0], keep)
                ig_nb = input_grad_part(place, [first_nb] + nbs[1:], pieces, scale)
                ig_got = from_mate(ig_nb, 2)
            if i == 2:
                first_cot = after(cots[0], kept[-1])
                ig_own.append(input_grad_part(place, [first_cot] + cots[1:], pieces, scale))
        if 0 <= i - 2:
            give_back(i - 2)
            if i - 2 < count - 1:
                finish(i - 2)
        if 0 <= i - 1 < count:
            sum_far(i - 1)

    input_grad = interleave(near.reshape(1).astype(jnp.int32), ig_own[0], ig_got, n_quad)

    finish(count - 1)
    new_weight, new_momentum = made
    return (input_grad, new_weight, new_momentum)


def solution(mesh):
    return jax.shard_map(
        per_device,
        mesh=mesh,
        in_specs=(
            P(("rep", "fsdp"), None),
            P(("rep", "fsdp"), None),
            P(("rep", "fsdp"), None),
            P(),
            P("rep", "fsdp", None),
            P("rep", "fsdp", None),
        ),
        out_specs=(P(("rep", "fsdp"), None), P("rep", "fsdp", None), P("rep", "fsdp", None)),
        check_vma=False,
    )
```

time: 209 us -> 206 us (0.986)
  waiting for transfers between devices: 129 us -> 114 us
  Pallas kernels: 33.1 us -> 41.2 us
  starting transfers between devices: 23.8 us -> 30.7 us
    ppermute x8, waiting for transfers between devices: 16.8 us -> 1.06 us  [from_partner(): lax.ppermute(block, 'rep', [(g, g ^ 1 << PARTNER_BIT) for g in range(coun...]
    ppermute x19 -> x22, waiting for transfers between devices: 59.5 us -> 46.8 us  [from_mate(): return lax.ppermute(block, 'fsdp', [(f, f ^ bit) for f in range(count)])]
    ppermute x6, waiting for transfers between devices: 53 us -> 65.7 us  [shift_far(): lax.ppermute(block, 'fsdp', [(f, (f + 4 * hops) % count) for f in range(c...]
    pallas_call x8 -> x12, Pallas kernels: 26.4 us -> 35.8 us  [the longest x3 11.2 us: forward_part(): pl.pallas_call(functools.partial(forward_kernel, scale, rows, parts), gri...]
    ppermute x19 -> x22, starting transfers between devices: 4.1 us -> 13.3 us  [from_mate(): return lax.ppermute(block, 'fsdp', [(f, f ^ bit) for f in range(count)])]
    transpose x2 -> x0, other arithmetic: 4.87 us -> none  [the longest x1 2.62 us: per_device(): jnp.concatenate([x_mine, x_theirs], axis=0)]
    unnamed x23 -> x29, local copies, waits for them, and re-layouts: 4.99 us -> 7.64 us
    transpose x2 -> x0, local copies, waits for them, and re-layouts: 2.52 us -> none  [the longest x1 2.43 us: per_device(): jnp.concatenate([x_mine, x_theirs], axis=0)]
  transfers between devices with their start and end apart: 33 -> 36, of which waited for: 18 -> 18; matrix products, arithmetic and copies ran while one was open for 7% -> 4% of each run, Pallas kernels for 11% -> 17%
where the time goes in v3:
time: 206 us; the launch traced here: 205 us
  waiting for transfers between devices  114 us (55%)
  Pallas kernels  41.2 us (20%)
  starting transfers between devices  30.7 us (15%)
  local copies, waits for them, and re-layouts  12.3 us (6%)
  other arithmetic  6.15 us (3%)
    ppermute x6, waiting for transfers between devices, shift_far(): lax.ppermute(block, 'fsdp', [(f, (f + 4 * hops) % count) for f in range(c...  65.7 us
    ppermute x22, waiting for transfers between devices, from_mate(): return lax.ppermute(block, 'fsdp', [(f, f ^ bit) for f in range(count)])  46.8 us
    ppermute x22, starting transfers between devices, from_mate(): return lax.ppermute(block, 'fsdp', [(f, f ^ bit) for f in range(count)])  13.3 us
    pallas_call x3, Pallas kernels, forward_part(): pl.pallas_call(functools.partial(forward_kernel, scale, rows, parts), gri...  11.2 us
    pallas_call x2, Pallas kernels, input_grad_part(): pl.pallas_call(functools.partial(input_grad_kernel, scale, rows, len(cots...  11 us
    ppermute x6, starting transfers between devices, shift_far(): lax.ppermute(block, 'fsdp', [(f, (f + 4 * hops) % count) for f in range(c...  8.72 us
    ppermute x8, starting transfers between devices, from_partner(): lax.ppermute(block, 'rep', [(g, g ^ 1 << PARTNER_BIT) for g in range(coun...  8.67 us
    pallas_call x3, Pallas kernels, update(): pl.pallas_call(kernel, grid_spec=pltpu.PrefetchScalarGridSpec(num_scalar_...  7.75 us
  transfers between devices with their start and end apart: 36, of which 18 were waited for; matrix products, arithmetic and copies ran while one was open for 4% of the time, Pallas kernels for 17%

profile of v3, /device:TPU:0, one launch (start us, length us, event | category | flops | bytes accessed | tf_op | source)
XLA Modules:
  0.0 204.8 jit_solution(18038221742053861616)
XLA Ops:
  0.6 2.6 %fusion.1 = (bf16[320,1024]{1,0:T(8,128)(2,1)}, bf16[320,1024]{1,0:T(8,128)(2,1)}) fusion(bf16[320,2560]{1,0:T(8,128)(2,1)} %bitcast.12), kind=kLoop, calls=%fused_computation.14 | loop fusion | bytes 2621440 | tf_op jit(solution)/shard_map/slice | solution.py:378
  3.2 4.0 %collective-permute-start.2 = (bf16[320,1024]{1,0:T(8,128)(2,1)}, bf16[320,1024]{1,0:T(8,128)(2,1)}, u32[]{:S(2)}, u32[]{:S(2)}) collective-permute-start(bf16[320,1024]{1,0:T(8,128)(2,1)} %get-tuple-element.86.refs_0_.refs_3_), channel_id=1, source_target_pairs={{0,4},{1,5},{2,6},{3,7},{4,0},{5,1},{6,2},{7,3},{8,12},{9,13},{10,... | collective-permute-start | bytes 1966088 | tf_op jit(solution)/shard_map/ppermute | solution.py:57
  7.2 1.5 collective-permute-start.12
  9.0 0.8 slice.41.refs_0_.refs_11_
  9.7 1.3 copy-done.8
  11.3 1.6 collective-permute-start
  12.9 23.5 %collective-permute-done.2.refs_2_.refs_5_ = bf16[320,1024]{1,0:T(8,128)(2,1)} collective-permute-done((bf16[320,1024]{1,0:T(8,128)(2,1)}, bf16[320,1024]{1,0:T(8,128)(2,1)}, u32[]{:S(2)}, u32[]{:S(2)}) %collective-permute-start.2) | collective-permute-done | bytes 655392 | tf_op jit(solution)/shard_map/ppermute | solution.py:57
  36.5 3.3 %convert_bitcast_fusion = bf16[320,2560]{1,0:T(8,128)(2,1)} fusion(f32[1,320,2560]{2,1,0:T(8,128)} %refs_2_.5), kind=kLoop, calls=%fused_computation | loop fusion | flops 819200 | bytes 4915200 | tf_op jit(solution)/shard_map/convert_element_type | solution.py:381
  39.7 3.1 %collective-permute-done.nb_ref = bf16[256,1280]{1,0:T(8,128)(2,1)S(1)} collective-permute-done((bf16[256,1280]{1,0:T(8,128)(2,1)S(1)}, bf16[256,1280]{1,0:T(8,128)(2,1)S(1)}, u32[]{:S(2)}, u32[]{:S(2)}) %collective-permute-start) | collective-permute-done | bytes 655392 | tf_op jit(solution)/shard_map/ppermute | solution.py:52
  42.8 0.9 copy-done.4
  43.7 0.8 collective-permute-start.4
  44.6 1.1 copy-done.2
  45.7 1.1 copy-done.5
  46.8 4.7 %forward_part.3 = (f32[256,1024]{1,0:T(8,128)S(1)}, bf16[256,1024]{1,0:T(8,128)(2,1)}) custom-call(s32[4]{0:T(128)S(1)} %pad_add_fusion.place, bf16[256,1280]{1,0:T(8,128)(2,1)S(1)} %copy-done.2, bf16[256,1280]{1,0:T(8,128)(2,1)S(1)} %copy-done.5, bf16[320,1024]{1,0:T(8,128)(2,1)} %get-tuple-element.86.refs_0_.refs_3_, ...), custom_call_target="tpu_custom_call" | custom-call | flops 13421772 | bytes 65536 | tf_op jit(solution)/shard_map/forward_part/pallas_call | solution.py:93
  51.5 1.0 copy-done.9
  52.5 15.1 %collective-permute-done.6.refs_2_.refs_9_ = bf16[320,1024]{1,0:T(8,128)(2,1)} collective-permute-done((bf16[320,1024]{1,0:T(8,128)(2,1)}, bf16[320,1024]{1,0:T(8,128)(2,1)}, u32[]{:S(2)}, u32[]{:S(2)}) %collective-permute-start.6) | collective-permute-done | bytes 655392 | tf_op jit(solution)/shard_map/ppermute | solution.py:57
  67.6 1.7 collective-permute-start.10
  69.4 0.6 collective-permute-done.7.refs_3_.refs_10_
  70.0 1.1 copy-done.3
  71.1 1.1 copy-done.6
  72.2 3.9 %forward_part.4 = (f32[256,1024]{1,0:T(8,128)S(1)}, bf16[256,1024]{1,0:T(8,128)(2,1)S(1)}) custom-call(s32[4]{0:T(128)S(1)} %pad_add_fusion.place, bf16[256,1280]{1,0:T(8,128)(2,1)S(1)} %copy-done.3, bf16[256,1280]{1,0:T(8,128)(2,1)S(1)} %copy-done.6, bf16[320,1024]{1,0:T(8,128)(2,1)} %get-tuple-element.47.refs_0_.refs_7_, ...), custom_call_target="tpu_custom_call" | custom-call | flops 13421772 | bytes 65536 | tf_op jit(solution)/shard_map/forward_part/pallas_call | solution.py:93
  76.2 1.1 turn.1
  77.5 9.6 %collective-permute-done.10.refs_2_.refs_13_ = bf16[320,512]{1,0:T(8,128)(2,1)} collective-permute-done((bf16[320,512]{1,0:T(8,128)(2,1)}, bf16[320,512]{1,0:T(8,128)(2,1)}, u32[]{:S(2)}, u32[]{:S(2)}) %collective-permute-start.10) | collective-permute-done | bytes 327712 | tf_op jit(solution)/shard_map/ppermute | solution.py:57
  87.1 2.2 %collective-permute-start.15 = (bf16[256,1024]{1,0:T(8,128)(2,1)S(1)}, bf16[256,1024]{1,0:T(8,128)(2,1)S(1)}, u32[]{:S(2)}, u32[]{:S(2)}) collective-permute-start(bf16[256,1024]{1,0:T(8,128)(2,1)S(1)} %get-tuple-element.58), channel_id=1, source_target_pairs={{0,2},{1,3},{2,0},{3,1},{4,6},{5,7},{6,4},{7,5},{8,10},{9,11},{10,... | collective-permute-start | bytes 1572872 | tf_op jit(solution)/shard_map/ppermute | solution.py:52
  89.3 1.0 fusion.2
  90.3 0.3 collective-permute-start.14
  90.6 0.3 collective-permute-start.13
  90.9 0.9 collective-permute-done.14.refs_4_.refs_15_
  92.0 2.5 %forward_part.5 = (f32[256,512]{1,0:T(8,128)S(1)}, bf16[256,512]{1,0:T(8,128)(2,1)S(1)}) custom-call(s32[4]{0:T(128)S(1)} %pad_add_fusion.place, bf16[256,1280]{1,0:T(8,128)(2,1)S(1)} %copy-done.3, bf16[256,1280]{1,0:T(8,128)(2,1)S(1)} %copy-done.7, bf16[320,512]{1,0:T(8,128)(2,1)} %slice.41.refs_0_.refs_11_, ...), custom_call_target="tpu_custom_call" | custom-call | flops 6710886 | bytes 39321 | tf_op jit(solution)/shard_map/forward_part/pallas_call | solution.py:93
  94.5 0.5 collective-permute-start.16
  95.3 12.1 %collective-permute-done.16.refs_5_ = bf16[256,512]{1,0:T(8,128)(2,1)S(1)} collective-permute-done((bf16[256,512]{1,0:T(8,128)(2,1)S(1)}, bf16[256,512]{1,0:T(8,128)(2,1)S(1)}, u32[]{:S(2)}, u32[]{:S(2)}) %collective-permute-start.16) | collective-permute-done | bytes 262176 | tf_op jit(solution)/shard_map/ppermute | solution.py:52
  107.5 3.6 %norm_cot.1 = (bf16[256,1024]{1,0:T(8,128)(2,1)S(1)}, bf16[256,1024]{1,0:T(8,128)(2,1)S(1)}, bf16[256,512]{1,0:T(8,128)(2,1)S(1)}) custom-call(bf16[256,2560]{1,0:T(8,128)(2,1)} %res_ref.1, bf16[256,2560]{1,0:T(8,128)(2,1)} %up_ref.1, f32[1,2560]{1,0:T(1,128)S(1)} %reshape.18.gain_ref, f32[256,1024]{1,0:T(8,128)S(1)} %copy-done.10, ...), custom_call_target="tpu_custom_call" | custom-call | flops 131072 | bytes 78643 | tf_op jit(solution)/shard_map/norm_cot/pallas_call | solution.py:149
  111.1 1.8 collective-permute-start.17
  112.9 12.0 %collective-permute-done.17.refs_1_.refs_0_ = bf16[256,1024]{1,0:T(8,128)(2,1)S(1)} collective-permute-done((bf16[256,1024]{1,0:T(8,128)(2,1)S(1)}, bf16[256,1024]{1,0:T(8,128)(2,1)S(1)}, u32[]{:S(2)}, u32[]{:S(2)}) %collective-permute-start.17) | collective-permute-done | bytes 524320 | tf_op jit(solution)/shard_map/ppermute | solution.py:52
  124.9 1.5 collective-permute-start.22
  126.4 0.4 collective-permute-done.19.refs_3_
  126.8 1.5 gradient_part.3
  128.3 1.3 collective-permute-start.27
  129.7 1.5 collective-permute-start.20
  131.2 8.4 %collective-permute-done.22.refs_1_ = bf16[256,1024]{1,0:T(8,128)(2,1)S(1)} collective-permute-done((bf16[256,1024]{1,0:T(8,128)(2,1)S(1)}, bf16[256,1024]{1,0:T(8,128)(2,1)S(1)}, u32[]{:S(2)}, u32[]{:S(2)}) %collective-permute-start.22) | collective-permute-done | bytes 524320 | tf_op jit(solution)/shard_map/ppermute | solution.py:52
  139.6 5.2 %collective-permute-done.20.refs_2_.refs_1_ = bf16[256,512]{1,0:T(8,128)(2,1)S(1)} collective-permute-done((bf16[256,512]{1,0:T(8,128)(2,1)S(1)}, bf16[256,512]{1,0:T(8,128)(2,1)S(1)}, u32[]{:S(2)}, u32[]{:S(2)}) %collective-permute-start.20) | collective-permute-done | bytes 262176 | tf_op jit(solution)/shard_map/ppermute | solution.py:52
  144.9 1.5 collective-permute-done.21.refs_3_
  146.4 2.4 %gradient_part.4 = (f32[320,1024]{1,0:T(8,128)S(1)}, bf16[320,1024]{1,0:T(8,128)(2,1)}) custom-call(bf16[640,1024]{1,0:T(8,128)(2,1)S(1)} %constant_dynamic-update-slice_fusion.x_ref, bf16[256,1024]{1,0:T(8,128)(2,1)S(1)} %get-tuple-element.64.refs_0_.refs_1_, bf16[256,1024]{1,0:T(8,128)(2,1)S(1)} %collective-permute-done.22.refs_1_, ...), custom_call_target="tpu_custom_call" | custom-call | flops 13421772 | bytes 53739 | tf_op jit(solution)/shard_map/gradient_part/pallas_call | solution.py:208
  148.8 1.3 collective-permute-start.28
  150.3 2.8 %collective-permute-start.31 = (bf16[160,1024]{1,0:T(8,128)(2,1)S(1)}, bf16[160,1024]{1,0:T(8,128)(2,1)S(1)}, u32[]{:S(2)}, u32[]{:S(2)}) collective-permute-start(bf16[160,1024]{1,0:T(8,128)(2,1)S(1)} %slice.55), channel_id=1, source_target_pairs={{0,4},{1,5},{2,6},{3,7},{4,0},{5,1},{6,2},{7,3},{8,12},{9,13},{10,... | collective-permute-start | bytes 983048 | tf_op jit(solution)/shard_map/ppermute | solution.py:57
  153.1 5.5 %input_grad_part.2 = bf16[256,1280]{1,0:T(8,128)(2,1)S(1)} custom-call(s32[4]{0:T(128)S(1)} %pad_add_fusion.place, bf16[256,1024]{1,0:T(8,128)(2,1)S(1)} %collective-permute-done.17.refs_1_.refs_0_, bf16[256,1024]{1,0:T(8,128)(2,1)S(1)} %collective-permute-done.22.refs_1_, bf16[256,512]{1,0:T(8,128)(2,1)S(1)} %collective-permute-done.20.refs_2_.refs_1_, ...), custom_call_target="tpu_custom_call" | custom-call | flops 16777216 | bytes 85196 | tf_op jit(solution)/shard_map/input_grad_part/pallas_call | solution.py:242
  158.6 0.8 gradient_part.5
  159.5 8.4 %collective-permute-done.31 = bf16[160,1024]{1,0:T(8,128)(2,1)S(1)} collective-permute-done((bf16[160,1024]{1,0:T(8,128)(2,1)S(1)}, bf16[160,1024]{1,0:T(8,128)(2,1)S(1)}, u32[]{:S(2)}, u32[]{:S(2)}) %collective-permute-start.31) | collective-permute-done | bytes 327712 | tf_op jit(solution)/shard_map/ppermute | solution.py:57
  168.0 0.8 collective-permute-start.32
  168.8 1.3 collective-permute-start.29
  170.1 1.3 convert_add_fusion
  171.5 3.1 %collective-permute-start.26 = (bf16[256,1280]{1,0:T(8,128)(2,1)S(1)}, bf16[256,1280]{1,0:T(8,128)(2,1)S(1)}, u32[]{:S(2)}, u32[]{:S(2)}) collective-permute-start(bf16[256,1280]{1,0:T(8,128)(2,1)S(1)} %input_grad_part.2), channel_id=1, source_target_pairs={{0,2},{1,3},{2,0},{3,1},{4,6},{5,7},{6,4},{7,5},{8,10},{9,11},{10,... | collective-permute-start | bytes 1966088 | tf_op jit(solution)/shard_map/ppermute | solution.py:52
  174.6 5.5 %input_grad_part.3.own_ref = bf16[256,1280]{1,0:T(8,128)(2,1)S(1)} custom-call(s32[4]{0:T(128)S(1)} %pad_add_fusion.place, bf16[256,1024]{1,0:T(8,128)(2,1)S(1)} %get-tuple-element.69.refs_0_, bf16[256,1024]{1,0:T(8,128)(2,1)S(1)} %get-tuple-element.64.refs_0_.refs_1_, bf16[256,512]{1,0:T(8,128)(2,1)S(1)} %get-tuple-element.62.refs_0_.refs_2_, ...), custom_call_target="tpu_custom_call" | custom-call | flops 16777216 | bytes 85196 | tf_op jit(solution)/shard_map/input_grad_part/pallas_call | solution.py:242
  180.2 2.8 %update.3 = (bf16[1,320,2560]{2,1,0:T(8,128)(2,1)}, f32[1,320,2560]{2,1,0:T(8,128)}) custom-call(s32[1]{0:T(128)} %bitcast.10.side, bf16[1,320,2560]{2,1,0:T(8,128)(2,1)S(1)} %copy-done, bf16[320,2560]{1,0:T(8,128)(2,1)S(1)} %collective-permute-done.12.refs_1_, f32[1,320,2560]{2,1,0:T(8,128)} %refs_2_.5, bf16[320,2560]{1,0:T(8,128)(2,1)} %collective-permute-done.4.refs_3_, ...), custom_call_target="tpu_custom_call" | custom-call | flops 32768 | bytes 58982 | tf_op jit(solution)/shard_map/update/pallas_call | solution.py:346
  182.9 1.0 collective-permute-done.29
  184.0 1.1 convert_add_fusion.2
  185.2 2.5 %collective-permute-done.34 = bf16[160,1024]{1,0:T(8,128)(2,1)S(1)} collective-permute-done((bf16[160,1024]{1,0:T(8,128)(2,1)S(1)}, bf16[160,1024]{1,0:T(8,128)(2,1)S(1)}, u32[]{:S(2)}, u32[]{:S(2)}) %collective-permute-start.34) | collective-permute-done | bytes 327712 | tf_op jit(solution)/shard_map/ppermute | solution.py:57
  187.8 0.8 collective-permute-start.35
  188.6 6.6 %collective-permute-done.30 = bf16[160,512]{1,0:T(8,128)(2,1)S(1)} collective-permute-done((bf16[160,512]{1,0:T(8,128)(2,1)S(1)}, bf16[160,512]{1,0:T(8,128)(2,1)S(1)}, u32[]{:S(2)}, u32[]{:S(2)}) %collective-permute-start.30) | collective-permute-done | bytes 163872 | tf_op jit(solution)/shard_map/ppermute | solution.py:57
  195.2 0.8 collective-permute-start.33
  196.0 2.2 %collective-permute-done.26.got_ref = bf16[256,1280]{1,0:T(8,128)(2,1)S(1)} collective-permute-done((bf16[256,1280]{1,0:T(8,128)(2,1)S(1)}, bf16[256,1280]{1,0:T(8,128)(2,1)S(1)}, u32[]{:S(2)}, u32[]{:S(2)}) %collective-permute-start.26) | collective-permute-done | bytes 655392 | tf_op jit(solution)/shard_map/ppermute | solution.py:52
  198.2 1.6 interleave.1
  199.9 2.8 %update.4 = (bf16[1,320,2560]{2,1,0:T(8,128)(2,1)}, f32[1,320,2560]{2,1,0:T(8,128)}) custom-call(s32[1]{0:T(128)} %bitcast.10.side, bf16[1,320,2560]{2,1,0:T(8,128)(2,1)S(1)} %copy-done, bf16[320,2560]{1,0:T(8,128)(2,1)S(1)} %collective-permute-done.12.refs_1_, f32[1,320,2560]{2,1,0:T(8,128)} %refs_2_.5, ...), custom_call_target="tpu_custom_call", output_to_operand_aliasing={{0}: (7, {}), {1}: (8, {})} | custom-call | flops 32768 | bytes 58982 | tf_op jit(solution)/shard_map/update/pallas_call | solution.py:346
  202.6 2.2 %update.5 = (bf16[1,320,2560]{2,1,0:T(8,128)(2,1)}, f32[1,320,2560]{2,1,0:T(8,128)}) custom-call(s32[1]{0:T(128)} %bitcast.10.side, bf16[1,320,2560]{2,1,0:T(8,128)(2,1)S(1)} %copy-done, bf16[320,2560]{1,0:T(8,128)(2,1)S(1)} %collective-permute-done.12.refs_1_, f32[1,320,2560]{2,1,0:T(8,128)} %refs_2_.5, ...), custom_call_target="tpu_custom_call", output_to_operand_aliasing={{0}: (7, {}), {1}: (8, {})} | custom-call | flops 16384 | bytes 29491 | tf_op jit(solution)/shard_map/update/pallas_call | solution.py:346
  (71 shorter events, 2.1 us)
Async XLA Ops:
  0.6 6.6 %copy-start = (bf16[1,320,2560]{2,1,0:T(8,128)(2,1)S(1)}, bf16[1,320,2560]{2,1,0:T(8,128)(2,1)}, u32[]{:S(2)}) copy-start(bf16[1,320,2560]{2,1,0:T(8,128)(2,1)} %refs_0_.5) | copy-start | bytes 4915204
  3.2 33.2 %collective-permute-start.2 = (bf16[320,1024]{1,0:T(8,128)(2,1)}, bf16[320,1024]{1,0:T(8,128)(2,1)}, u32[]{:S(2)}, u32[]{:S(2)}) collective-permute-start(bf16[320,1024]{1,0:T(8,128)(2,1)} %get-tuple-element.86.refs_0_.refs_3_), channel_id=1, source_target_pairs={{0,4},{1,5},{2,6},{3,7},{4,0},{5,1},{6,2},{7,3},{8,12},{9,13},{10,... | collective-permute-start | bytes 1966088 | tf_op jit(solution)/shard_map/ppermute | solution.py:57
  7.2 29.2 %collective-permute-start.1 = (bf16[320,1024]{1,0:T(8,128)(2,1)}, bf16[320,1024]{1,0:T(8,128)(2,1)}, u32[]{:S(2)}, u32[]{:S(2)}) collective-permute-start(bf16[320,1024]{1,0:T(8,128)(2,1)} %get-tuple-element.86.refs_0_.refs_3_), channel_id=1, source_target_pairs={{0,1},{1,0},{2,3},{3,2},{4,5},{5,4},{6,7},{7,6},{8,9},{9,8},{10,11... | collective-permute-start | bytes 1966088 | tf_op jit(solution)/shard_map/ppermute | solution.py:52
  7.2 79.8 %collective-permute-start.12 = (bf16[320,2560]{1,0:T(8,128)(2,1)S(1)}, bf16[320,2560]{1,0:T(8,128)(2,1)S(1)}, u32[]{:S(2)}, u32[]{:S(2)}) collective-permute-start(bf16[320,2560]{1,0:T(8,128)(2,1)S(1)} %bitcast.13), channel_id=1, source_target_pairs={{0,16},{8,24},{16,0},{24,8},{1,17},{9,25},{17,1},{25,9},{2,18},{10... | collective-permute-start | bytes 4915208 | tf_op jit(solution)/shard_map/ppermute | solution.py:47
  8.8 58.8 %collective-permute-start.5 = (bf16[320,1024]{1,0:T(8,128)(2,1)}, bf16[320,1024]{1,0:T(8,128)(2,1)}, u32[]{:S(2)}, u32[]{:S(2)}) collective-permute-start(bf16[320,1024]{1,0:T(8,128)(2,1)} %get-tuple-element.47.refs_0_.refs_7_), channel_id=1, source_target_pairs={{0,1},{1,0},{2,3},{3,2},{4,5},{5,4},{6,7},{7,6},{8,9},{9,8},{10,11... | collective-permute-start | bytes 1966088 | tf_op jit(solution)/shard_map/ppermute | solution.py:52
  9.7 1.3 copy-start.8
  11.3 28.5 %copy-start.1 = (bf16[256,1280]{1,0:T(8,128)(2,1)}, bf16[256,1280]{1,0:T(8,128)(2,1)S(1)}, u32[]{:S(2)}) copy-start(bf16[256,1280]{1,0:T(8,128)(2,1)S(1)} %get-tuple-element.50.x_ref) | copy-start | bytes 1966084
  11.3 31.5 %collective-permute-start = (bf16[256,1280]{1,0:T(8,128)(2,1)S(1)}, bf16[256,1280]{1,0:T(8,128)(2,1)S(1)}, u32[]{:S(2)}, u32[]{:S(2)}) collective-permute-start(bf16[256,1280]{1,0:T(8,128)(2,1)S(1)} %get-tuple-element.45), channel_id=1, source_target_pairs={{0,2},{1,3},{2,0},{3,1},{4,6},{5,7},{6,4},{7,5},{8,10},{9,11},{10,... | collective-permute-start | bytes 1966088 | tf_op jit(solution)/shard_map/ppermute | solution.py:52
  36.4 31.2 %collective-permute-start.6 = (bf16[320,1024]{1,0:T(8,128)(2,1)}, bf16[320,1024]{1,0:T(8,128)(2,1)}, u32[]{:S(2)}, u32[]{:S(2)}) collective-permute-start(bf16[320,1024]{1,0:T(8,128)(2,1)} %get-tuple-element.47.refs_0_.refs_7_), channel_id=1, source_target_pairs={{0,4},{1,5},{2,6},{3,7},{4,0},{5,1},{6,2},{7,3},{8,12},{9,13},{10,... | collective-permute-start | bytes 1966088 | tf_op jit(solution)/shard_map/ppermute | solution.py:57
  36.4 8.2 %collective-permute-start.3 = (bf16[320,1024]{1,0:T(8,128)(2,1)}, bf16[320,1024]{1,0:T(8,128)(2,1)}, u32[]{:S(2)}, u32[]{:S(2)}) collective-permute-start(bf16[320,1024]{1,0:T(8,128)(2,1)} %collective-permute-done.2.refs_2_.refs_5_), channel_id=1, source_target_pairs={{0,1},{1,0},{2,3},{3,2},{4,5},{5,4},{6,7},{7,6},{8,9},{9,8},{10,11... | collective-permute-start | bytes 1966088 | tf_op jit(solution)/shard_map/ppermute | solution.py:52
  42.8 0.9 copy-start.4
  43.7 51.6 %collective-permute-start.4 = (bf16[320,2560]{1,0:T(8,128)(2,1)}, bf16[320,2560]{1,0:T(8,128)(2,1)}, u32[]{:S(2)}, u32[]{:S(2)}) collective-permute-start(bf16[320,2560]{1,0:T(8,128)(2,1)} %convert_bitcast_fusion), channel_id=1, source_target_pairs={{0,16},{8,24},{16,0},{24,8},{1,17},{9,25},{17,1},{25,9},{2,18},{10... | collective-permute-start | bytes 4915208 | tf_op jit(solution)/shard_map/ppermute | solution.py:47
  44.6 1.1 copy-start.2
  45.7 1.1 copy-start.5
  51.5 1.0 copy-start.9
  67.6 2.4 %collective-permute-start.7 = (bf16[320,1024]{1,0:T(8,128)(2,1)}, bf16[320,1024]{1,0:T(8,128)(2,1)}, u32[]{:S(2)}, u32[]{:S(2)}) collective-permute-start(bf16[320,1024]{1,0:T(8,128)(2,1)} %collective-permute-done.6.refs_2_.refs_9_), channel_id=1, source_target_pairs={{0,1},{1,0},{2,3},{3,2},{4,5},{5,4},{6,7},{7,6},{8,9},{9,8},{10,11... | collective-permute-start | bytes 1966088 | tf_op jit(solution)/shard_map/ppermute | solution.py:52
  67.6 21.7 %collective-permute-start.11 = (bf16[256,1024]{1,0:T(8,128)(2,1)}, bf16[256,1024]{1,0:T(8,128)(2,1)}, u32[]{:S(2)}, u32[]{:S(2)}) collective-permute-start(bf16[256,1024]{1,0:T(8,128)(2,1)} %get-tuple-element.55), channel_id=1, source_target_pairs={{0,2},{1,3},{2,0},{3,1},{4,6},{5,7},{6,4},{7,5},{8,10},{9,11},{10,... | collective-permute-start | bytes 1572872 | tf_op jit(solution)/shard_map/ppermute | solution.py:52
  67.6 19.5 %collective-permute-start.10 = (bf16[320,512]{1,0:T(8,128)(2,1)}, bf16[320,512]{1,0:T(8,128)(2,1)}, u32[]{:S(2)}, u32[]{:S(2)}) collective-permute-start(bf16[320,512]{1,0:T(8,128)(2,1)} %slice.41.refs_0_.refs_11_), channel_id=1, source_target_pairs={{0,4},{1,5},{2,6},{3,7},{4,0},{5,1},{6,2},{7,3},{8,12},{9,13},{10,... | collective-permute-start | bytes 983048 | tf_op jit(solution)/shard_map/ppermute | solution.py:57
  70.0 1.1 copy-start.3
  71.1 1.1 copy-start.6
  72.2 3.9 %copy-start.7 = (bf16[256,1280]{1,0:T(8,128)(2,1)S(1)}, bf16[256,1280]{1,0:T(8,128)(2,1)}, u32[]{:S(2)}) copy-start(bf16[256,1280]{1,0:T(8,128)(2,1)} %copy-done.4) | copy-start | bytes 1966084
  77.3 17.9 %collective-permute-start.8 = (bf16[640,512]{1,0:T(8,128)(2,1)S(1)}, bf16[640,512]{1,0:T(8,128)(2,1)S(1)}, u32[]{:S(2)}, u32[]{:S(2)}) collective-permute-start(bf16[640,512]{1,0:T(8,128)(2,1)S(1)} %get-tuple-element.52), channel_id=1, source_target_pairs={{0,1},{1,0},{2,3},{3,2},{4,5},{5,4},{6,7},{7,6},{8,9},{9,8},{10,11... | collective-permute-start | bytes 1966088 | tf_op jit(solution)/shard_map/ppermute | solution.py:52
  87.1 3.5 %collective-permute-start.9 = (bf16[320,512]{1,0:T(8,128)(2,1)}, bf16[320,512]{1,0:T(8,128)(2,1)S(1)}, u32[]{:S(2)}, u32[]{:S(2)}) collective-permute-start(bf16[320,512]{1,0:T(8,128)(2,1)} %slice.41.refs_0_.refs_11_), channel_id=1, source_target_pairs={{0,1},{1,0},{2,3},{3,2},{4,5},{5,4},{6,7},{7,6},{8,9},{9,8},{10,11... | collective-permute-start | bytes 983048 | tf_op jit(solution)/shard_map/ppermute | solution.py:52
  87.1 20.4 %collective-permute-start.15 = (bf16[256,1024]{1,0:T(8,128)(2,1)S(1)}, bf16[256,1024]{1,0:T(8,128)(2,1)S(1)}, u32[]{:S(2)}, u32[]{:S(2)}) collective-permute-start(bf16[256,1024]{1,0:T(8,128)(2,1)S(1)} %get-tuple-element.58), channel_id=1, source_target_pairs={{0,2},{1,3},{2,0},{3,1},{4,6},{5,7},{6,4},{7,5},{8,10},{9,11},{10,... | collective-permute-start | bytes 1572872 | tf_op jit(solution)/shard_map/ppermute | solution.py:52
  90.3 1.5 collective-permute-start.14
  90.6 4.5 %copy-start.13 = (f32[2560]{0:T(1024)S(1)}, f32[2560]{0:T(1024)}, u32[]{:S(2)}) copy-start(f32[2560]{0:T(1024)} %param.9) | copy-start | bytes 30724
  90.6 1.4 collective-permute-start.13
  94.5 12.9 %collective-permute-start.16 = (bf16[256,512]{1,0:T(8,128)(2,1)S(1)}, bf16[256,512]{1,0:T(8,128)(2,1)S(1)}, u32[]{:S(2)}, u32[]{:S(2)}) collective-permute-start(bf16[256,512]{1,0:T(8,128)(2,1)S(1)} %get-tuple-element.59), channel_id=1, source_target_pairs={{0,2},{1,3},{2,0},{3,1},{4,6},{5,7},{6,4},{7,5},{8,10},{9,11},{10,... | collective-permute-start | bytes 786440 | tf_op jit(solution)/shard_map/ppermute | solution.py:52
  95.1 12.4 %copy-start.10 = (f32[256,1024]{1,0:T(8,128)S(1)}, f32[256,1024]{1,0:T(8,128)}, u32[]{:S(2)}) copy-start(f32[256,1024]{1,0:T(8,128)} %copy-done.9) | copy-start | bytes 3145732
  111.1 13.8 %collective-permute-start.17 = (bf16[256,1024]{1,0:T(8,128)(2,1)S(1)}, bf16[256,1024]{1,0:T(8,128)(2,1)S(1)}, u32[]{:S(2)}, u32[]{:S(2)}) collective-permute-start(bf16[256,1024]{1,0:T(8,128)(2,1)S(1)} %get-tuple-element.69.refs_0_), channel_id=1, source_target_pairs={{0,2},{1,3},{2,0},{3,1},{4,6},{5,7},{6,4},{7,5},{8,10},{9,11},{10,... | collective-permute-start | bytes 1572872 | tf_op jit(solution)/shard_map/ppermute | solution.py:52
  112.9 13.6 %collective-permute-start.18 = (bf16[256,1024]{1,0:T(8,128)(2,1)S(1)}, bf16[256,1024]{1,0:T(8,128)(2,1)S(1)}, u32[]{:S(2)}, u32[]{:S(2)}) collective-permute-start(bf16[256,1024]{1,0:T(8,128)(2,1)S(1)} %get-tuple-element.69.refs_0_), channel_id=1, source_target_pairs={{0,1},{1,0},{2,3},{3,2},{4,5},{5,4},{6,7},{7,6},{8,9},{9,8},{10,11... | collective-permute-start | bytes 1572872 | tf_op jit(solution)/shard_map/ppermute | solution.py:52
  124.9 1.9 collective-permute-start.19
  124.9 14.7 %collective-permute-start.22 = (bf16[256,1024]{1,0:T(8,128)(2,1)S(1)}, bf16[256,1024]{1,0:T(8,128)(2,1)S(1)}, u32[]{:S(2)}, u32[]{:S(2)}) collective-permute-start(bf16[256,1024]{1,0:T(8,128)(2,1)S(1)} %get-tuple-element.64.refs_0_.refs_1_), channel_id=1, source_target_pairs={{0,2},{1,3},{2,0},{3,1},{4,6},{5,7},{6,4},{7,5},{8,10},{9,11},{10,... | collective-permute-start | bytes 1572872 | tf_op jit(solution)/shard_map/ppermute | solution.py:52
  128.3 20.4 %collective-permute-start.27 = (bf16[320,1024]{1,0:T(8,128)(2,1)S(1)}, bf16[320,1024]{1,0:T(8,128)(2,1)S(1)}, u32[]{:S(2)}, u32[]{:S(2)}) collective-permute-start(bf16[320,1024]{1,0:T(8,128)(2,1)S(1)} %get-tuple-element.72), channel_id=1, source_target_pairs={{0,16},{8,24},{16,0},{24,8},{1,17},{9,25},{17,1},{25,9},{2,18},{10... | collective-permute-start | bytes 1966088 | tf_op jit(solution)/shard_map/ppermute | solution.py:47
  129.7 15.2 %collective-permute-start.20 = (bf16[256,512]{1,0:T(8,128)(2,1)S(1)}, bf16[256,512]{1,0:T(8,128)(2,1)S(1)}, u32[]{:S(2)}, u32[]{:S(2)}) collective-permute-start(bf16[256,512]{1,0:T(8,128)(2,1)S(1)} %get-tuple-element.62.refs_0_.refs_2_), channel_id=1, source_target_pairs={{0,2},{1,3},{2,0},{3,1},{4,6},{5,7},{6,4},{7,5},{8,10},{9,11},{10,... | collective-permute-start | bytes 786440 | tf_op jit(solution)/shard_map/ppermute | solution.py:52
  131.2 15.2 %collective-permute-start.23 = (bf16[256,1024]{1,0:T(8,128)(2,1)S(1)}, bf16[256,1024]{1,0:T(8,128)(2,1)S(1)}, u32[]{:S(2)}, u32[]{:S(2)}) collective-permute-start(bf16[256,1024]{1,0:T(8,128)(2,1)S(1)} %get-tuple-element.64.refs_0_.refs_1_), channel_id=1, source_target_pairs={{0,1},{1,0},{2,3},{3,2},{4,5},{5,4},{6,7},{7,6},{8,9},{9,8},{10,11... | collective-permute-start | bytes 1572872 | tf_op jit(solution)/shard_map/ppermute | solution.py:52
  139.6 6.8 %collective-permute-start.24 = (bf16[256,1024]{1,0:T(8,128)(2,1)S(1)}, bf16[256,1024]{1,0:T(8,128)(2,1)S(1)}, u32[]{:S(2)}, u32[]{:S(2)}) collective-permute-start(bf16[256,1024]{1,0:T(8,128)(2,1)S(1)} %collective-permute-done.22.refs_1_), channel_id=1, source_target_pairs={{0,1},{1,0},{2,3},{3,2},{4,5},{5,4},{6,7},{7,6},{8,9},{9,8},{10,11... | collective-permute-start | bytes 1572872 | tf_op jit(solution)/shard_map/ppermute | solution.py:52
  144.9 1.5 collective-permute-start.21
  148.8 20.0 %collective-permute-start.28 = (bf16[320,1024]{1,0:T(8,128)(2,1)}, bf16[320,1024]{1,0:T(8,128)(2,1)}, u32[]{:S(2)}, u32[]{:S(2)}) collective-permute-start(bf16[320,1024]{1,0:T(8,128)(2,1)} %get-tuple-element.73), channel_id=1, source_target_pairs={{0,16},{8,24},{16,0},{24,8},{1,17},{9,25},{17,1},{25,9},{2,18},{10... | collective-permute-start | bytes 1966088 | tf_op jit(solution)/shard_map/ppermute | solution.py:47
  150.2 2.9 %copy-start.11 = (f32[320,1024]{1,0:T(8,128)}, f32[320,1024]{1,0:T(8,128)S(1)}, u32[]{:S(2)}) copy-start(f32[320,1024]{1,0:T(8,128)S(1)} %convert_add_fusion.1) | copy-start | bytes 3932164
  150.3 17.6 %collective-permute-start.31 = (bf16[160,1024]{1,0:T(8,128)(2,1)S(1)}, bf16[160,1024]{1,0:T(8,128)(2,1)S(1)}, u32[]{:S(2)}, u32[]{:S(2)}) collective-permute-start(bf16[160,1024]{1,0:T(8,128)(2,1)S(1)} %slice.55), channel_id=1, source_target_pairs={{0,4},{1,5},{2,6},{3,7},{4,0},{5,1},{6,2},{7,3},{8,12},{9,13},{10,... | collective-permute-start | bytes 983048 | tf_op jit(solution)/shard_map/ppermute | solution.py:57
  153.1 5.5 %collective-permute-start.25 = (bf16[256,512]{1,0:T(8,128)(2,1)S(1)}, bf16[256,512]{1,0:T(8,128)(2,1)S(1)}, u32[]{:S(2)}, u32[]{:S(2)}) collective-permute-start(bf16[256,512]{1,0:T(8,128)(2,1)S(1)} %get-tuple-element.62.refs_0_.refs_2_), channel_id=1, source_target_pairs={{0,1},{1,0},{2,3},{3,2},{4,5},{5,4},{6,7},{7,6},{8,9},{9,8},{10,11... | collective-permute-start | bytes 786440 | tf_op jit(solution)/shard_map/ppermute | solution.py:52
  158.6 9.3 %copy-start.12 = (f32[320,1024]{1,0:T(8,128)S(1)}, f32[320,1024]{1,0:T(8,128)}, u32[]{:S(2)}) copy-start(f32[320,1024]{1,0:T(8,128)} %copy-done.11) | copy-start | bytes 3932164
  168.0 12.2 %collective-permute-start.32 = (bf16[160,1024]{1,0:T(8,128)(2,1)S(1)}, bf16[160,1024]{1,0:T(8,128)(2,1)S(1)}, u32[]{:S(2)}, u32[]{:S(2)}) collective-permute-start(bf16[160,1024]{1,0:T(8,128)(2,1)S(1)} %get-tuple-element.83), channel_id=1, source_target_pairs={{0,16},{8,24},{16,0},{24,8},{1,17},{9,25},{17,1},{25,9},{2,18},{10... | collective-permute-start | bytes 983048 | tf_op jit(solution)/shard_map/ppermute | solution.py:47
  168.8 15.2 %collective-permute-start.29 = (bf16[320,512]{1,0:T(8,128)(2,1)S(1)}, bf16[320,512]{1,0:T(8,128)(2,1)}, u32[]{:S(2)}, u32[]{:S(2)}) collective-permute-start(bf16[320,512]{1,0:T(8,128)(2,1)S(1)} %get-tuple-element.74), channel_id=1, source_target_pairs={{0,16},{8,24},{16,0},{24,8},{1,17},{9,25},{17,1},{25,9},{2,18},{10... | collective-permute-start | bytes 983048 | tf_op jit(solution)/shard_map/ppermute | solution.py:47
  171.4 16.2 %collective-permute-start.34 = (bf16[160,1024]{1,0:T(8,128)(2,1)S(1)}, bf16[160,1024]{1,0:T(8,128)(2,1)S(1)}, u32[]{:S(2)}, u32[]{:S(2)}) collective-permute-start(bf16[160,1024]{1,0:T(8,128)(2,1)S(1)} %slice.54), channel_id=1, source_target_pairs={{0,4},{1,5},{2,6},{3,7},{4,0},{5,1},{6,2},{7,3},{8,12},{9,13},{10,... | collective-permute-start | bytes 983048 | tf_op jit(solution)/shard_map/ppermute | solution.py:57
  171.5 26.7 %collective-permute-start.26 = (bf16[256,1280]{1,0:T(8,128)(2,1)S(1)}, bf16[256,1280]{1,0:T(8,128)(2,1)S(1)}, u32[]{:S(2)}, u32[]{:S(2)}) collective-permute-start(bf16[256,1280]{1,0:T(8,128)(2,1)S(1)} %input_grad_part.2), channel_id=1, source_target_pairs={{0,2},{1,3},{2,0},{3,1},{4,6},{5,7},{6,4},{7,5},{8,10},{9,11},{10,... | collective-permute-start | bytes 1966088 | tf_op jit(solution)/shard_map/ppermute | solution.py:52
  185.1 10.1 %collective-permute-start.30 = (bf16[160,512]{1,0:T(8,128)(2,1)S(1)}, bf16[160,512]{1,0:T(8,128)(2,1)S(1)}, u32[]{:S(2)}, u32[]{:S(2)}) collective-permute-start(bf16[160,512]{1,0:T(8,128)(2,1)S(1)} %slice.56), channel_id=1, source_target_pairs={{0,4},{1,5},{2,6},{3,7},{4,0},{5,1},{6,2},{7,3},{8,12},{9,13},{10,... | collective-permute-start | bytes 491528 | tf_op jit(solution)/shard_map/ppermute | solution.py:57
  187.8 12.1 %collective-permute-start.35 = (bf16[160,1024]{1,0:T(8,128)(2,1)S(1)}, bf16[160,1024]{1,0:T(8,128)(2,1)S(1)}, u32[]{:S(2)}, u32[]{:S(2)}) collective-permute-start(bf16[160,1024]{1,0:T(8,128)(2,1)S(1)} %convert_element_type.46), channel_id=1, source_target_pairs={{0,16},{8,24},{16,0},{24,8},{1,17},{9,25},{17,1},{25,9},{2,18},{10... | collective-permute-start | bytes 983048 | tf_op jit(solution)/shard_map/ppermute | solution.py:47
  195.2 7.4 %collective-permute-start.33 = (bf16[160,512]{1,0:T(8,128)(2,1)S(1)}, bf16[160,512]{1,0:T(8,128)(2,1)S(1)}, u32[]{:S(2)}, u32[]{:S(2)}) collective-permute-start(bf16[160,512]{1,0:T(8,128)(2,1)S(1)} %convert_element_type.43), channel_id=1, source_target_pairs={{0,16},{8,24},{16,0},{24,8},{1,17},{9,25},{17,1},{25,9},{2,18},{10... | collective-permute-start | bytes 491528 | tf_op jit(solution)/shard_map/ppermute | solution.py:47

commit v4 on v3

--- a/solution.py
+++ b/solution.py
@@ -19,7 +19,7 @@
 SWAP_PARTS = 2
 GIVE_PARTS = 1
 COST_SHARE = 0.01
-VMEM_MIB = 48
+VMEM_MIB = 36
 BF = jnp.bfloat16
 F32 = jnp.float32
 
@@ -502,7 +502,7 @@
         if 0 <= i - 1 < count:
             sum_far(i - 1)
 
-    input_grad = interleave(near.reshape(1).astype(jnp.int32), ig_own[0], ig_got, n_quad)
+    input_grad = interleave(near.reshape(1).astype(jnp.int32), after(ig_own[0], *made), ig_got, n_quad)
 
     finish(count - 1)
     new_weight, new_momentum = made

time: 206 us -> 203 us (0.985)
  other arithmetic: 6.15 us -> 2.17 us
    ppermute x8, waiting for transfers between devices: 1.06 us -> 4.52 us  [from_partner(): lax.ppermute(block, 'rep', [(g, g ^ 1 << PARTNER_BIT) for g in range(coun...]
    unnamed x29 -> x33, local copies, waits for them, and re-layouts: 7.64 us -> 7.6 us
  transfers between devices with their start and end apart: 36 -> 36, of which waited for: 18 -> 18; matrix products, arithmetic and copies ran while one was open for 4% -> 3% of each run, Pallas kernels for 17% -> 17%
where the time goes in v4:
time: 203 us
  waiting for transfers between devices  116 us (57%)
  Pallas kernels  39.6 us (20%)
  starting transfers between devices  30.8 us (15%)
  local copies, waits for them, and re-layouts  13.2 us (7%)
  other arithmetic  2.17 us (1%)
    ppermute x6, waiting for transfers between devices, shift_far(): lax.ppermute(block, 'fsdp', [(f, (f + 4 * hops) % count) for f in range(c...  63.8 us
    ppermute x22, waiting for transfers between devices, from_mate(): return lax.ppermute(block, 'fsdp', [(f, f ^ bit) for f in range(count)])  47.5 us
    ppermute x22, starting transfers between devices, from_mate(): return lax.ppermute(block, 'fsdp', [(f, f ^ bit) for f in range(count)])  13.4 us
    pallas_call x3, Pallas kernels, forward_part(): pl.pallas_call(functools.partial(forward_kernel, scale, rows, parts), gri...  11.2 us
    pallas_call x2, Pallas kernels, input_grad_part(): pl.pallas_call(functools.partial(input_grad_kernel, scale, rows, len(cots...  11 us
    ppermute x8, starting transfers between devices, from_partner(): lax.ppermute(block, 'rep', [(g, g ^ 1 << PARTNER_BIT) for g in range(coun...  8.73 us
    ppermute x6, starting transfers between devices, shift_far(): lax.ppermute(block, 'fsdp', [(f, (f + 4 * hops) % count) for f in range(c...  8.72 us
    unnamed x33, local copies, waits for them, and re-layouts  7.6 us
  transfers between devices with their start and end apart: 36, of which 18 were waited for; matrix products, arithmetic and copies ran while one was open for 3% of the time, Pallas kernels for 17%

profile of v4, /device:TPU:0, one launch (start us, length us, event | category | flops | bytes accessed | tf_op | source)
XLA Modules:
  0.0 202.6 jit_solution(2992752463895425285)
XLA Ops:
  0.6 2.6 %fusion.1 = (bf16[320,1024]{1,0:T(8,128)(2,1)}, bf16[320,1024]{1,0:T(8,128)(2,1)}) fusion(bf16[320,2560]{1,0:T(8,128)(2,1)} %bitcast.12), kind=kLoop, calls=%fused_computation.14 | loop fusion | bytes 2621440 | tf_op jit(solution)/shard_map/slice | solution.py:378
  3.3 4.0 %collective-permute-start.2 = (bf16[320,1024]{1,0:T(8,128)(2,1)}, bf16[320,1024]{1,0:T(8,128)(2,1)}, u32[]{:S(2)}, u32[]{:S(2)}) collective-permute-start(bf16[320,1024]{1,0:T(8,128)(2,1)} %get-tuple-element.88.refs_0_.refs_3_), channel_id=1, source_target_pairs={{0,4},{1,5},{2,6},{3,7},{4,0},{5,1},{6,2},{7,3},{8,12},{9,13},{10,... | collective-permute-start | bytes 1966088 | tf_op jit(solution)/shard_map/ppermute | solution.py:57
  7.3 1.5 collective-permute-start.12
  8.8 0.2 collective-permute-start.5
  9.0 1.7 slice.41.refs_0_.refs_11_
  10.8 1.3 copy-done.10
  12.3 1.6 collective-permute-start
  13.9 22.6 %collective-permute-done.2.refs_2_.refs_5_ = bf16[320,1024]{1,0:T(8,128)(2,1)} collective-permute-done((bf16[320,1024]{1,0:T(8,128)(2,1)}, bf16[320,1024]{1,0:T(8,128)(2,1)}, u32[]{:S(2)}, u32[]{:S(2)}) %collective-permute-start.2) | collective-permute-done | bytes 655392 | tf_op jit(solution)/shard_map/ppermute | solution.py:57
  36.5 1.3 convert_bitcast_fusion
  37.8 6.0 %collective-permute-done.nb_ref = bf16[256,1280]{1,0:T(8,128)(2,1)S(1)} collective-permute-done((bf16[256,1280]{1,0:T(8,128)(2,1)S(1)}, bf16[256,1280]{1,0:T(8,128)(2,1)S(1)}, u32[]{:S(2)}, u32[]{:S(2)}) %collective-permute-start) | collective-permute-done | bytes 655392 | tf_op jit(solution)/shard_map/ppermute | solution.py:52
  43.8 0.8 copy-done.6
  44.7 0.8 collective-permute-start.4
  45.6 1.1 copy-done.3
  46.7 1.1 copy-done.7
  47.7 4.7 %forward_part.3 = (f32[256,1024]{1,0:T(8,128)S(1)}, bf16[256,1024]{1,0:T(8,128)(2,1)}) custom-call(s32[4]{0:T(128)S(1)} %pad_add_fusion.place, bf16[256,1280]{1,0:T(8,128)(2,1)S(1)} %copy-done.3, bf16[256,1280]{1,0:T(8,128)(2,1)S(1)} %copy-done.7, bf16[320,1024]{1,0:T(8,128)(2,1)} %get-tuple-element.88.refs_0_.refs_3_, ...), custom_call_target="tpu_custom_call" | custom-call | flops 13421772 | bytes 65536 | tf_op jit(solution)/shard_map/forward_part/pallas_call | solution.py:93
  52.5 1.0 copy-done.13
  53.4 14.2 %collective-permute-done.6.refs_2_.refs_9_ = bf16[320,1024]{1,0:T(8,128)(2,1)} collective-permute-done((bf16[320,1024]{1,0:T(8,128)(2,1)}, bf16[320,1024]{1,0:T(8,128)(2,1)}, u32[]{:S(2)}, u32[]{:S(2)}) %collective-permute-start.6) | collective-permute-done | bytes 655392 | tf_op jit(solution)/shard_map/ppermute | solution.py:57
  67.7 1.7 collective-permute-start.10
  69.5 0.6 collective-permute-done.7.refs_3_.refs_10_
  70.1 1.1 copy-done.4
  71.2 1.1 copy-done.8
  72.3 3.9 %forward_part.4 = (f32[256,1024]{1,0:T(8,128)S(1)}, bf16[256,1024]{1,0:T(8,128)(2,1)S(1)}) custom-call(s32[4]{0:T(128)S(1)} %pad_add_fusion.place, bf16[256,1280]{1,0:T(8,128)(2,1)S(1)} %copy-done.4, bf16[256,1280]{1,0:T(8,128)(2,1)S(1)} %copy-done.8, bf16[320,1024]{1,0:T(8,128)(2,1)} %get-tuple-element.48.refs_0_.refs_7_, ...), custom_call_target="tpu_custom_call" | custom-call | flops 13421772 | bytes 65536 | tf_op jit(solution)/shard_map/forward_part/pallas_call | solution.py:93
  76.2 1.1 turn.1
  77.5 9.6 %collective-permute-done.10.refs_2_.refs_13_ = bf16[320,512]{1,0:T(8,128)(2,1)} collective-permute-done((bf16[320,512]{1,0:T(8,128)(2,1)}, bf16[320,512]{1,0:T(8,128)(2,1)}, u32[]{:S(2)}, u32[]{:S(2)}) %collective-permute-start.10) | collective-permute-done | bytes 327712 | tf_op jit(solution)/shard_map/ppermute | solution.py:57
  87.1 2.2 %collective-permute-start.15 = (bf16[256,1024]{1,0:T(8,128)(2,1)S(1)}, bf16[256,1024]{1,0:T(8,128)(2,1)S(1)}, u32[]{:S(2)}, u32[]{:S(2)}) collective-permute-start(bf16[256,1024]{1,0:T(8,128)(2,1)S(1)} %get-tuple-element.59), channel_id=1, source_target_pairs={{0,2},{1,3},{2,0},{3,1},{4,6},{5,7},{6,4},{7,5},{8,10},{9,11},{10,... | collective-permute-start | bytes 1572872 | tf_op jit(solution)/shard_map/ppermute | solution.py:52
  89.3 1.0 fusion.2
  90.3 0.3 collective-permute-start.14
  90.6 0.3 collective-permute-start.13
  90.9 0.9 collective-permute-done.14.refs_4_.refs_15_
  91.8 0.2 collective-permute-done.13.refs_3_.refs_14_
  92.0 2.5 %forward_part.5 = (f32[256,512]{1,0:T(8,128)S(1)}, bf16[256,512]{1,0:T(8,128)(2,1)S(1)}) custom-call(s32[4]{0:T(128)S(1)} %pad_add_fusion.place, bf16[256,1280]{1,0:T(8,128)(2,1)S(1)} %copy-done.5, bf16[256,1280]{1,0:T(8,128)(2,1)S(1)} %copy-done.9, bf16[320,512]{1,0:T(8,128)(2,1)} %slice.41.refs_0_.refs_11_, ...), custom_call_target="tpu_custom_call" | custom-call | flops 6710886 | bytes 39321 | tf_op jit(solution)/shard_map/forward_part/pallas_call | solution.py:93
  94.6 0.5 collective-permute-start.16
  95.4 12.1 %collective-permute-done.16.refs_5_ = bf16[256,512]{1,0:T(8,128)(2,1)S(1)} collective-permute-done((bf16[256,512]{1,0:T(8,128)(2,1)S(1)}, bf16[256,512]{1,0:T(8,128)(2,1)S(1)}, u32[]{:S(2)}, u32[]{:S(2)}) %collective-permute-start.16) | collective-permute-done | bytes 262176 | tf_op jit(solution)/shard_map/ppermute | solution.py:52
  107.5 3.2 %norm_cot.1 = (bf16[256,1024]{1,0:T(8,128)(2,1)S(1)}, bf16[256,1024]{1,0:T(8,128)(2,1)S(1)}, bf16[256,512]{1,0:T(8,128)(2,1)S(1)}) custom-call(bf16[256,2560]{1,0:T(8,128)(2,1)S(1)} %copy-done.11, bf16[256,2560]{1,0:T(8,128)(2,1)S(1)} %copy-done.12, f32[1,2560]{1,0:T(1,128)S(1)} %reshape.18.gain_ref, f32[256,1024]{1,0:T(8,128)S(1)} %copy-done.14, ...), custom_call_target="tpu_custom_call" | custom-call | flops 131072 | bytes 78643 | tf_op jit(solution)/shard_map/norm_cot/pallas_call | solution.py:149
  110.7 1.8 collective-permute-start.17
  112.5 12.0 %collective-permute-done.17.refs_1_.refs_0_ = bf16[256,1024]{1,0:T(8,128)(2,1)S(1)} collective-permute-done((bf16[256,1024]{1,0:T(8,128)(2,1)S(1)}, bf16[256,1024]{1,0:T(8,128)(2,1)S(1)}, u32[]{:S(2)}, u32[]{:S(2)}) %collective-permute-start.17) | collective-permute-done | bytes 524320 | tf_op jit(solution)/shard_map/ppermute | solution.py:52
  124.5 1.5 collective-permute-start.22
  126.1 0.4 collective-permute-done.19.refs_3_
  126.4 1.5 gradient_part.3
  128.0 1.4 collective-permute-start.26
  129.3 1.5 collective-permute-start.20
  130.9 8.4 %collective-permute-done.22.refs_1_ = bf16[256,1024]{1,0:T(8,128)(2,1)S(1)} collective-permute-done((bf16[256,1024]{1,0:T(8,128)(2,1)S(1)}, bf16[256,1024]{1,0:T(8,128)(2,1)S(1)}, u32[]{:S(2)}, u32[]{:S(2)}) %collective-permute-start.22) | collective-permute-done | bytes 524320 | tf_op jit(solution)/shard_map/ppermute | solution.py:52
  139.3 5.2 %collective-permute-done.20.refs_2_.refs_1_ = bf16[256,512]{1,0:T(8,128)(2,1)S(1)} collective-permute-done((bf16[256,512]{1,0:T(8,128)(2,1)S(1)}, bf16[256,512]{1,0:T(8,128)(2,1)S(1)}, u32[]{:S(2)}, u32[]{:S(2)}) %collective-permute-start.20) | collective-permute-done | bytes 262176 | tf_op jit(solution)/shard_map/ppermute | solution.py:52
  144.5 1.5 collective-permute-done.21.refs_3_
  146.0 1.5 gradient_part.4
  147.6 1.3 collective-permute-start.27
  149.2 2.8 %collective-permute-start.30 = (bf16[160,1024]{1,0:T(8,128)(2,1)S(1)}, bf16[160,1024]{1,0:T(8,128)(2,1)S(1)}, u32[]{:S(2)}, u32[]{:S(2)}) collective-permute-start(bf16[160,1024]{1,0:T(8,128)(2,1)S(1)} %slice.54), channel_id=1, source_target_pairs={{0,4},{1,5},{2,6},{3,7},{4,0},{5,1},{6,2},{7,3},{8,12},{9,13},{10,... | collective-permute-start | bytes 983048 | tf_op jit(solution)/shard_map/ppermute | solution.py:57
  152.0 5.5 %input_grad_part.2 = bf16[256,1280]{1,0:T(8,128)(2,1)S(1)} custom-call(s32[4]{0:T(128)S(1)} %pad_add_fusion.place, bf16[256,1024]{1,0:T(8,128)(2,1)S(1)} %collective-permute-done.17.refs_1_.refs_0_, bf16[256,1024]{1,0:T(8,128)(2,1)S(1)} %collective-permute-done.22.refs_1_, bf16[256,512]{1,0:T(8,128)(2,1)S(1)} %collective-permute-done.20.refs_2_.refs_1_, ...), custom_call_target="tpu_custom_call" | custom-call | flops 16777216 | bytes 85196 | tf_op jit(solution)/shard_map/input_grad_part/pallas_call | solution.py:242
  157.5 0.8 gradient_part.5
  158.4 8.4 %collective-permute-done.30 = bf16[160,1024]{1,0:T(8,128)(2,1)S(1)} collective-permute-done((bf16[160,1024]{1,0:T(8,128)(2,1)S(1)}, bf16[160,1024]{1,0:T(8,128)(2,1)S(1)}, u32[]{:S(2)}, u32[]{:S(2)}) %collective-permute-start.30) | collective-permute-done | bytes 327712 | tf_op jit(solution)/shard_map/ppermute | solution.py:57
  166.9 0.8 collective-permute-start.31
  167.7 1.3 collective-permute-start.33
  169.3 3.1 %collective-permute-start.32 = (bf16[256,1280]{1,0:T(8,128)(2,1)S(1)}, bf16[256,1280]{1,0:T(8,128)(2,1)S(1)}, u32[]{:S(2)}, u32[]{:S(2)}) collective-permute-start(bf16[256,1280]{1,0:T(8,128)(2,1)S(1)} %input_grad_part.2), channel_id=1, source_target_pairs={{0,2},{1,3},{2,0},{3,1},{4,6},{5,7},{6,4},{7,5},{8,10},{9,11},{10,... | collective-permute-start | bytes 1966088 | tf_op jit(solution)/shard_map/ppermute | solution.py:52
  172.4 5.5 %input_grad_part.3.own_ref = bf16[256,1280]{1,0:T(8,128)(2,1)S(1)} custom-call(s32[4]{0:T(128)S(1)} %pad_add_fusion.place, bf16[256,1024]{1,0:T(8,128)(2,1)S(1)} %get-tuple-element.70.refs_0_, bf16[256,1024]{1,0:T(8,128)(2,1)S(1)} %get-tuple-element.65.refs_0_.refs_1_, bf16[256,512]{1,0:T(8,128)(2,1)S(1)} %get-tuple-element.63.refs_0_.refs_2_, ...), custom_call_target="tpu_custom_call" | custom-call | flops 16777216 | bytes 85196 | tf_op jit(solution)/shard_map/input_grad_part/pallas_call | solution.py:242
  178.0 2.7 %update.3 = (bf16[1,320,2560]{2,1,0:T(8,128)(2,1)}, f32[1,320,2560]{2,1,0:T(8,128)}) custom-call(s32[1]{0:T(128)} %bitcast.10.side, bf16[1,320,2560]{2,1,0:T(8,128)(2,1)S(1)} %copy-done.1, bf16[320,2560]{1,0:T(8,128)(2,1)} %collective-permute-done.12.refs_1_, f32[1,320,2560]{2,1,0:T(8,128)S(1)} %copy-done, bf16[320,2560]{1,0:T(8,128)(2,1)} %collective-permute-done.4.refs_3_, ...), custom_call_target="tpu_custom_call" | custom-call | flops 32768 | bytes 58982 | tf_op jit(solution)/shard_map/update/pallas_call | solution.py:346
  180.6 2.1 %collective-permute-done.33 = bf16[320,512]{1,0:T(8,128)(2,1)S(1)} collective-permute-done((bf16[320,512]{1,0:T(8,128)(2,1)S(1)}, bf16[320,512]{1,0:T(8,128)(2,1)S(1)}, u32[]{:S(2)}, u32[]{:S(2)}) %collective-permute-start.33) | collective-permute-done | bytes 327712 | tf_op jit(solution)/shard_map/ppermute | solution.py:47
  182.9 2.5 %collective-permute-done.28 = bf16[160,1024]{1,0:T(8,128)(2,1)S(1)} collective-permute-done((bf16[160,1024]{1,0:T(8,128)(2,1)S(1)}, bf16[160,1024]{1,0:T(8,128)(2,1)S(1)}, u32[]{:S(2)}, u32[]{:S(2)}) %collective-permute-start.28) | collective-permute-done | bytes 327712 | tf_op jit(solution)/shard_map/ppermute | solution.py:57
  185.6 0.8 collective-permute-start.29
  186.4 6.6 %collective-permute-done.34 = bf16[160,512]{1,0:T(8,128)(2,1)S(1)} collective-permute-done((bf16[160,512]{1,0:T(8,128)(2,1)S(1)}, bf16[160,512]{1,0:T(8,128)(2,1)S(1)}, u32[]{:S(2)}, u32[]{:S(2)}) %collective-permute-start.34) | collective-permute-done | bytes 163872 | tf_op jit(solution)/shard_map/ppermute | solution.py:57
  193.0 0.8 collective-permute-start.35
  193.8 2.4 %collective-permute-done.29.refs_5_ = bf16[160,1024]{1,0:T(8,128)(2,1)S(1)} collective-permute-done((bf16[160,1024]{1,0:T(8,128)(2,1)S(1)}, bf16[160,1024]{1,0:T(8,128)(2,1)S(1)}, u32[]{:S(2)}, u32[]{:S(2)}) %collective-permute-start.29) | collective-permute-done | bytes 327712 | tf_op jit(solution)/shard_map/ppermute | solution.py:47
  196.2 2.6 %update.4 = (bf16[1,320,2560]{2,1,0:T(8,128)(2,1)}, f32[1,320,2560]{2,1,0:T(8,128)}) custom-call(s32[1]{0:T(128)} %bitcast.10.side, bf16[1,320,2560]{2,1,0:T(8,128)(2,1)S(1)} %copy-done.1, bf16[320,2560]{1,0:T(8,128)(2,1)} %collective-permute-done.12.refs_1_, f32[1,320,2560]{2,1,0:T(8,128)S(1)} %copy-done, ...), custom_call_target="tpu_custom_call", output_to_operand_aliasing={{0}: (7, {}), {1}: (8, {})} | custom-call | flops 32768 | bytes 58982 | tf_op jit(solution)/shard_map/update/pallas_call | solution.py:346
  198.8 2.2 %update.5 = (bf16[1,320,2560]{2,1,0:T(8,128)(2,1)}, f32[1,320,2560]{2,1,0:T(8,128)}) custom-call(s32[1]{0:T(128)} %bitcast.10.side, bf16[1,320,2560]{2,1,0:T(8,128)(2,1)S(1)} %copy-done.1, bf16[320,2560]{1,0:T(8,128)(2,1)} %collective-permute-done.12.refs_1_, f32[1,320,2560]{2,1,0:T(8,128)S(1)} %copy-done, ...), custom_call_target="tpu_custom_call", output_to_operand_aliasing={{0}: (7, {}), {1}: (8, {})} | custom-call | flops 16384 | bytes 29491 | tf_op jit(solution)/shard_map/update/pallas_call | solution.py:346
  201.0 1.6 interleave.1
  (75 shorter events, 1.9 us)
Async XLA Ops:
  0.6 35.9 %copy-start = (f32[1,320,2560]{2,1,0:T(8,128)S(1)}, f32[1,320,2560]{2,1,0:T(8,128)}, u32[]{:S(2)}) copy-start(f32[1,320,2560]{2,1,0:T(8,128)} %refs_2_.5) | copy-start | bytes 9830404
  3.3 33.2 %collective-permute-start.2 = (bf16[320,1024]{1,0:T(8,128)(2,1)}, bf16[320,1024]{1,0:T(8,128)(2,1)}, u32[]{:S(2)}, u32[]{:S(2)}) collective-permute-start(bf16[320,1024]{1,0:T(8,128)(2,1)} %get-tuple-element.88.refs_0_.refs_3_), channel_id=1, source_target_pairs={{0,4},{1,5},{2,6},{3,7},{4,0},{5,1},{6,2},{7,3},{8,12},{9,13},{10,... | collective-permute-start | bytes 1966088 | tf_op jit(solution)/shard_map/ppermute | solution.py:57
  7.3 29.2 %collective-permute-start.1 = (bf16[320,1024]{1,0:T(8,128)(2,1)}, bf16[320,1024]{1,0:T(8,128)(2,1)}, u32[]{:S(2)}, u32[]{:S(2)}) collective-permute-start(bf16[320,1024]{1,0:T(8,128)(2,1)} %get-tuple-element.88.refs_0_.refs_3_), channel_id=1, source_target_pairs={{0,1},{1,0},{2,3},{3,2},{4,5},{5,4},{6,7},{7,6},{8,9},{9,8},{10,11... | collective-permute-start | bytes 1966088 | tf_op jit(solution)/shard_map/ppermute | solution.py:52
  7.3 79.8 %collective-permute-start.12 = (bf16[320,2560]{1,0:T(8,128)(2,1)}, bf16[320,2560]{1,0:T(8,128)(2,1)}, u32[]{:S(2)}, u32[]{:S(2)}) collective-permute-start(bf16[320,2560]{1,0:T(8,128)(2,1)} %bitcast.13), channel_id=1, source_target_pairs={{0,16},{8,24},{16,0},{24,8},{1,17},{9,25},{17,1},{25,9},{2,18},{10... | collective-permute-start | bytes 4915208 | tf_op jit(solution)/shard_map/ppermute | solution.py:47
  8.8 58.8 %collective-permute-start.5 = (bf16[320,1024]{1,0:T(8,128)(2,1)}, bf16[320,1024]{1,0:T(8,128)(2,1)}, u32[]{:S(2)}, u32[]{:S(2)}) collective-permute-start(bf16[320,1024]{1,0:T(8,128)(2,1)} %get-tuple-element.48.refs_0_.refs_7_), channel_id=1, source_target_pairs={{0,1},{1,0},{2,3},{3,2},{4,5},{5,4},{6,7},{7,6},{8,9},{9,8},{10,11... | collective-permute-start | bytes 1966088 | tf_op jit(solution)/shard_map/ppermute | solution.py:52
  10.8 1.3 copy-start.10
  12.3 25.6 %copy-start.2 = (bf16[256,1280]{1,0:T(8,128)(2,1)}, bf16[256,1280]{1,0:T(8,128)(2,1)S(1)}, u32[]{:S(2)}) copy-start(bf16[256,1280]{1,0:T(8,128)(2,1)S(1)} %get-tuple-element.51.x_ref) | copy-start | bytes 1966084
  12.3 31.6 %collective-permute-start = (bf16[256,1280]{1,0:T(8,128)(2,1)S(1)}, bf16[256,1280]{1,0:T(8,128)(2,1)S(1)}, u32[]{:S(2)}, u32[]{:S(2)}) collective-permute-start(bf16[256,1280]{1,0:T(8,128)(2,1)S(1)} %get-tuple-element.46), channel_id=1, source_target_pairs={{0,2},{1,3},{2,0},{3,1},{4,6},{5,7},{6,4},{7,5},{8,10},{9,11},{10,... | collective-permute-start | bytes 1966088 | tf_op jit(solution)/shard_map/ppermute | solution.py:52
  36.5 31.2 %collective-permute-start.6 = (bf16[320,1024]{1,0:T(8,128)(2,1)}, bf16[320,1024]{1,0:T(8,128)(2,1)}, u32[]{:S(2)}, u32[]{:S(2)}) collective-permute-start(bf16[320,1024]{1,0:T(8,128)(2,1)} %get-tuple-element.48.refs_0_.refs_7_), channel_id=1, source_target_pairs={{0,4},{1,5},{2,6},{3,7},{4,0},{5,1},{6,2},{7,3},{8,12},{9,13},{10,... | collective-permute-start | bytes 1966088 | tf_op jit(solution)/shard_map/ppermute | solution.py:57
  36.5 9.1 %collective-permute-start.3 = (bf16[320,1024]{1,0:T(8,128)(2,1)}, bf16[320,1024]{1,0:T(8,128)(2,1)}, u32[]{:S(2)}, u32[]{:S(2)}) collective-permute-start(bf16[320,1024]{1,0:T(8,128)(2,1)} %collective-permute-done.2.refs_2_.refs_5_), channel_id=1, source_target_pairs={{0,1},{1,0},{2,3},{3,2},{4,5},{5,4},{6,7},{7,6},{8,9},{9,8},{10,11... | collective-permute-start | bytes 1966088 | tf_op jit(solution)/shard_map/ppermute | solution.py:52
  43.8 0.8 copy-start.6
  44.7 50.7 %collective-permute-start.4 = (bf16[320,2560]{1,0:T(8,128)(2,1)}, bf16[320,2560]{1,0:T(8,128)(2,1)}, u32[]{:S(2)}, u32[]{:S(2)}) collective-permute-start(bf16[320,2560]{1,0:T(8,128)(2,1)} %convert_bitcast_fusion), channel_id=1, source_target_pairs={{0,16},{8,24},{16,0},{24,8},{1,17},{9,25},{17,1},{25,9},{2,18},{10... | collective-permute-start | bytes 4915208 | tf_op jit(solution)/shard_map/ppermute | solution.py:47
  45.6 1.1 copy-start.3
  46.7 1.1 copy-start.7
  52.5 1.0 copy-start.13
  67.7 2.4 %collective-permute-start.7 = (bf16[320,1024]{1,0:T(8,128)(2,1)}, bf16[320,1024]{1,0:T(8,128)(2,1)}, u32[]{:S(2)}, u32[]{:S(2)}) collective-permute-start(bf16[320,1024]{1,0:T(8,128)(2,1)} %collective-permute-done.6.refs_2_.refs_9_), channel_id=1, source_target_pairs={{0,1},{1,0},{2,3},{3,2},{4,5},{5,4},{6,7},{7,6},{8,9},{9,8},{10,11... | collective-permute-start | bytes 1966088 | tf_op jit(solution)/shard_map/ppermute | solution.py:52
  67.7 21.7 %collective-permute-start.11 = (bf16[256,1024]{1,0:T(8,128)(2,1)}, bf16[256,1024]{1,0:T(8,128)(2,1)}, u32[]{:S(2)}, u32[]{:S(2)}) collective-permute-start(bf16[256,1024]{1,0:T(8,128)(2,1)} %get-tuple-element.56), channel_id=1, source_target_pairs={{0,2},{1,3},{2,0},{3,1},{4,6},{5,7},{6,4},{7,5},{8,10},{9,11},{10,... | collective-permute-start | bytes 1572872 | tf_op jit(solution)/shard_map/ppermute | solution.py:52
  67.7 19.5 %collective-permute-start.10 = (bf16[320,512]{1,0:T(8,128)(2,1)}, bf16[320,512]{1,0:T(8,128)(2,1)}, u32[]{:S(2)}, u32[]{:S(2)}) collective-permute-start(bf16[320,512]{1,0:T(8,128)(2,1)} %slice.41.refs_0_.refs_11_), channel_id=1, source_target_pairs={{0,4},{1,5},{2,6},{3,7},{4,0},{5,1},{6,2},{7,3},{8,12},{9,13},{10,... | collective-permute-start | bytes 983048 | tf_op jit(solution)/shard_map/ppermute | solution.py:57
  70.1 1.1 copy-start.4
  71.2 1.1 copy-start.8
  72.3 3.9 %copy-start.5 = (bf16[256,1280]{1,0:T(8,128)(2,1)S(1)}, bf16[256,1280]{1,0:T(8,128)(2,1)}, u32[]{:S(2)}) copy-start(bf16[256,1280]{1,0:T(8,128)(2,1)} %copy-done.2) | copy-start | bytes 1966084
  72.3 3.9 %copy-start.9 = (bf16[256,1280]{1,0:T(8,128)(2,1)S(1)}, bf16[256,1280]{1,0:T(8,128)(2,1)}, u32[]{:S(2)}) copy-start(bf16[256,1280]{1,0:T(8,128)(2,1)} %copy-done.6) | copy-start | bytes 1966084
  77.3 17.9 %collective-permute-start.8 = (bf16[640,512]{1,0:T(8,128)(2,1)S(1)}, bf16[640,512]{1,0:T(8,128)(2,1)S(1)}, u32[]{:S(2)}, u32[]{:S(2)}) collective-permute-start(bf16[640,512]{1,0:T(8,128)(2,1)S(1)} %get-tuple-element.53), channel_id=1, source_target_pairs={{0,1},{1,0},{2,3},{3,2},{4,5},{5,4},{6,7},{7,6},{8,9},{9,8},{10,11... | collective-permute-start | bytes 1966088 | tf_op jit(solution)/shard_map/ppermute | solution.py:52
  87.1 3.5 %collective-permute-start.9 = (bf16[320,512]{1,0:T(8,128)(2,1)}, bf16[320,512]{1,0:T(8,128)(2,1)S(1)}, u32[]{:S(2)}, u32[]{:S(2)}) collective-permute-start(bf16[320,512]{1,0:T(8,128)(2,1)} %slice.41.refs_0_.refs_11_), channel_id=1, source_target_pairs={{0,1},{1,0},{2,3},{3,2},{4,5},{5,4},{6,7},{7,6},{8,9},{9,8},{10,11... | collective-permute-start | bytes 983048 | tf_op jit(solution)/shard_map/ppermute | solution.py:52
  87.1 20.4 %collective-permute-start.15 = (bf16[256,1024]{1,0:T(8,128)(2,1)S(1)}, bf16[256,1024]{1,0:T(8,128)(2,1)S(1)}, u32[]{:S(2)}, u32[]{:S(2)}) collective-permute-start(bf16[256,1024]{1,0:T(8,128)(2,1)S(1)} %get-tuple-element.59), channel_id=1, source_target_pairs={{0,2},{1,3},{2,0},{3,1},{4,6},{5,7},{6,4},{7,5},{8,10},{9,11},{10,... | collective-permute-start | bytes 1572872 | tf_op jit(solution)/shard_map/ppermute | solution.py:52
  90.3 1.5 collective-permute-start.14
  90.6 4.5 %copy-start.15 = (f32[2560]{0:T(1024)S(1)}, f32[2560]{0:T(1024)}, u32[]{:S(2)}) copy-start(f32[2560]{0:T(1024)} %param.9) | copy-start | bytes 30724
  90.6 1.4 collective-permute-start.13
  92.0 15.5 %copy-start.14 = (f32[256,1024]{1,0:T(8,128)S(1)}, f32[256,1024]{1,0:T(8,128)}, u32[]{:S(2)}) copy-start(f32[256,1024]{1,0:T(8,128)} %copy-done.13) | copy-start | bytes 3145732
  94.6 12.9 %collective-permute-start.16 = (bf16[256,512]{1,0:T(8,128)(2,1)S(1)}, bf16[256,512]{1,0:T(8,128)(2,1)S(1)}, u32[]{:S(2)}, u32[]{:S(2)}) collective-permute-start(bf16[256,512]{1,0:T(8,128)(2,1)S(1)} %get-tuple-element.60), channel_id=1, source_target_pairs={{0,2},{1,3},{2,0},{3,1},{4,6},{5,7},{6,4},{7,5},{8,10},{9,11},{10,... | collective-permute-start | bytes 786440 | tf_op jit(solution)/shard_map/ppermute | solution.py:52
  95.2 12.4 %copy-start.11 = (bf16[256,2560]{1,0:T(8,128)(2,1)S(1)}, bf16[256,2560]{1,0:T(8,128)(2,1)}, u32[]{:S(2)}) copy-start(bf16[256,2560]{1,0:T(8,128)(2,1)} %res_ref.1) | copy-start | bytes 3932164
  95.2 12.4 %copy-start.12 = (bf16[256,2560]{1,0:T(8,128)(2,1)S(1)}, bf16[256,2560]{1,0:T(8,128)(2,1)}, u32[]{:S(2)}) copy-start(bf16[256,2560]{1,0:T(8,128)(2,1)} %up_ref.1) | copy-start | bytes 3932164
  110.7 13.8 %collective-permute-start.17 = (bf16[256,1024]{1,0:T(8,128)(2,1)S(1)}, bf16[256,1024]{1,0:T(8,128)(2,1)S(1)}, u32[]{:S(2)}, u32[]{:S(2)}) collective-permute-start(bf16[256,1024]{1,0:T(8,128)(2,1)S(1)} %get-tuple-element.70.refs_0_), channel_id=1, source_target_pairs={{0,2},{1,3},{2,0},{3,1},{4,6},{5,7},{6,4},{7,5},{8,10},{9,11},{10,... | collective-permute-start | bytes 1572872 | tf_op jit(solution)/shard_map/ppermute | solution.py:52
  112.5 13.6 %collective-permute-start.18 = (bf16[256,1024]{1,0:T(8,128)(2,1)S(1)}, bf16[256,1024]{1,0:T(8,128)(2,1)S(1)}, u32[]{:S(2)}, u32[]{:S(2)}) collective-permute-start(bf16[256,1024]{1,0:T(8,128)(2,1)S(1)} %get-tuple-element.70.refs_0_), channel_id=1, source_target_pairs={{0,1},{1,0},{2,3},{3,2},{4,5},{5,4},{6,7},{7,6},{8,9},{9,8},{10,11... | collective-permute-start | bytes 1572872 | tf_op jit(solution)/shard_map/ppermute | solution.py:52
  124.5 1.9 collective-permute-start.19
  124.5 14.7 %collective-permute-start.22 = (bf16[256,1024]{1,0:T(8,128)(2,1)S(1)}, bf16[256,1024]{1,0:T(8,128)(2,1)S(1)}, u32[]{:S(2)}, u32[]{:S(2)}) collective-permute-start(bf16[256,1024]{1,0:T(8,128)(2,1)S(1)} %get-tuple-element.65.refs_0_.refs_1_), channel_id=1, source_target_pairs={{0,2},{1,3},{2,0},{3,1},{4,6},{5,7},{6,4},{7,5},{8,10},{9,11},{10,... | collective-permute-start | bytes 1572872 | tf_op jit(solution)/shard_map/ppermute | solution.py:52
  128.0 19.6 %collective-permute-start.26 = (bf16[320,1024]{1,0:T(8,128)(2,1)S(1)}, bf16[320,1024]{1,0:T(8,128)(2,1)S(1)}, u32[]{:S(2)}, u32[]{:S(2)}) collective-permute-start(bf16[320,1024]{1,0:T(8,128)(2,1)S(1)} %get-tuple-element.72), channel_id=1, source_target_pairs={{0,16},{8,24},{16,0},{24,8},{1,17},{9,25},{17,1},{25,9},{2,18},{10... | collective-permute-start | bytes 1966088 | tf_op jit(solution)/shard_map/ppermute | solution.py:47
  129.3 15.2 %collective-permute-start.20 = (bf16[256,512]{1,0:T(8,128)(2,1)S(1)}, bf16[256,512]{1,0:T(8,128)(2,1)S(1)}, u32[]{:S(2)}, u32[]{:S(2)}) collective-permute-start(bf16[256,512]{1,0:T(8,128)(2,1)S(1)} %get-tuple-element.63.refs_0_.refs_2_), channel_id=1, source_target_pairs={{0,2},{1,3},{2,0},{3,1},{4,6},{5,7},{6,4},{7,5},{8,10},{9,11},{10,... | collective-permute-start | bytes 786440 | tf_op jit(solution)/shard_map/ppermute | solution.py:52
  130.9 15.2 %collective-permute-start.23 = (bf16[256,1024]{1,0:T(8,128)(2,1)S(1)}, bf16[256,1024]{1,0:T(8,128)(2,1)S(1)}, u32[]{:S(2)}, u32[]{:S(2)}) collective-permute-start(bf16[256,1024]{1,0:T(8,128)(2,1)S(1)} %get-tuple-element.65.refs_0_.refs_1_), channel_id=1, source_target_pairs={{0,1},{1,0},{2,3},{3,2},{4,5},{5,4},{6,7},{7,6},{8,9},{9,8},{10,11... | collective-permute-start | bytes 1572872 | tf_op jit(solution)/shard_map/ppermute | solution.py:52
  139.3 6.8 %collective-permute-start.24 = (bf16[256,1024]{1,0:T(8,128)(2,1)S(1)}, bf16[256,1024]{1,0:T(8,128)(2,1)S(1)}, u32[]{:S(2)}, u32[]{:S(2)}) collective-permute-start(bf16[256,1024]{1,0:T(8,128)(2,1)S(1)} %collective-permute-done.22.refs_1_), channel_id=1, source_target_pairs={{0,1},{1,0},{2,3},{3,2},{4,5},{5,4},{6,7},{7,6},{8,9},{9,8},{10,11... | collective-permute-start | bytes 1572872 | tf_op jit(solution)/shard_map/ppermute | solution.py:52
  144.5 1.5 collective-permute-start.21
  147.6 20.1 %collective-permute-start.27 = (bf16[320,1024]{1,0:T(8,128)(2,1)S(1)}, bf16[320,1024]{1,0:T(8,128)(2,1)S(1)}, u32[]{:S(2)}, u32[]{:S(2)}) collective-permute-start(bf16[320,1024]{1,0:T(8,128)(2,1)S(1)} %get-tuple-element.73), channel_id=1, source_target_pairs={{0,16},{8,24},{16,0},{24,8},{1,17},{9,25},{17,1},{25,9},{2,18},{10... | collective-permute-start | bytes 1966088 | tf_op jit(solution)/shard_map/ppermute | solution.py:47
  149.2 17.6 %collective-permute-start.30 = (bf16[160,1024]{1,0:T(8,128)(2,1)S(1)}, bf16[160,1024]{1,0:T(8,128)(2,1)S(1)}, u32[]{:S(2)}, u32[]{:S(2)}) collective-permute-start(bf16[160,1024]{1,0:T(8,128)(2,1)S(1)} %slice.54), channel_id=1, source_target_pairs={{0,4},{1,5},{2,6},{3,7},{4,0},{5,1},{6,2},{7,3},{8,12},{9,13},{10,... | collective-permute-start | bytes 983048 | tf_op jit(solution)/shard_map/ppermute | solution.py:57
  152.0 5.5 %collective-permute-start.25 = (bf16[256,512]{1,0:T(8,128)(2,1)S(1)}, bf16[256,512]{1,0:T(8,128)(2,1)S(1)}, u32[]{:S(2)}, u32[]{:S(2)}) collective-permute-start(bf16[256,512]{1,0:T(8,128)(2,1)S(1)} %get-tuple-element.63.refs_0_.refs_2_), channel_id=1, source_target_pairs={{0,1},{1,0},{2,3},{3,2},{4,5},{5,4},{6,7},{7,6},{8,9},{9,8},{10,11... | collective-permute-start | bytes 786440 | tf_op jit(solution)/shard_map/ppermute | solution.py:52
  166.9 11.1 %collective-permute-start.31 = (bf16[160,1024]{1,0:T(8,128)(2,1)S(1)}, bf16[160,1024]{1,0:T(8,128)(2,1)S(1)}, u32[]{:S(2)}, u32[]{:S(2)}) collective-permute-start(bf16[160,1024]{1,0:T(8,128)(2,1)S(1)} %get-tuple-element.85), channel_id=1, source_target_pairs={{0,16},{8,24},{16,0},{24,8},{1,17},{9,25},{17,1},{25,9},{2,18},{10... | collective-permute-start | bytes 983048 | tf_op jit(solution)/shard_map/ppermute | solution.py:47
  167.7 15.1 %collective-permute-start.33 = (bf16[320,512]{1,0:T(8,128)(2,1)S(1)}, bf16[320,512]{1,0:T(8,128)(2,1)S(1)}, u32[]{:S(2)}, u32[]{:S(2)}) collective-permute-start(bf16[320,512]{1,0:T(8,128)(2,1)S(1)} %get-tuple-element.81), channel_id=1, source_target_pairs={{0,16},{8,24},{16,0},{24,8},{1,17},{9,25},{17,1},{25,9},{2,18},{10... | collective-permute-start | bytes 983048 | tf_op jit(solution)/shard_map/ppermute | solution.py:47
  169.2 16.2 %collective-permute-start.28 = (bf16[160,1024]{1,0:T(8,128)(2,1)S(1)}, bf16[160,1024]{1,0:T(8,128)(2,1)S(1)}, u32[]{:S(2)}, u32[]{:S(2)}) collective-permute-start(bf16[160,1024]{1,0:T(8,128)(2,1)S(1)} %slice.55), channel_id=1, source_target_pairs={{0,4},{1,5},{2,6},{3,7},{4,0},{5,1},{6,2},{7,3},{8,12},{9,13},{10,... | collective-permute-start | bytes 983048 | tf_op jit(solution)/shard_map/ppermute | solution.py:57
  169.3 31.7 %collective-permute-start.32 = (bf16[256,1280]{1,0:T(8,128)(2,1)S(1)}, bf16[256,1280]{1,0:T(8,128)(2,1)S(1)}, u32[]{:S(2)}, u32[]{:S(2)}) collective-permute-start(bf16[256,1280]{1,0:T(8,128)(2,1)S(1)} %input_grad_part.2), channel_id=1, source_target_pairs={{0,2},{1,3},{2,0},{3,1},{4,6},{5,7},{6,4},{7,5},{8,10},{9,11},{10,... | collective-permute-start | bytes 1966088 | tf_op jit(solution)/shard_map/ppermute | solution.py:52
  172.4 5.5 %copy-start.1 = (bf16[1,320,2560]{2,1,0:T(8,128)(2,1)S(1)}, bf16[1,320,2560]{2,1,0:T(8,128)(2,1)}, u32[]{:S(2)}) copy-start(bf16[1,320,2560]{2,1,0:T(8,128)(2,1)} %refs_0_.5) | copy-start | bytes 4915204
  182.9 10.1 %collective-permute-start.34 = (bf16[160,512]{1,0:T(8,128)(2,1)S(1)}, bf16[160,512]{1,0:T(8,128)(2,1)S(1)}, u32[]{:S(2)}, u32[]{:S(2)}) collective-permute-start(bf16[160,512]{1,0:T(8,128)(2,1)S(1)} %slice.56), channel_id=1, source_target_pairs={{0,4},{1,5},{2,6},{3,7},{4,0},{5,1},{6,2},{7,3},{8,12},{9,13},{10,... | collective-permute-start | bytes 491528 | tf_op jit(solution)/shard_map/ppermute | solution.py:57
  185.6 10.7 %collective-permute-start.29 = (bf16[160,1024]{1,0:T(8,128)(2,1)S(1)}, bf16[160,1024]{1,0:T(8,128)(2,1)S(1)}, u32[]{:S(2)}, u32[]{:S(2)}) collective-permute-start(bf16[160,1024]{1,0:T(8,128)(2,1)S(1)} %convert_element_type.40), channel_id=1, source_target_pairs={{0,16},{8,24},{16,0},{24,8},{1,17},{9,25},{17,1},{25,9},{2,18},{10... | collective-permute-start | bytes 983048 | tf_op jit(solution)/shard_map/ppermute | solution.py:47
  193.0 5.8 %collective-permute-start.35 = (bf16[160,512]{1,0:T(8,128)(2,1)S(1)}, bf16[160,512]{1,0:T(8,128)(2,1)S(1)}, u32[]{:S(2)}, u32[]{:S(2)}) collective-permute-start(bf16[160,512]{1,0:T(8,128)(2,1)S(1)} %convert_element_type.46), channel_id=1, source_target_pairs={{0,16},{8,24},{16,0},{24,8},{1,17},{9,25},{17,1},{25,9},{2,18},{10... | collective-permute-start | bytes 491528 | tf_op jit(solution)/shard_map/ppermute | solution.py:47
